TPU v7x, 32 devices: a whole 2x2x4 slice. The times are simulated.
32 devices in a mesh: exp: 4 (over z), dp: 8 (over y, x, core).
Axes of the slice: x: 2, y: 2, z: 4, core: 2. Of those that a mesh axis runs over, the one named last changes fastest.
Arguments:
- tokens: bfloat16 [8, 1024, 512], P('dp', 'exp'), may hold values from -6 to 6
- cotangent: bfloat16 [8, 1024, 512], P('dp', 'exp'), may hold values from -6 to 6
- routes: int32 [2, 8, 1024, 8], P(None, 'dp'), may hold values from 0 to 23, all different within a row; in each aligned block of 256 rows (0 to 255, 256 to 511, ..., all dimensions but the last counted through in order) at most 128 rows name the same one
- keep: int32 [8, 1024], P('dp'), may hold values 0 or 1
- lengths: int32 [8, 9], P('dp'), may hold values from 1 to 896, 1024 in all within a row
- norm1_gain: float32 [2, 512], replicated, may hold values from 0.1 to 1.9
- norm1_bias: float32 [2, 512], replicated, may hold values from -1 to 1
- w_kv: bfloat16 [2, 512, 128], replicated, may hold values from -0.25 to 0.25
- w_router: bfloat16 [2, 512, 24], replicated, may hold values from -0.125 to 0.125
- w_query: bfloat16 [2, 24, 512, 64], P(None, 'exp'), may hold values from -0.625 to 0.625
- w_out: bfloat16 [2, 24, 64, 512], P(None, 'exp'), may hold values from -2 to 2
- norm2_gain: float32 [2, 512], replicated, may hold values from 0.1 to 1.9
- norm2_bias: float32 [2, 512], replicated, may hold values from -1 to 1
- w_up: bfloat16 [2, 512, 2048], replicated, may hold values from -0.25 to 0.25
- w_down: bfloat16 [2, 2048, 512], replicated, may hold values from -0.125 to 0.125
Outputs:
- activations: bfloat16 [8, 1024, 512], P('dp', 'exp')
- input_grad: float32 [8, 1024, 512], P('dp', 'exp')
- norm1_gain_grad: float32 [2, 512], replicated
- norm1_bias_grad: float32 [2, 512], replicated
- w_kv_grad: float32 [2, 512, 128], replicated
- w_router_grad: float32 [2, 512, 24], replicated
- w_query_grad: float32 [2, 24, 512, 64], P(None, 'exp')
- w_out_grad: float32 [2, 24, 64, 512], P(None, 'exp')
- norm2_gain_grad: float32 [2, 512], replicated
- norm2_bias_grad: float32 [2, 512], replicated
- w_up_grad: float32 [2, 512, 2048], replicated
- w_down_grad: float32 [2, 2048, 512], replicated
- counts: float32 [2, 24], replicated
Inputs may be any that keep to these rules, and one draw needn't show every extreme that they name: `routes`: in each layer, the rows of one device (aligned blocks of 256 rows of a group) name no head expert more than 128 times, a bound that some block reaches. Each group's lengths sum to 1024 and the largest is exactly 896.
All inputs are finite; a program needn't handle non-finite values. No bound on the sum of `keep` on one device may be relied on, other than what follows from the above.
Results may differ from a plain program's by a relative error of at most 0.025.
The roundings to bfloat16 on the way count: a program that leaves them out, or rounds other values in their place, can miss the bound.
Values may be sent and summed in bfloat16 or wider, within the bound.
A program may use at most 128 MiB of HBM per device.

v0:
```python
from functools import partial
import math

import jax
import jax.numpy as jnp
from jax import lax
from jax.sharding import PartitionSpec as P

CAP = 128


epsilon = 1e-05
neg_big = -1e30


def normalize(values, gain, bias):
    center = values - jnp.mean(values, axis=-1, keepdims=True)
    spread = jnp.mean(center * center, axis=-1, keepdims=True)
    return center * lax.rsqrt(spread + epsilon) * gain + bias


def route_table(chosen_dev, capacity, experts):
    row_count = chosen_dev.shape[0]
    expert_hot = (
        chosen_dev[:, :, None] == jnp.arange(experts, dtype=jnp.int32)[None, None, :]
    ).astype(jnp.int32)
    one_hot = jnp.sum(expert_hot, axis=1)
    running = jnp.cumsum(one_hot, axis=0)
    before = running - one_hot
    slot_of = jnp.sum(before[:, None, :] * expert_hot, axis=2)
    flat_slot = chosen_dev * capacity + slot_of
    targets = jnp.arange(1, capacity + 1, dtype=jnp.int32)
    token_of = jnp.sum((running.T[:, None, :] < targets[None, :, None]).astype(jnp.int32), axis=2)
    filled = targets[None, :] <= running[-1][:, None]
    token_of = jnp.minimum(token_of, row_count - 1)
    return (flat_slot, token_of, filled)


def block_scores(block_rows, block_position, segment, bounds, keep_keys, keys):
    group = segment.shape[0]
    key_position = jnp.arange(group, dtype=jnp.int32)
    scores = jnp.einsum("rh,kh->rk", block_rows, keys, preferred_element_type=jnp.float32) * 0.125
    row_segment = jnp.sum((block_position[:, None] >= bounds[None, :]).astype(jnp.int32), axis=1)
    same = row_segment[:, None] == segment[None, :]
    causal = key_position[None, :] <= block_position[:, None]
    usable = (keep_keys[None, :] > 0) | (key_position[None, :] == block_position[:, None])
    allowed = same & causal & usable
    return (jnp.where(allowed, scores, neg_big), allowed)


def attend_rows(flat_queries, flat_position, segment, bounds, keep_keys, keyval):
    total_rows, head = flat_queries.shape
    block = math.gcd(total_rows, 512)
    keys = keyval[:, :head]
    values = keyval[:, head:]

    def one_block(item):
        block_rows, block_position = item
        masked, allowed = block_scores(block_rows, block_position, segment, bounds, keep_keys, keys)
        top = jnp.max(masked, axis=1, keepdims=True)
        spread = jnp.where(allowed, jnp.exp(masked - top), 0.0)
        total = jnp.sum(spread, axis=1, keepdims=True)
        shares = (spread / total).astype(jnp.bfloat16)
        attended = jnp.dot(shares, values, preferred_element_type=jnp.float32).astype(jnp.bfloat16)
        return (attended, top[:, 0], total[:, 0])

    attended, tops, totals = lax.map(
        one_block, (flat_queries.reshape(-1, block, head), flat_position.reshape(-1, block))
    )
    return (
        attended.reshape(total_rows, head),
        tops.reshape(total_rows),
        totals.reshape(total_rows),
    )


def attend_back(
    flat_queries, flat_position, tops, totals, att_grad, segment, bounds, keep_keys, keyval
):
    total_rows, head = flat_queries.shape
    block = math.gcd(total_rows, 512)
    group = keyval.shape[0]
    keys = keyval[:, :head]
    values = keyval[:, head:]

    def one_block(carry, item):
        key_grad, value_grad = carry
        block_rows, block_position, top, total, block_grad = item
        masked, allowed = block_scores(block_rows, block_position, segment, bounds, keep_keys, keys)
        shares = jnp.where(allowed, jnp.exp(masked - top[:, None]), 0.0) / total[:, None]
        rounded = shares.astype(jnp.bfloat16)
        value_grad = value_grad + jnp.einsum(
            "rk,rh->kh", rounded, block_grad, preferred_element_type=jnp.float32
        )
        share_grad = jnp.einsum("rh,kh->rk", block_grad, values, preferred_element_type=jnp.float32)
        score_grad = (
            shares * (share_grad - jnp.sum(share_grad * shares, axis=1, keepdims=True))
        ).astype(jnp.bfloat16)
        query_grad = jnp.dot(score_grad, keys, preferred_element_type=jnp.float32) * 0.125
        key_grad = (
            key_grad
            + jnp.einsum("rk,rh->kh", score_grad, block_rows, preferred_element_type=jnp.float32)
            * 0.125
        )
        return ((key_grad, value_grad), query_grad.astype(jnp.bfloat16))

    empty = jnp.zeros((group, head), jnp.float32)
    items = (
        flat_queries.reshape(-1, block, head),
        flat_position.reshape(-1, block),
        tops.reshape(-1, block),
        totals.reshape(-1, block),
        att_grad.reshape(-1, block, head),
    )
    (key_grad, value_grad), query_grad = lax.scan(one_block, (empty, empty), items)
    return (jnp.concatenate([key_grad, value_grad], axis=1), query_grad.reshape(total_rows, head))


def body(
    tokens,
    cotangent,
    routes,
    keep,
    lengths,
    norm1_gain,
    norm1_bias,
    w_kv,
    w_router,
    w_query,
    w_out,
    norm2_gain,
    norm2_bias,
    w_up,
    w_down,
):
    layers = w_kv.shape[0]
    tok_count = tokens.shape[1]
    width = tokens.shape[2]
    experts = w_router.shape[2]
    topk = routes.shape[3]
    group = routes.shape[2]
    local_experts = w_query.shape[1]
    capacity = CAP
    exp_count = lax.axis_size("exp")
    own_index = lax.axis_index("exp")
    start = own_index * tok_count
    keep_group = keep[0]
    ends = jnp.cumsum(lengths[0])
    bounds = ends[:-1]
    key_position = jnp.arange(group, dtype=jnp.int32)
    segment = jnp.sum((key_position[:, None] >= bounds[None, :]).astype(jnp.int32), axis=1)
    keep_own = lax.dynamic_slice_in_dim(keep_group, start, tok_count, 0)
    keep_float = keep_own.astype(jnp.float32)
    expert_ids = jnp.arange(experts, dtype=jnp.int32)
    token_ids = jnp.arange(tok_count, dtype=jnp.int32)
    slot_ids = jnp.arange(experts * capacity, dtype=jnp.int32)
    stream = tokens[0].astype(jnp.float32)
    saved = []
    count_list = []
    for layer_no in range(layers):
        chosen = routes[layer_no, 0]
        own_routes = lax.dynamic_slice_in_dim(chosen, start, tok_count, 0)
        flat_slot, token_of, filled = route_table(own_routes, capacity, experts)
        one_hot = (own_routes[:, :, None] == expert_ids[None, None, :]).astype(jnp.float32)
        pick = (filled[:, :, None] & (token_of[:, :, None] == token_ids[None, None, :])).astype(
            jnp.float32
        )
        slot_hot = (flat_slot[:, :, None] == slot_ids[None, None, :]).astype(jnp.bfloat16)
        count_list.append(jnp.einsum("t,tke->e", keep_float, one_hot))
        normed = normalize(stream, norm1_gain[layer_no], norm1_bias[layer_no]).astype(jnp.bfloat16)
        keyval_own = jnp.dot(normed, w_kv[layer_no], preferred_element_type=jnp.float32).astype(
            jnp.bfloat16
        )
        keyval = lax.all_gather(keyval_own, "exp", axis=0, tiled=True)
        logits = jnp.dot(normed, w_router[layer_no], preferred_element_type=jnp.float32)
        picked = jnp.einsum("te,tke->tk", logits, one_hot, precision=lax.Precision.HIGHEST)
        picked = jnp.exp(picked - jnp.max(picked, axis=1, keepdims=True))
        gates = picked / jnp.sum(picked, axis=1, keepdims=True)
        outgoing = jnp.einsum(
            "ect,td->ecd", pick.astype(jnp.bfloat16), normed, preferred_element_type=jnp.float32
        ).astype(jnp.bfloat16)
        inputs = lax.all_to_all(
            outgoing.reshape(exp_count, local_experts, capacity, width),
            "exp",
            split_axis=0,
            concat_axis=0,
            tiled=True,
        )
        every_routes = chosen.reshape(exp_count, tok_count, topk)
        _, every_token, _ = jax.vmap(partial(route_table, capacity=capacity, experts=experts))(
            every_routes
        )
        mine = lax.dynamic_slice_in_dim(every_token, own_index * local_experts, local_experts, 1)
        position = mine + (jnp.arange(exp_count, dtype=jnp.int32) * tok_count)[:, None, None]
        query_weights = w_query[layer_no]
        out_weights = w_out[layer_no]
        queries = jnp.einsum(
            "secd,edh->sech", inputs, query_weights, preferred_element_type=jnp.float32
        ).astype(jnp.bfloat16)
        total_rows = queries.shape[0] * queries.shape[1] * queries.shape[2]
        head = queries.shape[3]
        flat_att, tops, totals = attend_rows(
            queries.reshape(total_rows, head),
            position.reshape(total_rows),
            segment,
            bounds,
            keep_group,
            keyval,
        )
        attended = flat_att.reshape(queries.shape)
        outputs = jnp.einsum(
            "sech,ehd->secd", attended, out_weights, preferred_element_type=jnp.float32
        ).astype(jnp.bfloat16)
        returned = lax.all_to_all(outputs, "exp", split_axis=0, concat_axis=0, tiled=True).reshape(
            experts, capacity, width
        )
        fetched = jnp.einsum(
            "tks,sd->tkd",
            slot_hot,
            returned.reshape(experts * capacity, width),
            preferred_element_type=jnp.float32,
        ).astype(jnp.bfloat16)
        mix = jnp.sum(gates[:, :, None] * fetched, axis=1)
        middle = stream + mix
        normed2 = normalize(middle, norm2_gain[layer_no], norm2_bias[layer_no]).astype(jnp.bfloat16)
        upper = jnp.dot(normed2, w_up[layer_no], preferred_element_type=jnp.float32)
        active = jax.nn.gelu(upper, approximate=True).astype(jnp.bfloat16)
        saved.append(
            (
                stream,
                pick,
                slot_hot,
                one_hot,
                normed,
                keyval,
                gates,
                inputs,
                position,
                query_weights,
                out_weights,
                queries,
                attended,
                tops,
                totals,
                fetched,
                middle,
                normed2,
                upper,
                active,
            )
        )
        stream = middle + jnp.dot(active, w_down[layer_no], preferred_element_type=jnp.float32)
    activations = stream.astype(jnp.bfloat16)[None]
    stream_grad = cotangent[0].astype(jnp.float32) * keep_float[:, None]
    grad_lists = [[None] * layers for item in range(10)]
    for layer_no in reversed(range(layers)):
        (
            resident,
            pick,
            slot_hot,
            one_hot,
            normed,
            keyval,
            gates,
            inputs,
            position,
            query_weights,
            out_weights,
            queries,
            attended,
            tops,
            totals,
            fetched,
            middle,
            normed2,
            upper,
            active,
        ) = saved[layer_no]
        branch_grad = stream_grad.astype(jnp.bfloat16)
        down_grad = jnp.einsum("tf,td->fd", active, branch_grad, preferred_element_type=jnp.float32)
        active_grad = jnp.einsum(
            "td,fd->tf", branch_grad, w_down[layer_no], preferred_element_type=jnp.float32
        )
        _, gelu_back = jax.vjp(partial(jax.nn.gelu, approximate=True), upper)
        upper_grad = gelu_back(active_grad)[0].astype(jnp.bfloat16)
        up_grad = jnp.einsum("td,tf->df", normed2, upper_grad, preferred_element_type=jnp.float32)
        normed2_grad = jnp.einsum(
            "tf,df->td", upper_grad, w_up[layer_no], preferred_element_type=jnp.float32
        )
        _, second_back = jax.vjp(normalize, middle, norm2_gain[layer_no], norm2_bias[layer_no])
        middle_part, gain2_grad, bias2_grad = second_back(normed2_grad)
        middle_grad = stream_grad + middle_part
        gate_grad = jnp.sum(middle_grad[:, None, :] * fetched, axis=2)
        pick_grad = gates * (gate_grad - jnp.sum(gate_grad * gates, axis=1, keepdims=True))
        logit_grad = jnp.einsum(
            "tk,tke->te", pick_grad, one_hot, precision=lax.Precision.HIGHEST
        ).astype(jnp.bfloat16)
        router_grad = jnp.einsum(
            "td,te->de", normed, logit_grad, preferred_element_type=jnp.float32
        )
        normed_grad = jnp.einsum(
            "te,de->td", logit_grad, w_router[layer_no], preferred_element_type=jnp.float32
        )
        gate_dense = jnp.einsum("tk,tke->et", gates, one_hot, precision=lax.Precision.HIGHEST)
        gate_pick = pick * gate_dense[:, None, :]
        out_grad = jnp.einsum(
            "ect,td->ecd", gate_pick, middle_grad, precision=lax.Precision.HIGHEST
        ).astype(jnp.bfloat16)
        incoming_grad = lax.all_to_all(
            out_grad.reshape(exp_count, local_experts, capacity, width),
            "exp",
            split_axis=0,
            concat_axis=0,
            tiled=True,
        )
        out_weight_grad = jnp.einsum(
            "sech,secd->ehd", attended, incoming_grad, preferred_element_type=jnp.float32
        )
        att_grad = jnp.einsum(
            "secd,ehd->sech", incoming_grad, out_weights, preferred_element_type=jnp.float32
        ).astype(jnp.bfloat16)
        total_rows = queries.shape[0] * queries.shape[1] * queries.shape[2]
        head = queries.shape[3]
        keyval_part, flat_query_grad = attend_back(
            queries.reshape(total_rows, head),
            position.reshape(total_rows),
            tops,
            totals,
            att_grad.reshape(total_rows, head),
            segment,
            bounds,
            keep_group,
            keyval,
        )
        query_grad = flat_query_grad.reshape(queries.shape)
        query_weight_grad = jnp.einsum(
            "secd,sech->edh", inputs, query_grad, preferred_element_type=jnp.float32
        )
        row_grad = jnp.einsum(
            "sech,edh->secd", query_grad, query_weights, preferred_element_type=jnp.float32
        ).astype(jnp.bfloat16)
        back_rows = lax.all_to_all(
            row_grad, "exp", split_axis=0, concat_axis=0, tiled=True
        ).reshape(experts, capacity, width)
        normed_grad = normed_grad + jnp.einsum(
            "tks,sd->td",
            slot_hot,
            back_rows.reshape(experts * capacity, width),
            preferred_element_type=jnp.float32,
        )
        keyval_grad = lax.psum_scatter(
            keyval_part.astype(jnp.bfloat16), "exp", scatter_dimension=0, tiled=True
        )
        kv_weight_grad = jnp.einsum(
            "td,tc->dc", normed, keyval_grad, preferred_element_type=jnp.float32
        )
        normed_grad = normed_grad + jnp.einsum(
            "tc,dc->td", keyval_grad, w_kv[layer_no], preferred_element_type=jnp.float32
        )
        _, first_back = jax.vjp(normalize, resident, norm1_gain[layer_no], norm1_bias[layer_no])
        resident_part, gain1_grad, bias1_grad = first_back(normed_grad)
        stream_grad = middle_grad + resident_part
        results = (
            gain1_grad,
            bias1_grad,
            kv_weight_grad,
            router_grad,
            query_weight_grad,
            out_weight_grad,
            gain2_grad,
            bias2_grad,
            up_grad,
            down_grad,
        )
        for which in range(10):
            grad_lists[which][layer_no] = results[which]
    stacked = [jnp.stack(entries) for entries in grad_lists]
    counts = jnp.stack(count_list)
    expert_query = stacked[4]
    expert_output = stacked[5]
    expert_query, expert_output = (
        lax.psum(expert_query.astype(jnp.bfloat16), "dp").astype(jnp.float32),
        lax.psum(expert_output.astype(jnp.bfloat16), "dp").astype(jnp.float32),
    )
    shared = lax.psum(
        (
            stacked[0],
            stacked[1],
            stacked[2],
            stacked[3],
            stacked[6],
            stacked[7],
            stacked[8],
            stacked[9],
            counts,
        ),
        ("exp", "dp"),
    )
    return (
        activations,
        stream_grad[None],
        shared[0],
        shared[1],
        shared[2],
        shared[3],
        expert_query,
        expert_output,
        shared[4],
        shared[5],
        shared[6],
        shared[7],
        shared[8],
    )


def solution(mesh):
    return jax.shard_map(
        body,
        mesh=mesh,
        in_specs=(
            P("dp", "exp", None),
            P("dp", "exp", None),
            P(None, "dp", None, None),
            P("dp", None),
            P("dp", None),
            P(),
            P(),
            P(),
            P(),
            P(None, "exp", None, None),
            P(None, "exp", None, None),
            P(),
            P(),
            P(),
            P(),
        ),
        out_specs=(
            P("dp", "exp", None),
            P("dp", "exp", None),
            P(),
            P(),
            P(),
            P(),
            P(None, "exp", None, None),
            P(None, "exp", None, None),
            P(),
            P(),
            P(),
            P(),
            P(),
        ),
        check_vma=False,
    )
```

profile of v0, /device:TPU:0, one launch (start us, length us, event | category | flops | bytes accessed | tf_op | source)
XLA Modules:
  0.0 1250.9 jit_solution(13395813842500498259)
XLA Ops:
  19.2 4.1 convolution_convert_fusion.3
  23.3 6.3 all-to-all-start
  31.1 4.2 reduce-window.41
  40.4 5.2 reduce-window.34
  51.1 4.0 convert_reduce_fusion.6
  59.3 48.7 %all_gather.6 = bf16[1024,128]{1,0:T(8,128)(2,1)S(1)} all-gather(bf16[256,128]{1,0:T(8,128)(2,1)S(1)} %convolution_convert_fusion.5), channel_id=1, replica_groups=mesh['exp'=4,'dp'=8] {'exp'}, dimensions={0}, use_global_device_ids=true | all-gather | bytes 327680 | tf_op jit(solution)/shard_map/all_gather | solution.py:174
  109.6 3.1 fusion.210
  115.0 38.6 %while.58 = (s32[]{:T(128)}, bf16[6,512,64]{1,2,0:T(8,128)(2,1)S(1)}, f32[6,512]{1,0:T(8,128)S(1)}, f32[6,512]{1,0:T(8,128)S(1)}, s32[6,512]{1,0:T(8,128)}, /*in...) while((s32[]{:T(128)}, ...), condition=%wide.region_19.20_spmd, body=%wide.region_15.19_spmd.sunk | while | flops 151039488 | bytes 7596245 | solution.py:67
  157.7 4.9 all-to-all-start.1
  165.7 64.4 %all-to-all-done.1 = bf16[4,6,128,512]{3,2,1,0:T(8,128)(2,1)S(1)} async-done(((bf16[4,6,128,512]{3,2,1,0:T(8,128)(2,1)}), bf16[4,6,128,512]{3,2,1,0:T(8,128)(2,1)S(1)}, u32[]{:S(2)}, u32[]{:S(2)}) %all-to-all-start.1) | async-done | bytes 3145760 | tf_op jit(solution)/shard_map/all_to_all | solution.py:214
  230.1 8.0 fusion.78
  243.0 3.1 convolution_convert_fusion.2
  246.1 4.8 all-to-all-start.2
  251.2 77.6 %all_gather.7 = bf16[1024,128]{1,0:T(8,128)(2,1)S(1)} all-gather(bf16[256,128]{1,0:T(8,128)(2,1)S(1)} %convolution_convert_fusion.4), channel_id=1, replica_groups=mesh['exp'=4,'dp'=8] {'exp'}, dimensions={0}, use_global_device_ids=true | all-gather | bytes 327680 | tf_op jit(solution)/shard_map/all_gather | solution.py:174
  328.9 3.0 fusion.207
  333.2 33.5 %while.59 = (s32[]{:T(128)}, bf16[6,512,64]{1,2,0:T(8,128)(2,1)S(1)}, f32[6,512]{1,0:T(8,128)S(1)}, f32[6,512]{1,0:T(8,128)S(1)}, s32[6,512]{1,0:T(8,128)S(1)}, ...) while((s32[]{:T(128)}, ...), condition=%wide.region_40.41_spmd, body=%wide.region_36.40_spmd.sunk | while | flops 151039488 | bytes 6940857 | solution.py:67
  374.6 5.0 all-to-all-start.3
  380.0 67.6 %all-to-all-done.3 = bf16[4,6,128,512]{3,2,1,0:T(8,128)(2,1)} async-done(((bf16[4,6,128,512]{3,2,1,0:T(8,128)(2,1)}), bf16[4,6,128,512]{3,2,1,0:T(8,128)(2,1)}, u32[]{:S(2)}, u32[]{:S(2)}) %all-to-all-start.3) | async-done | bytes 3145760 | tf_op jit(solution)/shard_map/all_to_all | solution.py:214
  447.7 9.1 fusion.80
  465.1 7.1 fusion.102
  472.1 5.1 all-to-all-start.4
  477.3 70.2 %all-to-all-done.4 = bf16[4,6,128,512]{3,2,1,0:T(8,128)(2,1)} async-done(((bf16[4,6,128,512]{3,2,1,0:T(8,128)(2,1)}), bf16[4,6,128,512]{3,2,1,0:T(8,128)(2,1)}, u32[]{:S(2)}, u32[]{:S(2)}) %all-to-all-start.4) | async-done | bytes 3145760 | tf_op jit(solution)/shard_map/all_to_all | solution.py:309
  547.5 3.8 fusion.216
  554.2 56.0 %while.60 = (s32[]{:T(128)}, f32[1024,64]{0,1:T(8,128)S(1)}, f32[1024,64]{0,1:T(8,128)S(1)}, bf16[6,512,64]{1,2,0:T(8,128)(2,1)}, s32[6,512]{1,0:T(8,128)}, /*in...) while((s32[]{:T(128)}, f32[1024,64]{0,1:T(8,128)S(1)}, ...), condition=%wide.region_52.53_spmd.clone, body=%wide.region_49.52_spmd.clone.sunk | while | flops 344862720 | bytes 17799396 | solution.py:115
  565.0 2.4 select_divide_fusion.4
  574.4 2.4 select_divide_fusion.4
  593.1 2.4 select_divide_fusion.4
  602.4 2.4 select_divide_fusion.4
  617.7 4.6 all-to-all-start.5
  622.4 5.0 convert_reduce_fusion.5
  628.3 68.5 %all-to-all-done.5 = bf16[4,6,128,512]{3,2,1,0:T(8,128)(2,1)} async-done(((bf16[4,6,128,512]{3,2,1,0:T(8,128)(2,1)}), bf16[4,6,128,512]{3,2,1,0:T(8,128)(2,1)}, u32[]{:S(2)}, u32[]{:S(2)}) %all-to-all-start.5) | async-done | bytes 3145760 | tf_op jit(solution)/shard_map/all_to_all | solution.py:342
  696.8 3.3 fusion.368
  704.0 3.5 fusion.114
  712.0 7.1 fusion.105
  719.1 4.8 all-to-all-start.6
  724.3 4.2 convolution_bitcast_fusion.2
  728.5 3.0 convolution_bitcast_fusion
  731.5 3.3 fusion.205
  735.0 3.3 fusion.199
  739.6 4.2 convolution_bitcast_fusion.3
  746.0 4.4 pad_maximum_fusion.1
  750.4 43.7 %all-to-all-done.6 = bf16[4,6,128,512]{3,2,1,0:T(8,128)(2,1)} async-done(((bf16[4,6,128,512]{3,2,1,0:T(8,128)(2,1)}), bf16[4,6,128,512]{3,2,1,0:T(8,128)(2,1)}, u32[]{:S(2)}, u32[]{:S(2)}) %all-to-all-start.6) | async-done | bytes 3145760 | tf_op jit(solution)/shard_map/all_to_all | solution.py:309
  794.1 3.7 fusion.213
  800.0 45.5 %while.61 = (s32[]{:T(128)}, f32[1024,64]{0,1:T(8,128)S(1)}, f32[1024,64]{0,1:T(8,128)S(1)}, bf16[6,512,64]{1,2,0:T(8,128)(2,1)}, s32[6,512]{1,0:T(8,128)}, /*in...) while((s32[]{:T(128)}, f32[1024,64]{0,1:T(8,128)S(1)}, ...), condition=%wide.region_64.65_spmd.clone, body=%wide.region_61.64_spmd.clone.sunk | while | flops 344862720 | bytes 17930468 | solution.py:115
  801.5 2.4 select_divide_fusion.5
  809.1 2.4 select_divide_fusion.5
  816.7 2.4 select_divide_fusion.5
  824.3 2.4 select_divide_fusion.5
  831.9 2.4 select_divide_fusion.5
  839.4 2.4 select_divide_fusion.5
  847.9 2.7 fusion.202
  854.5 8.0 pad_maximum_fusion
  862.4 4.3 reduce-scatter.5.cloned.1.call-done
  873.0 4.9 all-to-all-start.7
  878.0 5.1 convert_reduce_fusion.4
  883.2 3.1 fusion.219
  886.5 41.5 %all-reduce.8.cloned.1.call-done = (bf16[2,6,512,64]{2,3,1,0:T(8,128)(2,1)}, bf16[2,6,64,512]{3,2,1,0:T(8,128)(2,1)}) async-done(((bf16[2,6,512,64]{2,3,1,0:T(8,128)(2,1)}, bf16[2,6,64,512]{3,2,1,0:T(8,128)(2,1)}), (bf16[2,6,512,64]{2,3,1,0:T(8,128)(2,1)}, bf16[2,6,64,512]{3,2,1,0:T(8,128)(2,1)})) %all-reduce.8.cloned.1.call-update) | async-done | bytes 1572880 | tf_op jit(solution)/shard_map/psum | solution.py:382
  928.0 2.6 convert_element_type.339
  932.0 18.8 %all-to-all-done.7 = bf16[4,6,128,512]{3,2,1,0:T(8,128)(2,1)} async-done(((bf16[4,6,128,512]{3,2,1,0:T(8,128)(2,1)}), bf16[4,6,128,512]{3,2,1,0:T(8,128)(2,1)}, u32[]{:S(2)}, u32[]{:S(2)}) %all-to-all-start.7) | async-done | bytes 3145760 | tf_op jit(solution)/shard_map/all_to_all | solution.py:342
  950.8 3.0 fusion.369
  954.9 41.5 %all-reduce = (f32[2,512]{1,0:T(2,128)}, f32[2,512]{1,0:T(2,128)}, f32[2,512]{1,0:T(2,128)}, f32[2,512]{1,0:T(2,128)}, f32[2,24]{1,0:T(2,128)}) all-reduce(f32[2,512]{1,0:T(2,128)S(1)} %pad_maximum_fusion.8, f32[2,512]{1,0:T(2,128)S(1)} %pad_maximum_fusion.9, ...), channel_id=1, replica_groups=mesh['exp'=4,'dp'=8] {'exp','dp'}, use_global_device_ids=true, to_apply=%region_70.71 | all-reduce | flops 4144 | bytes 33152 | tf_op jit(solution)/shard_map/psum | solution.py:385
  997.4 231.7 %all-reduce.6.cloned.1.call-done = (f32[2,512,128]{2,1,0:T(8,128)}, f32[2,512,24]{1,2,0:T(8,128)}, f32[2,512,2048]{2,1,0:T(8,128)}, f32[2,2048,512]{2,1,0:T(8,128)}) async-done(((f32[2,512,128]{2,1,0:T(8,128)}, f32[2,512,24]{1,2,0:T(8,128)}, f32[2,512,2048]{2,1,0:T(8,128)}, f32[2,2048,512]{2,1,0:T(8,128)}), (f32[2,512,128]{2,1,0:T(8,128)}, f32[2,512,24]{1,2,0:T(8,128)}, f32[2,512,2048]{2,1,0:T(8,128)}, ...) | async-done | bytes 17399824 | tf_op jit(solution)/shard_map/psum | solution.py:385
  1232.7 8.0 copy.428
  1240.7 3.4 copy.429
  (675 shorter events, 255.2 us)
Async XLA Ops:
  7.2 16.1 %copy-start.120 = (s32[128]{0:T(128)}, s32[128]{0:T(128)S(1)}, u32[]{:S(2)}) copy-start(s32[128]{0:T(128)S(1)} %iota_add_fusion) | copy-start | bytes 1540
  8.3 15.0 %copy-start.74 = (f32[256]{0:T(256)}, f32[256]{0:T(256)S(1)}, u32[]{:S(2)}) copy-start(f32[256]{0:T(256)S(1)} %broadcast_multiply_fusion.3) | copy-start | bytes 3076
  9.5 13.8 %copy-start.91 = (f32[256]{0:T(256)}, f32[256]{0:T(256)S(1)}, u32[]{:S(2)}) copy-start(f32[256]{0:T(256)S(1)} %fusion.333) | copy-start | bytes 3076
  10.8 12.4 copy-start.61
  12.2 11.1 copy-start.114
  13.6 9.6 copy-start.48
  18.5 4.8 copy-start.98
  23.3 6.3 copy-start.130
  23.3 86.3 %all-to-all-start = ((bf16[4,6,128,512]{3,2,1,0:T(8,128)(2,1)}), bf16[4,6,128,512]{3,2,1,0:T(8,128)(2,1)S(1)}, u32[]{:S(2)}, u32[]{:S(2)}) async-start(bf16[4,6,128,512]{3,2,1,0:T(8,128)(2,1)} %bitcast.578), calls=%async_computation | async-start | bytes 6291456 | tf_op jit(solution)/shard_map/all_to_all | solution.py:182
  29.6 27.6 %copy-start.1 = (bf16[1,256,512]{2,1,0:T(8,128)(2,1)S(1)}, bf16[1,256,512]{2,1,0:T(8,128)(2,1)}, u32[]{:S(2)}) copy-start(bf16[1,256,512]{2,1,0:T(8,128)(2,1)} %param.23) | copy-start | bytes 786436
  58.1 50.6 %copy-start.22 = (bf16[256,512]{1,0:T(8,128)(2,1)}, bf16[256,512]{1,0:T(8,128)(2,1)S(1)}, u32[]{:S(2)}) copy-start(bf16[256,512]{1,0:T(8,128)(2,1)S(1)} %fusion.276) | copy-start | bytes 786436
  109.6 5.4 copy-start.24
  157.7 6.1 copy-start.42
  157.7 6.2 copy-start.51
  157.7 6.2 copy-start.105
  157.7 7.9 copy-start.65
  157.7 72.4 %all-to-all-start.1 = ((bf16[4,6,128,512]{3,2,1,0:T(8,128)(2,1)}), bf16[4,6,128,512]{3,2,1,0:T(8,128)(2,1)S(1)}, u32[]{:S(2)}, u32[]{:S(2)}) async-start(bf16[4,6,128,512]{3,2,1,0:T(8,128)(2,1)} %copy.199), calls=%async_computation.1 | async-start | bytes 6291456 | tf_op jit(solution)/shard_map/all_to_all | solution.py:214
  163.8 74.2 %copy-start.89 = (f32[256]{0:T(256)}, f32[256]{0:T(256)S(1)}, u32[]{:S(2)}) copy-start(f32[256]{0:T(256)S(1)} %reduce_max.36) | copy-start | bytes 3076
  165.6 72.9 %copy-start.57 = (f32[1,512]{1,0:T(1,128)}, f32[1,512]{1,0:T(1,128)S(1)}, u32[]{:S(2)}) copy-start(f32[1,512]{1,0:T(1,128)S(1)} %get-tuple-element.750) | copy-start | bytes 6148
  165.6 72.5 %copy-start.80 = (f32[256,8]{0,1:T(8,128)}, f32[256,8]{0,1:T(8,128)S(1)}, u32[]{:S(2)}) copy-start(f32[256,8]{0,1:T(8,128)S(1)} %fusion.320) | copy-start | bytes 24580
  165.6 72.5 %copy-start.78 = (s32[256,8]{0,1:T(8,128)}, s32[256,8]{0,1:T(8,128)S(1)}, u32[]{:S(2)}) copy-start(s32[256,8]{0,1:T(8,128)S(1)} %multiply_add_fusion.1) | copy-start | bytes 24580
  165.6 77.4 %copy-start.100 = (s32[24,128]{1,0:T(8,128)}, s32[24,128]{1,0:T(8,128)S(1)}, u32[]{:S(2)}) copy-start(s32[24,128]{1,0:T(8,128)S(1)} %broadcast_minimum_fusion) | copy-start | bytes 36868
  230.1 9.0 copy-start.17
  238.2 470.7 %copy-start.72 = (f32[256]{0:T(256)}, f32[256]{0:T(256)S(1)}, u32[]{:S(2)}) copy-start(f32[256]{0:T(256)S(1)} %broadcast_multiply_fusion.2) | copy-start | bytes 3076
  246.1 4.8 copy-start.60
  246.1 4.8 copy-start.34
  246.1 82.8 %all-to-all-start.2 = ((bf16[4,6,128,512]{3,2,1,0:T(8,128)(2,1)}), bf16[4,6,128,512]{3,2,1,0:T(8,128)(2,1)}, u32[]{:S(2)}, u32[]{:S(2)}) async-start(bf16[4,6,128,512]{3,2,1,0:T(8,128)(2,1)} %bitcast.581), calls=%async_computation.2 | async-start | bytes 6291456 | tf_op jit(solution)/shard_map/all_to_all | solution.py:182
  374.5 5.0 copy-start.49
  374.5 5.0 copy-start.103
  374.5 5.1 copy-start.44
  374.5 5.2 copy-start.52
  374.6 73.1 %all-to-all-start.3 = ((bf16[4,6,128,512]{3,2,1,0:T(8,128)(2,1)}), bf16[4,6,128,512]{3,2,1,0:T(8,128)(2,1)}, u32[]{:S(2)}, u32[]{:S(2)}) async-start(bf16[4,6,128,512]{3,2,1,0:T(8,128)(2,1)} %copy.211), calls=%async_computation.3 | async-start | bytes 6291456 | tf_op jit(solution)/shard_map/all_to_all | solution.py:214
  379.6 84.1 %copy-start.112 = (f32[1,256]{1,0:T(1,128)}, f32[1,256]{1,0:T(1,128)S(1)}, u32[]{:S(2)}) copy-start(f32[1,256]{1,0:T(1,128)S(1)} %fusion.328) | copy-start | bytes 3076
  447.7 9.5 copy-start.18
  456.9 6.5 copy-start.70
  457.1 6.3 copy-start.82
  463.9 8.3 copy-start.13
  472.1 75.3 %all-to-all-start.4 = ((bf16[4,6,128,512]{3,2,1,0:T(8,128)(2,1)}), bf16[4,6,128,512]{3,2,1,0:T(8,128)(2,1)}, u32[]{:S(2)}, u32[]{:S(2)}) async-start(bf16[4,6,128,512]{3,2,1,0:T(8,128)(2,1)} %bitcast.582), calls=%async_computation.4 | async-start | bytes 6291456 | tf_op jit(solution)/shard_map/all_to_all | solution.py:309
  477.3 76.9 %copy-start.47 = (s32[8]{0:T(128)S(1)}, s32[8]{0:T(128)}, u32[]{:S(2)}) copy-start(s32[8]{0:T(128)} %copy-done.46) | copy-start | bytes 100
  617.7 79.1 %all-to-all-start.5 = ((bf16[4,6,128,512]{3,2,1,0:T(8,128)(2,1)}), bf16[4,6,128,512]{3,2,1,0:T(8,128)(2,1)}, u32[]{:S(2)}, u32[]{:S(2)}) async-start(bf16[4,6,128,512]{3,2,1,0:T(8,128)(2,1)} %copy.218), calls=%async_computation.5 | async-start | bytes 6291456 | tf_op jit(solution)/shard_map/all_to_all | solution.py:342
  622.4 78.8 %reduce-scatter.3.cloned.1.call-start = ((), (), s32[]{:S(2)}) async-start(), calls=%async_computation.10 | async-start | bytes 327680 | tf_op jit(solution)/shard_map/reduce_scatter | solution.py:351
  709.4 9.7 copy-start.15
  719.1 5.2 copy-start.71
  719.1 5.2 copy-start.83
  719.1 75.0 %all-to-all-start.6 = ((bf16[4,6,128,512]{3,2,1,0:T(8,128)(2,1)}), bf16[4,6,128,512]{3,2,1,0:T(8,128)(2,1)}, u32[]{:S(2)}, u32[]{:S(2)}) async-start(bf16[4,6,128,512]{3,2,1,0:T(8,128)(2,1)} %bitcast.579), calls=%async_computation.7 | async-start | bytes 6291456 | tf_op jit(solution)/shard_map/all_to_all | solution.py:309
  723.9 142.9 %reduce-scatter.5.cloned.1.call-start = ((), (), s32[]{:S(2)}) async-start(), calls=%async_computation.11 | async-start | bytes 327680 | tf_op jit(solution)/shard_map/reduce_scatter | solution.py:351
  734.9 4.7 copy-start.58
  734.9 4.7 copy-start.73
  746.0 48.1 %copy-start.38 = (bf16[2,6,64,512]{3,2,1,0:T(8,128)(2,1)S(1)}, bf16[2,6,64,512]{3,2,1,0:T(8,128)(2,1)}, u32[]{:S(2)}) copy-start(bf16[2,6,64,512]{3,2,1,0:T(8,128)(2,1)} %param.33) | copy-start | bytes 2359300
  750.4 49.6 %copy-start.5 = (bf16[1024,64]{1,0:T(8,128)(2,1)S(1)}, bf16[1024,64]{1,0:T(8,128)(2,1)}, u32[]{:S(2)}) copy-start(bf16[1024,64]{1,0:T(8,128)(2,1)} %get-tuple-element.1312) | copy-start | bytes 393220
  750.4 49.6 %copy-start.6 = (bf16[1024,64]{1,0:T(8,128)(2,1)S(1)}, bf16[1024,64]{1,0:T(8,128)(2,1)}, u32[]{:S(2)}) copy-start(bf16[1024,64]{1,0:T(8,128)(2,1)} %get-tuple-element.1313) | copy-start | bytes 393220
  847.9 80.1 %all-reduce.8.cloned.1.call-start = ((), (), s32[]{:S(2)}) async-start(), calls=%async_computation.13 | async-start | bytes 3145728 | tf_op jit(solution)/shard_map/psum | solution.py:382
  853.5 375.6 %all-reduce.6.cloned.1.call-start = ((), (), s32[]{:S(2)}) async-start(), calls=%async_computation.12 | async-start | bytes 34799616 | tf_op jit(solution)/shard_map/psum | solution.py:385
  854.5 12.3 copy-start.76
  854.5 12.3 copy-start.93
  854.5 12.3 copy-start.116
  873.0 4.9 copy-start.79
  873.0 10.0 copy-start.63
  873.0 10.1 copy-start.9
  873.0 77.8 %all-to-all-start.7 = ((bf16[4,6,128,512]{3,2,1,0:T(8,128)(2,1)}), bf16[4,6,128,512]{3,2,1,0:T(8,128)(2,1)}, u32[]{:S(2)}, u32[]{:S(2)}) async-start(bf16[4,6,128,512]{3,2,1,0:T(8,128)(2,1)} %copy.225), calls=%async_computation.8 | async-start | bytes 6291456 | tf_op jit(solution)/shard_map/all_to_all | solution.py:342
  928.0 22.8 %copy-start.28 = (bf16[256,3072]{1,0:T(8,128)(2,1)S(1)}, bf16[256,3072]{1,0:T(8,128)(2,1)}, u32[]{:S(2)}) copy-start(bf16[256,3072]{1,0:T(8,128)(2,1)} %convert_reduce_fusion.4) | copy-start | bytes 4718596
  953.9 42.5 %copy-start.16 = (f32[256,512]{1,0:T(8,128)S(1)}, f32[256,512]{1,0:T(8,128)}, u32[]{:S(2)}) copy-start(f32[256,512]{1,0:T(8,128)} %copy-done.15) | copy-start | bytes 1572868
  1231.0 9.7 slice-start
  1232.7 8.0 slice-start.1
  (86 other events, 210.3 us)
Sparse Core Ops, SparseCore 0:
  628.4 24.7 reduce-scatter.2
  848.0 18.7 reduce-scatter.4
  870.6 57.3 all-reduce.7
  936.6 292.5 all-reduce.5
where the time goes:
time: 1270 us; the launch traced here: 1250 us
  waiting for transfers between devices  611 us (48%)
  matrix products  237 us (19%)
  blocking collectives  168 us (13%)
  local copies, waits for them, and re-layouts  92.8 us (7%)
  other arithmetic  85.1 us (7%)
  starting transfers between devices  41 us (3%)
  between operations  15.8 us (1%)
    psum x1, waiting for transfers between devices, body(): lax.psum((stacked[0], stacked[1], stacked[2], stacked[3], stacked[6], sta...  232 us
    all_to_all x2, waiting for transfers between devices, body(): lax.all_to_all(outputs, 'exp', split_axis=0, concat_axis=0, tiled=True)  132 us
    all_gather x2, blocking collectives, body(): keyval = lax.all_gather(keyval_own, 'exp', axis=0, tiled=True)  126 us
    all_to_all x2, waiting for transfers between devices, body(): lax.all_to_all(out_grad.reshape(exp_count, local_experts, capacity, width...  114 us
    all_to_all x2, waiting for transfers between devices, body(): lax.all_to_all(row_grad, 'exp', split_axis=0, concat_axis=0, tiled=True)  87.3 us
    dot_general x24, matrix products, block_scores(): jnp.einsum('rh,kh->rk', block_rows, keys, preferred_element_type=jnp.floa...  54.8 us
    psum x1, waiting for transfers between devices, body(): lax.psum(expert_query.astype(jnp.bfloat16), 'dp').astype(jnp.float32)  41.5 us
    psum x1, blocking collectives, body(): lax.psum((stacked[0], stacked[1], stacked[2], stacked[3], stacked[6], sta...  41.5 us
  transfers between devices with their start and end apart: 12, of which 9 were waited for; matrix products, arithmetic and copies ran while one was open for 8% of the time, Pallas kernels for 0%

commit v1 on v0

v1 whole, which is shorter than its diff:
```python
from functools import partial
import math

import jax
import jax.numpy as jnp
from jax import lax
from jax.experimental import pallas as pl
from jax.experimental.pallas import tpu as pltpu
from jax.sharding import PartitionSpec as P

F32 = jnp.float32
BF16 = jnp.bfloat16
LANES = 128
epsilon = 1e-05
neg_big = -1e30
never = 1 << 30
gelu_c = 0.7978845608028654
gelu_a = 0.044715
VMEM_LIMIT = 56 << 20


def nn(a, b):
    return jnp.dot(a, b, preferred_element_type=F32)


def nt(a, b):
    return lax.dot_general(a, b, (((1,), (1,)), ((), ())), preferred_element_type=F32)


def tn(a, b):
    return lax.dot_general(a, b, (((0,), (0,)), ((), ())), preferred_element_type=F32)


def iota(shape, axis):
    return lax.broadcasted_iota(jnp.int32, shape, axis)


def norm_parts(values):
    center = values - jnp.mean(values, axis=-1, keepdims=True)
    spread = jnp.mean(center * center, axis=-1, keepdims=True)
    scale = lax.rsqrt(spread + epsilon)
    return center * scale, scale


def norm_back(hat, scale, gain, grad):
    scaled = grad * gain
    first = jnp.mean(scaled, axis=-1, keepdims=True)
    second = jnp.mean(scaled * hat, axis=-1, keepdims=True)
    back = scale * (scaled - first - hat * second)
    return back, jnp.sum(grad * hat, axis=0, keepdims=True), jnp.sum(grad, axis=0, keepdims=True)


def gelu_parts(v):
    inner = jnp.tanh(gelu_c * (v + gelu_a * v * v * v))
    half = 0.5 * (1.0 + inner)
    return v * half, half + 0.5 * v * (1.0 - inner * inner) * gelu_c * (1.0 + 3.0 * gelu_a * v * v)


def lane_half(shape):
    return (iota(shape, 1) >= LANES // 2).astype(jnp.int32)


def select_tiles(dense, chosen):
    out = jnp.zeros(chosen.shape, F32)
    for tile in range(dense.shape[1] // LANES):
        out = jnp.where(chosen == 2 * tile, dense[:, tile * LANES : (tile + 1) * LANES], out)
    return out


def place_tiles(dense, chosen, values):
    for tile in range(dense.shape[1] // LANES):
        where = slice(tile * LANES, (tile + 1) * LANES)
        dense[:, where] = jnp.where(chosen == 2 * tile, values, dense[:, where])


def own_columns(ref, count):
    start = lax.axis_index("exp") * count
    return ref[:, pl.ds(pl.multiple_of(start, count), count)]


def spread_routes(routes, spread):
    topk, count, lanes = spread.shape
    own = own_columns(routes, count)
    for k in range(topk):
        spread[k] = jnp.broadcast_to(own[k : k + 1, :], (lanes, count)).T


def fill_mask(lengths, keep, mask):
    group, count = mask.shape
    start = lax.axis_index("exp") * count
    position = start + iota((1, count), 1)
    low = jnp.zeros((1, count), jnp.int32)
    end = 0
    for s in range(lengths.shape[1] - 1):
        end = end + lengths[0, s]
        low = jnp.where(position >= end, end, low)
    kept = jnp.broadcast_to(keep[...], (LANES, group)).T
    kept = jnp.concatenate([kept] * (count // LANES), axis=1)
    key = iota((group, count), 0)
    usable = jnp.where(kept > 0, key, never)
    allowed = ((usable >= low) & (usable <= position)) | (key == position)
    mask[...] = jnp.where(allowed, 0.0, neg_big)


def split_keyval(keyval):
    both = keyval.astype(F32)
    swapped = pltpu.roll(both, LANES // 2, 1)
    first = iota(both.shape, 1) < LANES // 2
    return jnp.where(first, both, swapped), jnp.where(first, swapped, both)


def pre_layer(x, gain1, bias1, w_kv, normed, keyval_own):
    hat, _ = norm_parts(x)
    normed[...] = (hat * gain1 + bias1).astype(BF16)
    keyval_own[...] = nn(normed[...], w_kv).astype(BF16)


def make_gates(normed, w_router, spread):
    logits = nt(normed, w_router)
    experts = logits.shape[1]
    lanes = iota(logits.shape, 1)
    picked = spread[0][:, :experts] == lanes
    for k in range(1, spread.shape[0]):
        picked = picked | (spread[k][:, :experts] == lanes)
    top = jnp.max(jnp.where(picked, logits, neg_big), axis=1, keepdims=True)
    shares = jnp.where(picked, jnp.exp(jnp.minimum(logits - top, 0.0)), 0.0)
    return shares / jnp.sum(shares, axis=1, keepdims=True), picked


def gate_column(gates, spread_k):
    lanes = iota(gates.shape, 1)
    return jnp.sum(
        jnp.where(spread_k[:, : gates.shape[1]] == lanes, gates, 0.0), axis=1, keepdims=True
    )


def layer_forward(x, normed, weights, mask, spread, dense, gated, kept):
    count = normed.shape[0]
    gates, picked = make_gates(normed[...], weights.w_router[...], spread)
    kept.gates[...] = gates
    dense[...] = nt(normed[...], weights.w_query[...]).astype(BF16).astype(F32) * 0.125
    gated[...] = jnp.zeros(gated.shape, F32)
    keys, values = split_keyval(kept.keyval[...])
    keys = keys.astype(BF16)
    values_t = values.T.astype(BF16)

    def slot(k, carry):
        which = spread[k]
        chosen = which - lane_half((count, LANES))
        query = select_tiles(dense, chosen).astype(BF16)
        kept.query[k] = query
        scores = nt(keys, query) + mask[...]
        top = jnp.max(scores, axis=0, keepdims=True)
        shares = jnp.exp(scores - top)
        total = jnp.sum(shares, axis=0, keepdims=True)
        kept.lse[k] = jnp.broadcast_to(top + jnp.log(total), kept.lse.shape[1:])
        shares = (shares * (1.0 / total)).astype(BF16)
        attended = nn(values_t, shares).T.astype(BF16)
        kept.attended[k] = attended
        gate = gate_column(kept.gates[...], which)
        place_tiles(gated, chosen, gate * attended.astype(F32))
        return carry

    lax.fori_loop(0, spread.shape[0], slot, 0)
    kept.gated[...] = gated[...].astype(BF16)
    middle = x + nn(kept.gated[...], weights.w_out[...])
    kept.middle[...] = middle
    hat, _ = norm_parts(middle)
    normed2 = (hat * weights.gain2[...] + weights.bias2[...]).astype(BF16)
    active = gelu_parts(nn(normed2, weights.w_up[...]))[0].astype(BF16)
    return middle + nn(active, weights.w_down[...]), picked


def layer_back(stream_grad, normed, weights, mask, spread, dense, gated, kept, sums, out):
    count, width = normed.shape
    hidden = weights.w_up.shape[1]
    branch = stream_grad.astype(BF16)
    hat2, scale2 = norm_parts(kept.middle[...])
    normed2 = (hat2 * weights.gain2[...] + weights.bias2[...]).astype(BF16)
    normed2_t = normed2.astype(F32).T.astype(BF16)
    sums.wide[...] = jnp.zeros(sums.wide.shape, F32)

    blocks = out.up.shape[0]
    piece = hidden // blocks
    own = weights.w_query.shape[0] // blocks

    def part(c, carry):
        cols = pl.ds(pl.multiple_of(c * piece, piece), piece)
        active, slope = gelu_parts(nn(normed2, weights.w_up[:, cols]))
        out.down[c, 0:piece, :] = nn(active.T.astype(BF16), branch).astype(BF16)
        upper_grad = (nt(branch, weights.w_down[cols, :]) * slope).astype(BF16)
        out.up[c, 0:width, :] = nn(normed2_t, upper_grad).astype(BF16)
        sums.wide[...] += nt(upper_grad, weights.w_up[:, cols])
        return carry

    lax.fori_loop(0, blocks, part, 0)
    back, gain2_grad, bias2_grad = norm_back(hat2, scale2, weights.gain2[...], sums.wide[...])
    out.small[2:3, :] = gain2_grad
    out.small[3:4, :] = bias2_grad
    middle_grad = stream_grad + back
    out.middle_grad[...] = middle_grad
    rounded = middle_grad.astype(BF16)
    gated_t = kept.gated[...].astype(F32).T.astype(BF16)
    for block in range(blocks):
        rows = slice(block * own, (block + 1) * own)
        out.w_out[block, 0:own, :] = nn(gated_t[rows], rounded).astype(BF16)
    dense[...] = nt(rounded, weights.w_out[...])
    gated[...] = jnp.zeros(gated.shape, F32)
    keys, values = split_keyval(kept.keyval[...])
    keys_t = keys.T.astype(BF16)
    keys = keys.astype(BF16)
    values = values.astype(BF16)
    sums.keys[...] = jnp.zeros(sums.keys.shape, F32)
    sums.values[...] = jnp.zeros(sums.values.shape, F32)
    sums.gates[...] = jnp.zeros(sums.gates.shape, F32)
    lanes = iota(sums.gates.shape, 1)

    def slot(k, carry):
        which = spread[k]
        chosen = which - lane_half((count, LANES))
        grad = select_tiles(dense, chosen)
        gate = gate_column(kept.gates[...], which)
        gate_grad = jnp.sum(grad * kept.attended[k].astype(F32), axis=1, keepdims=True)
        sums.gates[...] += jnp.where(which[:, : lanes.shape[1]] == lanes, gate * gate_grad, 0.0)
        att_grad = (gate * grad).astype(BF16)
        query = kept.query[k]
        shares = jnp.exp(nt(keys, query) + mask[...] - kept.lse[k, 0:1, :])
        sums.values[...] += nn(shares.astype(BF16), att_grad)
        share_grad = nt(values, att_grad)
        score_grad = shares * (share_grad - jnp.sum(share_grad * shares, axis=0, keepdims=True))
        score_grad = score_grad.astype(BF16)
        sums.keys[...] += nn(score_grad, query)
        query_grad = nn(keys_t, score_grad).T * 0.125
        place_tiles(gated, chosen, query_grad.astype(BF16).astype(F32))
        return carry

    lax.fori_loop(0, kept.query.shape[0], slot, 0)
    both_keys = sums.keys[...] + pltpu.roll(sums.keys[...], LANES // 2, 1)
    both_values = sums.values[...] + pltpu.roll(sums.values[...], LANES // 2, 1)
    first = iota(both_keys.shape, 1) < LANES // 2
    out.keyval[...] = jnp.where(first, both_keys, both_values).astype(BF16)
    weighted = sums.gates[...]
    logit_grad = weighted - kept.gates[...] * jnp.sum(weighted, axis=1, keepdims=True)
    logit_grad = logit_grad.astype(BF16)
    out.router[...] = tn(logit_grad, normed[...])
    query_grad = gated[...].astype(BF16)
    query_grad_t = gated[...].T.astype(BF16)
    for block in range(blocks):
        rows = slice(block * own, (block + 1) * own)
        out.w_query[block, 0:own, :] = nn(query_grad_t[rows], normed[...]).astype(BF16)
    out.normed_grad[...] = nn(query_grad, weights.w_query[...]) + nn(logit_grad, weights.w_router[...])


def layer_finish(x, normed, received, gain1, w_kv, middle_grad, normed_grad, keyval_out, small):
    total = received[0].astype(F32)
    for j in range(1, received.shape[0]):
        total = total + received[j].astype(F32)
    total = total.astype(BF16)
    keyval_out[...] = nn(total.astype(F32).T.astype(BF16), normed[...]).astype(BF16)
    grad = normed_grad[...] + nt(total, w_kv)
    hat, scale = norm_parts(x)
    back, gain1_grad, bias1_grad = norm_back(hat, scale, gain1, grad)
    small[0:1, :] = gain1_grad
    small[1:2, :] = bias1_grad
    return middle_grad[...] + back


def count_chosen(picked, keep, small):
    count, experts = picked.shape
    kept = jnp.broadcast_to(own_columns(keep, count).astype(F32), (LANES, count)).T[:, :experts]
    small[4:5, 0:experts] = jnp.sum(jnp.where(picked, kept, 0.0), axis=0, keepdims=True)


class Refs:
    def __init__(self, **refs):
        self.__dict__.update(refs)


def named(names, refs):
    return Refs(**dict(zip(names, refs[: len(names)]))), refs[len(names) :]


def weights_of(layer, refs):
    weights, refs = named(WEIGHTS, refs)
    for name in ("gain1", "bias1", "gain2", "bias2"):
        setattr(weights, name, getattr(weights, name).at[pl.ds(layer, 1), :])
    return weights, refs


WEIGHTS = ("gain1", "bias1", "w_kv", "w_router", "w_query", "w_out", "gain2", "bias2", "w_up", "w_down")
KEPT = ("keyval", "gates", "query", "lse", "attended", "gated", "middle")
SUMS = ("wide", "keys", "values", "gates")
OUT = ("up", "down", "w_out", "w_query", "router", "keyval", "small", "middle_grad", "normed_grad")
LATER = ("x", "normed", "received", "gain1", "w_kv", "middle_grad", "normed_grad", "small")


def pre_kernel(x, gain1, bias1, w_kv, normed, keyval_own):
    pre_layer(x[...].astype(F32), gain1[0:1, :], bias1[0:1, :], w_kv[...], normed, keyval_own)


def first_kernel(*refs):
    weights, refs = weights_of(0, refs)
    (x, normed, keyval, routes, lengths, keep, next_gain1, next_bias1, next_w_kv), refs = refs[:9], refs[9:]
    kept, refs = named(KEPT[1:], refs)
    kept.keyval = keyval
    (stream, next_normed, next_keyval, small), refs = refs[:4], refs[4:]
    mask, spread, dense, gated = refs
    fill_mask(lengths, keep, mask)
    spread_routes(routes, spread)
    result, picked = layer_forward(
        x[...].astype(F32), normed, weights, mask, spread, dense, gated, kept
    )
    small[...] = jnp.zeros(small.shape, F32)
    count_chosen(picked, keep, small)
    stream[...] = result
    pre_layer(result, next_gain1[1:2, :], next_bias1[1:2, :], next_w_kv[...], next_normed, next_keyval)


def turn_kernel(*refs):
    weights, refs = weights_of(1, refs)
    (x, normed, keyval, routes, lengths, keep, cotangent), refs = refs[:7], refs[7:]
    (activations,), refs = refs[:1], refs[1:]
    out, refs = named(OUT, refs)
    kept, refs = named(KEPT[1:], refs)
    kept.keyval = keyval
    sums, refs = named(SUMS, refs)
    mask, spread, dense, gated = refs
    fill_mask(lengths, keep, mask)
    spread_routes(routes, spread)
    result, picked = layer_forward(x[...], normed, weights, mask, spread, dense, gated, kept)
    activations[...] = result.astype(BF16)
    count = x.shape[0]
    kept_col = jnp.broadcast_to(own_columns(keep, count).astype(F32), (LANES, count)).T
    kept_col = jnp.concatenate([kept_col] * (x.shape[1] // LANES), axis=1)
    out.small[...] = jnp.zeros(out.small.shape, F32)
    count_chosen(picked, keep, out.small)
    stream_grad = cotangent[...].astype(F32) * kept_col
    layer_back(stream_grad, normed, weights, mask, spread, dense, gated, kept, sums, out)


def back_kernel(*refs):
    weights, refs = weights_of(0, refs)
    later, refs = named(LATER, refs)
    (normed, routes, lengths, keep, small), refs = refs[:5], refs[5:]
    kept, refs = named(KEPT, refs)
    (later_keyval, later_small), refs = refs[:2], refs[2:]
    out, refs = named(OUT, refs)
    sums, refs = named(SUMS, refs)
    mask, spread, dense, gated = refs
    later_small[...] = later.small[...]
    out.small[...] = small[...]
    stream_grad = layer_finish(
        later.x[...], later.normed, later.received, later.gain1[1:2, :], later.w_kv[...],
        later.middle_grad, later.normed_grad, later_keyval, later_small,
    )
    fill_mask(lengths, keep, mask)
    spread_routes(routes, spread)
    layer_back(stream_grad, normed, weights, mask, spread, dense, gated, kept, sums, out)


def end_kernel(x, normed, received, gain1, w_kv, middle_grad, normed_grad, small_in, keyval_out, small, grad):
    small[...] = small_in[...]
    grad[...] = layer_finish(
        x[...].astype(F32), normed, received, gain1[0:1, :], w_kv[...], middle_grad, normed_grad,
        keyval_out, small,
    )


def share_kernel(n, scatter, mine, everyones, send_sem, recv_sem):
    me = lax.axis_index("exp")
    rows = everyones.shape[1]
    barrier = pltpu.get_barrier_semaphore()
    others = [lax.rem(me + step, n) for step in range(1, n)]
    for other in others:
        pl.semaphore_signal(
            barrier, inc=1, device_id={"exp": other}, device_id_type=pl.DeviceIdType.MESH
        )

    def part(owner):
        return mine.at[pl.ds(pl.multiple_of(owner * rows, rows), rows)] if scatter else mine

    pl.semaphore_wait(barrier, n - 1)
    copies = []
    for step, other in enumerate(others):
        copy = pltpu.make_async_remote_copy(
            src_ref=part(other),
            dst_ref=everyones.at[me],
            send_sem=send_sem.at[step],
            recv_sem=recv_sem.at[step],
            device_id={"exp": other},
            device_id_type=pl.DeviceIdType.MESH,
        )
        copy.start()
        copies.append(copy)
    everyones[me] = part(me)[...]
    for copy in copies:
        copy.wait()


def vmem():
    return pl.BlockSpec(memory_space=pltpu.VMEM)


def axis_sizes():
    chips = lax.axis_size("dp") // 2
    across = math.isqrt(chips)
    across = across if across * across == chips else chips
    return {"c": 2, "x": across, "y": chips // across, "z": lax.axis_size("exp")}


def place_of():
    size = axis_sizes()
    d = lax.axis_index("dp")
    at = {"c": lax.rem(d, 2), "x": lax.rem(d // 2, size["x"]), "y": d // (2 * size["x"]), "z": lax.axis_index("exp")}
    return at, size


def peers_of(axis, at, size):
    out = []
    for step in range(1, size[axis]):
        where = dict(at)
        where[axis] = lax.rem(at[axis] + step, size[axis])
        out.append((where[axis], {"exp": where["z"], "dp": (where["y"] * size["x"] + where["x"]) * 2 + where["c"]}))
    return out


def greet(axes, at, size):
    barrier = pltpu.get_barrier_semaphore()
    total = 0
    for axis in axes:
        for _, device in peers_of(axis, at, size):
            pl.semaphore_signal(barrier, inc=1, device_id=device, device_id_type=pl.DeviceIdType.MESH)
            total += 1
    pl.semaphore_wait(barrier, total)


class Chunk:
    def __init__(self, array, first, rows, order, kind, result, layer, held_here):
        self.array, self.first, self.rows, self.order = array, first, rows, order
        self.kind, self.result, self.layer, self.held_here = kind, result, layer, held_here

    def shapes(self, blocks, width, size):
        own = (blocks, self.rows // size[self.order[0]], width)
        z, rows = blocks, self.rows
        got = []
        for axis in self.order:
            if axis == "z":
                z = 1
            else:
                rows = rows // size[axis]
            got.append((size[axis] - 1, z, rows, width))
        return ([] if self.held_here else [own]) + got


class Sums:
    def __init__(self, chunks, sources, results, scratch, sems):
        self.chunks, self.sources, self.results = chunks, sources, results
        self.down_send, self.down_recv, self.up_send, self.up_recv, self.own_sem = sems
        self.at, self.size = place_of()
        self.waiting = {}
        self.own, self.base, self.got = [], [], []
        scratch = list(scratch)
        for chunk in chunks:
            part = chunk.rows // self.size[chunk.order[0]]
            if chunk.held_here:
                self.own.append(sources[chunk.array])
                self.base.append(chunk.first + self.at[chunk.order[0]] * part)
            else:
                self.own.append(scratch.pop(0))
                self.base.append(0)
            self.got.append([scratch.pop(0) for _ in chunk.order])

    def region(self, i, stages):
        chunk = self.chunks[i]
        first, rows, z = 0, chunk.rows, None
        for k, axis in enumerate(chunk.order[:stages]):
            if axis == "z":
                z = self.at["z"]
            else:
                rows = rows // self.size[axis]
                if k > 0:
                    first = first + self.at[axis] * rows
        return z, first, rows

    def copy_to(self, source, target, send, recv, device):
        copy = pltpu.make_async_remote_copy(
            src_ref=source, dst_ref=target, send_sem=send, recv_sem=recv, device_id=device,
            device_id_type=pl.DeviceIdType.MESH,
        )
        copy.start()
        return copy

    def send_down(self, i, s):
        chunk, axis = self.chunks[i], self.chunks[i].order[s]
        copies = []
        z, first, rows = self.region(i, s)
        part = rows if axis == "z" else rows // self.size[axis]
        for step, (place, device) in enumerate(peers_of(axis, self.at, self.size)):
            if s == 0:
                start = chunk.first + place * part
                source = self.sources[chunk.array].at[:, pl.ds(pl.multiple_of(start, 16), part), :]
            elif axis == "z":
                start = self.base[i] + first
                source = self.own[i].at[pl.ds(place, 1), pl.ds(pl.multiple_of(start, 16), part), :]
            else:
                start = pl.multiple_of(self.base[i] + first + place * part, 16)
                blocks = slice(None) if z is None else pl.ds(z, 1)
                source = self.own[i].at[blocks, pl.ds(start, part), :]
            index = (i, s, step)
            copies.append(
                self.copy_to(source, self.got[i][s].at[step], self.down_send.at[index], self.down_recv.at[index], device)
            )
        if s == 0 and not chunk.held_here:
            start = pl.multiple_of(chunk.first + self.at[axis] * part, 16)
            load = pltpu.make_async_copy(
                self.sources[chunk.array].at[:, pl.ds(start, part), :], self.own[i], self.own_sem.at[i]
            )
            load.start()
            copies.append(load)
        self.waiting[i] = copies

    def add_up(self, i, s):
        chunk, axis = self.chunks[i], self.chunks[i].order[s]
        for copy in self.waiting[i]:
            copy.wait()
        z, first, rows = self.region(i, s + 1)
        blocks = self.got[i][s].shape[1]
        piece = math.gcd(rows, 64)
        own, got = self.own[i], self.got[i][s]

        def one(t, carry):
            block, row = t // (rows // piece), lax.rem(t, rows // piece) * piece
            where = pl.ds(pl.multiple_of(self.base[i] + first + row, 16), piece)
            arrived = pl.ds(pl.multiple_of(row, 16), piece)
            held = block if z is None else z
            total = own[held, where, :].astype(F32)
            for step in range(self.size[axis] - 1):
                total = total + got[step, block, arrived, :].astype(F32)
            own[held, where, :] = total.astype(BF16)
            return carry

        lax.fori_loop(0, blocks * (rows // piece), one, 0)

    def target(self, i, stages):
        chunk = self.chunks[i]
        z, first, rows = self.region(i, stages)
        start = chunk.first + self.at[chunk.order[0]] * (chunk.rows // self.size[chunk.order[0]]) + first
        where = pl.ds(pl.multiple_of(start, 16), rows)
        result = self.results[chunk.result].at[chunk.layer]
        if chunk.kind == "own":
            return result.at[where, :]
        if chunk.kind == "stack":
            return result.at[:, where, :] if z is None else result.at[z, where, :]
        width = self.own[i].shape[2]
        return result.at[where, :] if z is None else result.at[where, pl.ds(pl.multiple_of(z * width, width), width)]

    def send_up(self, i, s):
        chunk, axis = self.chunks[i], self.chunks[i].order[s]
        target = self.target(i, s + 1)
        copies = []
        source = target
        if s == len(chunk.order) - 1:
            z, first, rows = self.region(i, s + 1)
            where = pl.ds(pl.multiple_of(self.base[i] + first, 16), rows)
            source = self.own[i].at[z, where, :]
            keep = pltpu.make_async_copy(source, target, self.own_sem.at[i])
            keep.start()
            copies.append(keep)
        if axis != "z" or chunk.kind != "own":
            for step, (_, device) in enumerate(peers_of(axis, self.at, self.size)):
                index = (i, s, step)
                copies.append(self.copy_to(source, target, self.up_send.at[index], self.up_recv.at[index], device))
        self.waiting[i] = copies

    def stages(self, i):
        return 2 * len(self.chunks[i].order)

    def advance(self, i, stage):
        depth = len(self.chunks[i].order)
        if stage < depth:
            self.add_up(i, stage)
            if stage + 1 < depth:
                self.send_down(i, stage + 1)
            else:
                self.send_up(i, depth - 1)
        else:
            for copy in self.waiting[i]:
                copy.wait()
            if stage + 1 < 2 * depth:
                self.send_up(i, 2 * depth - 2 - stage)


class SmallSum:
    def __init__(self, array, result, got, send, recv):
        self.array, self.result, self.got, self.send, self.recv = array, result, got, send, recv
        self.at, self.size = place_of()

    def start(self, s):
        axis = "cxyz"[s]
        source = self.array if s == 0 else self.result
        self.copies = []
        for step, (_, device) in enumerate(peers_of(axis, self.at, self.size)):
            copy = pltpu.make_async_remote_copy(
                src_ref=source, dst_ref=self.got[s].at[self.at[axis]], send_sem=self.send.at[s, step],
                recv_sem=self.recv.at[s, step], device_id=device, device_id_type=pl.DeviceIdType.MESH,
            )
            copy.start()
            self.copies.append(copy)
        self.got[s][self.at[axis]] = source[...]

    def advance(self, s):
        for copy in self.copies:
            copy.wait()
        total = self.got[s][0]
        for j in range(1, self.size["cxyz"[s]]):
            total = total + self.got[s][j]
        self.result[...] = total
        if s < 3:
            self.start(s + 1)


def sum_scratch(chunks, shapes, size):
    scratch = []
    for chunk in chunks:
        blocks, _, width = shapes[chunk.array]
        scratch += [pltpu.VMEM(shape, BF16) for shape in chunk.shapes(blocks, width, size)]
    most = max(size.values()) - 1
    sems = pltpu.SemaphoreType.DMA((len(chunks), 4, most))
    return scratch, [sems] * 4 + [pltpu.SemaphoreType.DMA((len(chunks),))]


def small_scratch(shape, size):
    most = max(size.values()) - 1
    sems = pltpu.SemaphoreType.DMA((4, most))
    return [pltpu.VMEM((size[axis],) + shape, F32) for axis in "cxyz"] + [sems] * 2


def reduce_kernel(chunks, starts, counts, *refs):
    sources, refs = refs[: counts[0]], refs[counts[0] :]
    small_in, refs = refs[0], refs[1:]
    results, refs = refs[: counts[1]], refs[counts[1] :]
    small_out, refs = refs[0], refs[1:]
    scratch, sems, refs = refs[: counts[2]], refs[counts[2] : counts[2] + 5], refs[counts[2] + 5 :]
    small = SmallSum(small_in, small_out, refs[:4], refs[4], refs[5])
    sums = Sums(chunks, sources, results, scratch, sems)
    greet("cxyz", sums.at, sums.size)
    ahead = AHEAD
    for i, start in enumerate(starts):
        if start < ahead:
            sums.send_down(i, 0)
    small.start(0)
    for t in range(max(start + sums.stages(i) for i, start in enumerate(starts))):
        order = range(len(chunks))
        for i in (reversed(order) if NEWEST else order):
            if 0 <= t - starts[i] < sums.stages(i):
                sums.advance(i, t - starts[i])
        for i, start in enumerate(starts):
            if start == t + ahead:
                sums.send_down(i, 0)
        if t < 4:
            small.advance(t)


AHEAD = 2
NEWEST = False


def pieces(rows, unit):
    units = rows // unit
    if units < 2 or not HALVES:
        return [(0, rows)]
    return [(0, -(-units // 2) * unit), (-(-units // 2) * unit, units // 2 * unit)]


HALVES = False


def sum_plan(n, up_rows, down_rows, own_rows, dp, tail_rows):
    unit = 16 * dp
    chunks, starts = [], []

    def pad(rows):
        return -(-rows // unit) * unit

    def add(pair, rows_pair):
        cuts = [pieces(pad(rows), unit) for rows in rows_pair]
        for k in range(max(len(cut) for cut in cuts)):
            start = starts[-1] + 1 if starts else 0
            for (array, kind, result, layer, order), cut in zip(pair, cuts):
                if k < len(cut):
                    chunks.append(Chunk(array, cut[k][0], cut[k][1], order, kind, result, layer, False))
                    starts.append(start)

    add([(0, "wide", 0, 1, "cxyz"), (1, "stack", 1, 1, "cyxz")], (up_rows, down_rows))
    add([(4, "wide", 0, 0, "cxyz"), (5, "stack", 1, 0, "cyxz")], (up_rows, down_rows))
    add([(2, "own", 2, 1, "cxyz"), (3, "own", 3, 1, "cyxz")], (own_rows, own_rows))
    add([(6, "own", 2, 0, "cxyz"), (7, "own", 3, 0, "cyxz")], (own_rows, own_rows))
    chunks.append(Chunk(8, 0, tail_rows, "cxyz", "stack", 4, 0, False))
    starts.append(0)
    return chunks, starts


def reduce_all(arrays, chunks, starts, result_shapes, small, sizes, collective_id):
    scratch, sems = sum_scratch(chunks, [array.shape for array in arrays], sizes)
    counts = (len(arrays), len(result_shapes), len(scratch))
    anywhere = pl.BlockSpec(memory_space=pl.ANY)
    return pl.pallas_call(
        partial(reduce_kernel, chunks, starts, counts),
        out_shape=[jax.ShapeDtypeStruct(shape, BF16) for shape in result_shapes] + [jax.ShapeDtypeStruct(small.shape, F32)],
        in_specs=[anywhere] * len(arrays) + [vmem()],
        out_specs=[anywhere] * len(result_shapes) + [vmem()],
        scratch_shapes=scratch + sems + small_scratch(small.shape, sizes),
        compiler_params=pltpu.CompilerParams(
            collective_id=collective_id, has_side_effects=True, vmem_limit_bytes=VMEM_LIMIT
        ),
        name="sum_gradients",
    )(*arrays, small)


def gather_kernel(orders, *refs):
    count = len(orders)
    mine, results, sems = refs[:2], refs[2 : 2 + count], refs[2 + count :]
    mine = [mine[i % 2].at[i // 2] for i in range(count)]
    send_sem, recv_sem, own_sem = sems
    at, size = place_of()
    greet("cxyz", at, size)
    waiting = {}

    def region(i, s):
        first, rows = 0, mine[i].shape[0]
        for axis in reversed(orders[i][s:]):
            rows = rows // size[axis]
            first = first + at[axis] * rows
        return pl.ds(pl.multiple_of(first, rows), rows)

    def send(i, s):
        axis = orders[i][s]
        copies = []
        if s == 0:
            where = region(i, 1)
            own = pltpu.make_async_copy(mine[i], results[i].at[at["z"]], own_sem.at[i])
            own.start()
            copies.append(own)
        else:
            where = region(i, s)
        for step, (_, device) in enumerate(peers_of(axis, at, size)):
            for other in range(1 if s == 0 else size["z"] - 1):
                block = at["z"] if s == 0 else lax.rem(at["z"] + 1 + other, size["z"])
                source = mine[i].at[where, :] if s == 0 else results[i].at[block, where, :]
                copy = pltpu.make_async_remote_copy(
                    src_ref=source,
                    dst_ref=results[i].at[block, where, :],
                    send_sem=send_sem.at[i, s, step, other],
                    recv_sem=recv_sem.at[i, s, step, other],
                    device_id=device,
                    device_id_type=pl.DeviceIdType.MESH,
                )
                copy.start()
                copies.append(copy)
        waiting[i] = copies

    for t in range(count // 2 + max(len(order) for order in orders)):
        for i in range(count):
            stage = t - i // 2
            if 0 <= stage <= len(orders[i]):
                if stage > 0:
                    for copy in waiting[i]:
                        copy.wait()
                if stage < len(orders[i]):
                    send(i, stage)


def gather_all(arrays, sizes, collective_id):
    layers, rows, width = arrays[0].shape
    n = sizes["z"]
    orders = []
    for i in range(2 * layers):
        left, axes = rows // 16, ""
        for axis in "cxy" if i % 2 else "cyx":
            if left % sizes[axis] == 0:
                left, axes = left // sizes[axis], axis + axes
        orders.append("z" + axes)
    anywhere = pl.BlockSpec(memory_space=pl.ANY)
    most = max(sizes.values()) - 1
    sems = pltpu.SemaphoreType.DMA((len(orders), 4, most, n - 1))
    return pl.pallas_call(
        partial(gather_kernel, orders),
        out_shape=[jax.ShapeDtypeStruct((n, rows, width), BF16) for _ in orders],
        in_specs=[vmem()] * 2,
        out_specs=[vmem()] * len(orders),
        scratch_shapes=[sems, sems, pltpu.SemaphoreType.DMA((len(orders),))],
        compiler_params=pltpu.CompilerParams(collective_id=collective_id, has_side_effects=True),
        name="gather_experts",
    )(*arrays)


def layer_spec(array, layer):
    block = (None,) + array.shape[1:]
    return pl.BlockSpec(block, lambda *_: (layer,) + (0,) * (array.ndim - 1), pipeline_mode=pl.Buffered(1))


def share(mine, n, scatter, collective_id, name):
    rows = mine.shape[0] // n if scatter else mine.shape[0]
    return pl.pallas_call(
        partial(share_kernel, n, scatter),
        out_shape=jax.ShapeDtypeStruct((n, rows, mine.shape[1]), mine.dtype),
        in_specs=[vmem()],
        out_specs=vmem(),
        scratch_shapes=[pltpu.SemaphoreType.DMA((n - 1,)), pltpu.SemaphoreType.DMA((n - 1,))],
        compiler_params=pltpu.CompilerParams(collective_id=collective_id, has_side_effects=True),
        name=name,
    )(mine)


def call(kernel, args, outs, scratch, name):
    specs, arrays = [], []
    for array, layer in args:
        arrays.append(array)
        if layer == "smem":
            specs.append(pl.BlockSpec(memory_space=pltpu.SMEM))
        elif layer is None:
            specs.append(pl.BlockSpec(array.shape, lambda *_, nd=array.ndim: (0,) * nd, pipeline_mode=pl.Buffered(1)))
        else:
            specs.append(layer_spec(array, layer))
    return pl.pallas_call(
        kernel,
        out_shape=[jax.ShapeDtypeStruct(shape, dtype) for shape, dtype in outs],
        grid=(1,),
        in_specs=specs,
        out_specs=[pl.BlockSpec(shape, lambda *_, nd=len(shape): (0,) * nd, pipeline_mode=pl.Buffered(1)) for shape, _ in outs],
        scratch_shapes=[pltpu.VMEM(shape, dtype) for shape, dtype in scratch],
        compiler_params=pltpu.CompilerParams(vmem_limit_bytes=VMEM_LIMIT),
        name=name,
    )(*arrays)


def body(
    tokens, cotangent, routes, keep, lengths, norm1_gain, norm1_bias, w_kv, w_router, w_query, w_out,
    norm2_gain, norm2_bias, w_up, w_down,
):
    n = lax.axis_size("exp")
    dp = lax.axis_size("dp")
    layers, width, pair = w_kv.shape
    count = tokens.shape[1]
    group = routes.shape[2]
    topk = routes.shape[3]
    experts = w_router.shape[2]
    head = w_query.shape[3]
    local = w_query.shape[1]
    hidden = w_up.shape[2]
    flat = experts * head
    own = local * head
    x0 = tokens[0]
    routes_t = jnp.swapaxes(routes[:, 0], 1, 2)
    router_t = jnp.swapaxes(w_router, 1, 2)
    gain1, bias1, gain2, bias2 = norm1_gain, norm1_bias, norm2_gain, norm2_bias
    queries_t = jnp.swapaxes(w_query, 2, 3).reshape(layers, own, width)
    outs = w_out.reshape(layers, own, width)
    sizes = axis_sizes()
    gathered = [array.reshape(flat, width) for array in gather_all((queries_t, outs), sizes, 2)]
    wq, wo = gathered[0::2], gathered[1::2]

    def rows_of(least):
        return -(-least // (16 * dp)) * 16 * dp

    def weights(l):
        return [(gain1, None), (bias1, None), (w_kv, l), (router_t, l), (wq[l], None), (wo[l], None), (gain2, None), (bias2, None), (w_up, l), (w_down, l)]

    kept_shapes = [
        ((count, experts), F32), ((topk, count, LANES), BF16), ((topk, 8, count), F32),
        ((topk, count, LANES), BF16), ((count, flat), BF16), ((count, width), F32),
    ]
    work = [((group, count), F32), ((topk, count, LANES), jnp.int32), ((count, flat), F32), ((count, flat), F32)]
    sum_shapes = [((count, width), F32), ((group, pair), F32), ((group, pair), F32), ((count, experts), F32)]
    out_shapes = [
        ((n, rows_of(width), hidden // n), BF16), ((n, rows_of(hidden // n), width), BF16),
        ((n, rows_of(own), width), BF16), ((n, rows_of(own), width), BF16),
        ((experts, width), F32), ((group, pair), BF16), ((8, width), F32), ((count, width), F32), ((count, width), F32),
    ]
    normed0, keyval0 = call(
        pre_kernel, [(x0, None), (gain1, None), (bias1, None), (w_kv, 0)],
        [((count, width), BF16), ((count, pair), BF16)], [], "pre",
    )
    keyval0 = share(keyval0, n, False, 0, "gather_keyval").reshape(group, pair)
    *kept0, x1, normed1, keyval1, small0 = call(
        first_kernel,
        weights(0) + [(x0, None), (normed0, None), (keyval0, None), (routes_t, 0), (lengths, "smem"), (keep, None), (gain1, None), (bias1, None), (w_kv, 1)],
        kept_shapes + [((count, width), F32), ((count, width), BF16), ((count, pair), BF16), ((8, width), F32)],
        work, "first_block",
    )
    keyval1 = share(keyval1, n, False, 0, "gather_keyval").reshape(group, pair)
    activations, up1, down1, out1, query1, router1, part1, small1, mid1, ngrad1 = call(
        turn_kernel,
        weights(1) + [(x1, None), (normed1, None), (keyval1, None), (routes_t, 1), (lengths, "smem"), (keep, None), (cotangent[0], None)],
        [((count, width), BF16)] + out_shapes, kept_shapes + sum_shapes + work, "second_block",
    )
    received1 = share(part1, n, True, 1, "scatter_keyval")
    kv1, small1, up0, down0, out0, query0, router0, part0, small0, mid0, ngrad0 = call(
        back_kernel,
        weights(0) + [(x1, None), (normed1, None), (received1, None), (gain1, None), (w_kv, 1), (mid1, None), (ngrad1, None), (small1, None),
         (normed0, None), (routes_t, 0), (lengths, "smem"), (keep, None), (small0, None), (keyval0, None)] + [(v, None) for v in kept0],
        [((pair, width), BF16), ((8, width), F32)] + out_shapes, sum_shapes + work, "first_block_back",
    )
    received0 = share(part0, n, True, 1, "scatter_keyval")
    kv0, small0, input_grad = call(
        end_kernel,
        [(x0, None), (normed0, None), (received0, None), (gain1, None), (w_kv, 0), (mid0, None), (ngrad0, None), (small0, None)],
        [((pair, width), BF16), ((8, width), F32), ((count, width), F32)], [], "end",
    )
    kv_rows = experts + pair
    tail = jnp.concatenate([kv0, router0.astype(BF16), kv1, router1.astype(BF16)])
    tail_rows = rows_of(-(-tail.shape[0] // n))
    tail = jnp.pad(tail, ((0, n * tail_rows - tail.shape[0]), (0, 0))).reshape(n, tail_rows, width)
    chunks, starts = sum_plan(n, width, hidden // n, own, dp, tail_rows)
    arrays = [up1, down1, query1, out1, up0, down0, query0, out0, tail]
    up, down, expert_query, expert_out, tail, small = reduce_all(
        arrays, chunks, starts,
        [(layers,) + up1.shape[1:2] + (hidden,), (layers,) + down1.shape, (layers,) + query1.shape[1:], (layers,) + out1.shape[1:], (1,) + tail.shape],
        jnp.concatenate([small0, small1]), sizes, 3,
    )
    down = down[:, :, : hidden // n].reshape(layers, hidden, width).astype(F32)
    tail = tail.reshape(n * tail_rows, width)[: layers * kv_rows].reshape(layers, kv_rows, width).astype(F32)
    kv = jnp.swapaxes(tail[:, :pair], 1, 2)
    router = jnp.swapaxes(tail[:, pair:], 1, 2)
    norms = small.reshape(layers, -1, width)
    expert_query = jnp.swapaxes(expert_query[:, :own].reshape(layers, local, head, width), 2, 3).astype(F32)
    expert_out = expert_out[:, :own].reshape(layers, local, head, width).astype(F32)
    return (
        activations[None], input_grad[None], norms[:, 0], norms[:, 1], kv, router, expert_query, expert_out,
        norms[:, 2], norms[:, 3], up[:, :width].astype(F32), down, norms[:, 4, :experts],
    )


def solution(mesh):
    return jax.shard_map(
        body,
        mesh=mesh,
        in_specs=(
            P("dp", "exp", None), P("dp", "exp", None), P(None, "dp", None, None), P("dp", None), P("dp", None),
            P(), P(), P(), P(), P(None, "exp", None, None), P(None, "exp", None, None), P(), P(), P(), P(),
        ),
        out_specs=(
            P("dp", "exp", None), P("dp", "exp", None), P(), P(), P(), P(),
            P(None, "exp", None, None), P(None, "exp", None, None), P(), P(), P(), P(), P(),
        ),
        check_vma=False,
    )
```

time: 1270 us -> 320 us (0.25); the launches traced: 1250 us -> 319 us
  waiting for transfers between devices: 611 us -> 0 us
  Pallas kernels: 0 us -> 296 us
  matrix products: 237 us -> 0 us
  blocking collectives: 168 us -> 0 us
  local copies, waits for them, and re-layouts: 92.8 us -> 6.78 us
  other arithmetic: 85.1 us -> 16 us
  starting transfers between devices: 41 us -> 0 us
  between operations: 15.8 us -> 0.77 us
    all_to_all x8 -> x0, waiting for transfers between devices: 333 us -> none  [the longest x2 132 us: body(): lax.all_to_all(outputs, 'exp', split_axis=0, concat_axis=0, tiled=True)]
    pallas_call x0 -> x11, Pallas kernels: none -> 296 us  [the longest x1 128 us: reduce_all(): pl.pallas_call(partial(reduce_kernel, chunks, starts, counts), out_shape=...]
    psum x2 -> x0, waiting for transfers between devices: 273 us -> none  [the longest x1 232 us: body(): lax.psum((stacked[0], stacked[1], stacked[2], stacked[3], stacked[6], sta...]
    dot_general x130 -> x0, matrix products: 237 us -> none  [the longest x24 54.8 us: block_scores(): jnp.einsum('rh,kh->rk', block_rows, keys, preferred_element_type=jnp.floa...]
    all_gather x2 -> x0, blocking collectives: 126 us -> none  [body(): keyval = lax.all_gather(keyval_own, 'exp', axis=0, tiled=True)]
    reduce_sum x66 -> x0, other arithmetic: 42.1 us -> none  [the longest x12 16.9 us: one_block(): total = jnp.sum(spread, axis=1, keepdims=True)]
    psum x1 -> x0, blocking collectives: 41.5 us -> none  [body(): lax.psum((stacked[0], stacked[1], stacked[2], stacked[3], stacked[6], sta...]
    all_to_all x8 -> x0, starting transfers between devices: 40.4 us -> none  [the longest x2 11.1 us: body(): lax.all_to_all(outgoing.reshape(exp_count, local_experts, capacity, width...]
  transfers between devices with their start and end apart: 12 -> 0, of which waited for: 9 -> 0; matrix products, arithmetic and copies ran while one was open for 8% -> 0% of each run, Pallas kernels for 0% -> 0%
where the time goes in v1:
time: 320 us; the launch traced here: 319 us
  Pallas kernels  296 us (92%)
  other arithmetic  16 us (5%)
  local copies, waits for them, and re-layouts  6.78 us (2%)
    pallas_call x1, Pallas kernels, reduce_all(): pl.pallas_call(partial(reduce_kernel, chunks, starts, counts), out_shape=...  128 us
    pallas_call x5, Pallas kernels, call(): pl.pallas_call(kernel, out_shape=[jax.ShapeDtypeStruct(shape, dtype) for...  82.1 us
    pallas_call x4, Pallas kernels, share(): pl.pallas_call(partial(share_kernel, n, scatter), out_shape=jax.ShapeDtyp...  44.5 us
    pallas_call x1, Pallas kernels, gather_all(): pl.pallas_call(partial(gather_kernel, orders), out_shape=[jax.ShapeDtypeS...  41.2 us

profile of v1, /device:TPU:0, one launch (start us, length us, event | category | flops | bytes accessed | tf_op | source)
XLA Modules:
  0.0 319.5 jit_solution(374180656622741702)
XLA Ops:
  0.6 2.1 pre.1
  2.7 11.8 %gather_keyval.2 = bf16[4,256,128]{2,1,0:T(8,128)(2,1)} custom-call(bf16[256,128]{1,0:T(8,128)(2,1)} %get-tuple-element.64.mine), custom_call_target="tpu_custom_call" | custom-call | tf_op jit(solution)/shard_map/gather_keyval/pallas_call | solution.py:804
  14.5 41.2 %gather_experts.1 = (bf16[4,384,512]{2,1,0:T(8,128)(2,1)}, bf16[4,384,512]{2,1,0:T(8,128)(2,1)}, bf16[4,384,512]{2,1,0:T(8,128)(2,1)}, bf16[4,384,512]{2,1,0:T(8,128)(2,1)}) custom-call(bf16[2,384,512]{2,1,0:T(8,128)(2,1)} %bitcast.61, bf16[2,384,512]{2,1,0:T(8,128)(2,1)} %bitcast.62), custom_call_target="tpu_custom_call" | custom-call | tf_op jit(solution)/shard_map/gather_experts/pallas_call | solution.py:786
  55.7 16.9 %first_block.1 = (f32[256,24]{1,0:T(8,128)}, bf16[8,256,128]{2,1,0:T(8,128)(2,1)}, f32[8,8,256]{2,1,0:T(8,128)}, bf16[8,256,128]{2,1,0:T(8,128)(2,1)}, bf16[256,...) custom-call(f32[2,512]{1,0:T(2,128)} %gain1.3, ...), custom_call_target="tpu_custom_call" | custom-call | tf_op jit(solution)/shard_map/first_block/pallas_call | solution.py:825
  72.6 12.7 %gather_keyval.3 = bf16[4,256,128]{2,1,0:T(8,128)(2,1)} custom-call(bf16[256,128]{1,0:T(8,128)(2,1)} %get-tuple-element.67.mine), custom_call_target="tpu_custom_call" | custom-call | tf_op jit(solution)/shard_map/gather_keyval/pallas_call | solution.py:804
  85.3 35.1 %second_block.1 = (bf16[256,512]{1,0:T(8,128)(2,1)}, bf16[4,512,512]{2,1,0:T(8,128)(2,1)}, bf16[4,512,512]{2,1,0:T(8,128)(2,1)}, bf16[4,384,512]{2,1,0:T(8,128)(...) custom-call(f32[2,512]{1,0:T(2,128)} %gain1.3, ...), custom_call_target="tpu_custom_call" | custom-call | tf_op jit(solution)/shard_map/second_block/pallas_call | solution.py:825
  120.4 0.8 convert_element_type.39
  121.2 10.8 %scatter_keyval.2.refs_12_ = bf16[4,256,128]{2,1,0:T(8,128)(2,1)} custom-call(bf16[1024,128]{1,0:T(8,128)(2,1)} %get-tuple-element.69.mine), custom_call_target="tpu_custom_call" | custom-call | tf_op jit(solution)/shard_map/scatter_keyval/pallas_call | solution.py:804
  132.0 25.3 %first_block_back.1 = (bf16[128,512]{1,0:T(8,128)(2,1)}, f32[8,512]{1,0:T(8,128)}, bf16[4,512,512]{2,1,0:T(8,128)(2,1)}, bf16[4,512,512]{2,1,0:T(8,128)(2,1)}, b...) custom-call(f32[2,512]{1,0:T(2,128)} %gain1.3, ...), custom_call_target="tpu_custom_call" | custom-call | tf_op jit(solution)/shard_map/first_block_back/pallas_call | solution.py:825
  157.3 0.0 copy-start.6
  157.3 0.0 copy-start.5
  157.3 0.0 copy-start.4
  157.4 9.2 %scatter_keyval.3.received = bf16[4,256,128]{2,1,0:T(8,128)(2,1)} custom-call(bf16[1024,128]{1,0:T(8,128)(2,1)} %get-tuple-element.80.mine), custom_call_target="tpu_custom_call" | custom-call | tf_op jit(solution)/shard_map/scatter_keyval/pallas_call | solution.py:804
  166.6 2.8 end.1
  169.4 0.0 copy-done.6
  169.4 1.3 pad_maximum_fusion.refs_9_
  170.7 0.0 copy-done.5
  170.8 0.0 copy-done.4
  170.8 1.7 fusion.6
  172.5 128.1 %sum_gradients.1 = (bf16[2,512,2048]{2,1,0:T(8,128)(2,1)}, bf16[2,4,512,512]{3,2,1,0:T(8,128)(2,1)}, bf16[2,384,512]{2,1,0:T(8,128)(2,1)}, bf16[2,384,512]{2,1,0...) custom-call(bf16[4,512,512]{2,1,0:T(8,128)(2,1)} %get-tuple-element.85.refs_0_, ...), custom_call_target="tpu_custom_call" | custom-call | tf_op jit(solution)/shard_map/sum_gradients/pallas_call | solution.py:707
  300.6 0.0 copy-start.3
  300.6 1.1 slice.34
  301.7 1.3 slice.39
  302.9 0.9 fusion.7
  303.9 0.6 copy_bitcast_fusion
  304.5 0.6 copy_bitcast_fusion.2
  305.1 0.1 convert.5
  305.1 0.7 slice_bitcast_fusion.1
  305.8 0.0 copy-start.2
  305.8 1.0 copy.33
  306.8 0.0 copy-done.3
  306.8 0.0 copy-start.1
  306.8 1.4 convert_bitcast_fusion
  308.2 0.0 copy-done.2
  308.2 1.4 convert.7
  309.5 0.6 copy-done.1
  310.2 0.0 copy-start
  310.2 4.4 %convert_element_type.47 = f32[2,512,2048]{2,1,0:T(8,128)} convert(bf16[2,512,2048]{2,1,0:T(8,128)(2,1)S(1)} %copy-done.1) | non-fusion elementwise | flops 2097152 | bytes 12582912 | tf_op jit(solution)/shard_map/convert_element_type | solution.py:930
  314.6 0.0 copy-done
  314.6 4.9 %bitcast_convert_fusion = f32[2,2048,512]{2,1,0:T(8,128)} fusion(bf16[2,4,512,512]{3,2,1,0:T(8,128)(2,1)S(1)} %copy-done), kind=kLoop, calls=%fused_computation | loop fusion | flops 2097152 | bytes 12582912 | tf_op jit(solution)/shard_map/convert_element_type | solution.py:921
  (2 shorter events, 0.0 us)
Async XLA Ops:
  157.3 12.1 %copy-start.6 = (f32[8,512]{1,0:T(8,128)S(1)}, f32[8,512]{1,0:T(8,128)}, u32[]{:S(2)}) copy-start(f32[8,512]{1,0:T(8,128)} %get-tuple-element.98) | copy-start | bytes 49156
  157.3 13.4 %copy-start.5 = (f32[24,512]{1,0:T(8,128)S(1)}, f32[24,512]{1,0:T(8,128)}, u32[]{:S(2)}) copy-start(f32[24,512]{1,0:T(8,128)} %get-tuple-element.94) | copy-start | bytes 147460
  157.3 13.4 %copy-start.4 = (bf16[128,512]{1,0:T(8,128)(2,1)S(1)}, bf16[128,512]{1,0:T(8,128)(2,1)}, u32[]{:S(2)}) copy-start(bf16[128,512]{1,0:T(8,128)(2,1)} %get-tuple-element.95) | copy-start | bytes 393220
  300.6 6.2 %copy-start.3 = (bf16[2,384,512]{2,1,0:T(8,128)(2,1)S(1)}, bf16[2,384,512]{2,1,0:T(8,128)(2,1)}, u32[]{:S(2)}) copy-start(bf16[2,384,512]{2,1,0:T(8,128)(2,1)} %get-tuple-element.101) | copy-start | bytes 2359300
  305.8 2.4 copy-start.2
  306.8 3.3 %copy-start.1 = (bf16[2,512,2048]{2,1,0:T(8,128)(2,1)S(1)}, bf16[2,512,2048]{2,1,0:T(8,128)(2,1)}, u32[]{:S(2)}) copy-start(bf16[2,512,2048]{2,1,0:T(8,128)(2,1)} %get-tuple-element.103) | copy-start | bytes 12582916
  310.2 4.5 %copy-start = (bf16[2,4,512,512]{3,2,1,0:T(8,128)(2,1)S(1)}, bf16[2,4,512,512]{3,2,1,0:T(8,128)(2,1)}, u32[]{:S(2)}) copy-start(bf16[2,4,512,512]{3,2,1,0:T(8,128)(2,1)} %get-tuple-element.104) | copy-start | bytes 12582916

commit v2 on v1

--- a/solution.py
+++ b/solution.py
@@ -171,7 +171,8 @@
     return middle + nn(active, weights.w_down[...]), picked
 
 
-def layer_back(stream_grad, normed, weights, mask, spread, dense, gated, kept, sums, out):
+def layer_back(stream_grad, normed, weights, mask, spread, dense, gated, kept, sums, out, between=None):
+    between = between or (lambda *place: None)
     count, width = normed.shape
     hidden = weights.w_up.shape[1]
     branch = stream_grad.astype(BF16)
@@ -194,6 +195,7 @@
         return carry
 
     lax.fori_loop(0, blocks, part, 0)
+    between("hidden")
     back, gain2_grad, bias2_grad = norm_back(hat2, scale2, weights.gain2[...], sums.wide[...])
     out.small[2:3, :] = gain2_grad
     out.small[3:4, :] = bias2_grad
@@ -232,6 +234,7 @@
         sums.keys[...] += nn(score_grad, query)
         query_grad = nn(keys_t, score_grad).T * 0.125
         place_tiles(gated, chosen, query_grad.astype(BF16).astype(F32))
+        between("slot", k)
         return carry
 
     lax.fori_loop(0, kept.query.shape[0], slot, 0)
@@ -239,6 +242,7 @@
     both_values = sums.values[...] + pltpu.roll(sums.values[...], LANES // 2, 1)
     first = iota(both_keys.shape, 1) < LANES // 2
     out.keyval[...] = jnp.where(first, both_keys, both_values).astype(BF16)
+    between("keyval")
     weighted = sums.gates[...]
     logit_grad = weighted - kept.gates[...] * jnp.sum(weighted, axis=1, keepdims=True)
     logit_grad = logit_grad.astype(BF16)
@@ -251,11 +255,14 @@
     out.normed_grad[...] = nn(query_grad, weights.w_query[...]) + nn(logit_grad, weights.w_router[...])
 
 
-def layer_finish(x, normed, received, gain1, w_kv, middle_grad, normed_grad, keyval_out, small):
+def add_received(received):
     total = received[0].astype(F32)
     for j in range(1, received.shape[0]):
         total = total + received[j].astype(F32)
-    total = total.astype(BF16)
+    return total.astype(BF16)
+
+
+def layer_finish(x, normed, total, gain1, w_kv, middle_grad, normed_grad, keyval_out, small):
     keyval_out[...] = nn(total.astype(F32).T.astype(BF16), normed[...]).astype(BF16)
     grad = normed_grad[...] + nt(total, w_kv)
     hat, scale = norm_parts(x)
@@ -350,7 +357,7 @@
     later_small[...] = later.small[...]
     out.small[...] = small[...]
     stream_grad = layer_finish(
-        later.x[...], later.normed, later.received, later.gain1[1:2, :], later.w_kv[...],
+        later.x[...], later.normed, add_received(later.received), later.gain1[1:2, :], later.w_kv[...],
         later.middle_grad, later.normed_grad, later_keyval, later_small,
     )
     fill_mask(lengths, keep, mask)
@@ -361,7 +368,7 @@
 def end_kernel(x, normed, received, gain1, w_kv, middle_grad, normed_grad, small_in, keyval_out, small, grad):
     small[...] = small_in[...]
     grad[...] = layer_finish(
-        x[...].astype(F32), normed, received, gain1[0:1, :], w_kv[...], middle_grad, normed_grad,
+        x[...].astype(F32), normed, add_received(received), gain1[0:1, :], w_kv[...], middle_grad, normed_grad,
         keyval_out, small,
     )
 
@@ -457,7 +464,6 @@
         self.chunks, self.sources, self.results = chunks, sources, results
         self.down_send, self.down_recv, self.up_send, self.up_recv, self.own_sem = sems
         self.at, self.size = place_of()
-        self.waiting = {}
         self.own, self.base, self.got = [], [], []
         scratch = list(scratch)
         for chunk in chunks:
@@ -487,10 +493,13 @@
             src_ref=source, dst_ref=target, send_sem=send, recv_sem=recv, device_id=device,
             device_id_type=pl.DeviceIdType.MESH,
         )
-        copy.start()
         return copy
 
     def send_down(self, i, s):
+        for copy in self.down_copies(i, s):
+            copy.start()
+
+    def down_copies(self, i, s):
         chunk, axis = self.chunks[i], self.chunks[i].order[s]
         copies = []
         z, first, rows = self.region(i, s)
@@ -515,13 +524,12 @@
             load = pltpu.make_async_copy(
                 self.sources[chunk.array].at[:, pl.ds(start, part), :], self.own[i], self.own_sem.at[i]
             )
-            load.start()
             copies.append(load)
-        self.waiting[i] = copies
+        return copies
 
     def add_up(self, i, s):
         chunk, axis = self.chunks[i], self.chunks[i].order[s]
-        for copy in self.waiting[i]:
+        for copy in self.down_copies(i, s):
             copy.wait()
         z, first, rows = self.region(i, s + 1)
         blocks = self.got[i][s].shape[1]
@@ -555,6 +563,10 @@
         return result.at[where, :] if z is None else result.at[where, pl.ds(pl.multiple_of(z * width, width), width)]
 
     def send_up(self, i, s):
+        for copy in self.up_copies(i, s):
+            copy.start()
+
+    def up_copies(self, i, s):
         chunk, axis = self.chunks[i], self.chunks[i].order[s]
         target = self.target(i, s + 1)
         copies = []
@@ -563,14 +575,12 @@
             z, first, rows = self.region(i, s + 1)
             where = pl.ds(pl.multiple_of(self.base[i] + first, 16), rows)
             source = self.own[i].at[z, where, :]
-            keep = pltpu.make_async_copy(source, target, self.own_sem.at[i])
-            keep.start()
-            copies.append(keep)
+            copies.append(pltpu.make_async_copy(source, target, self.own_sem.at[i]))
         if axis != "z" or chunk.kind != "own":
             for step, (_, device) in enumerate(peers_of(axis, self.at, self.size)):
                 index = (i, s, step)
                 copies.append(self.copy_to(source, target, self.up_send.at[index], self.up_recv.at[index], device))
-        self.waiting[i] = copies
+        return copies
 
     def stages(self, i):
         return 2 * len(self.chunks[i].order)
@@ -584,7 +594,7 @@
             else:
                 self.send_up(i, depth - 1)
         else:
-            for copy in self.waiting[i]:
+            for copy in self.up_copies(i, 2 * depth - 1 - stage):
                 copy.wait()
             if stage + 1 < 2 * depth:
                 self.send_up(i, 2 * depth - 2 - stage)
@@ -812,7 +822,174 @@
     )(mine)
 
 
-def call(kernel, args, outs, scratch, name):
+class KeyvalSum:
+    def __init__(self, mine, got, send, recv):
+        self.mine, self.got, self.send, self.recv = mine, got, send, recv
+        self.at, self.size = place_of()
+
+    def part(self, place):
+        rows = self.got.shape[1]
+        return self.mine.at[pl.ds(pl.multiple_of(place * rows, rows), rows), :]
+
+    def start(self):
+        self.copies = []
+        for step, (place, device) in enumerate(peers_of("z", self.at, self.size)):
+            copy = pltpu.make_async_remote_copy(
+                src_ref=self.part(place), dst_ref=self.got.at[step], send_sem=self.send.at[step],
+                recv_sem=self.recv.at[step], device_id=device, device_id_type=pl.DeviceIdType.MESH,
+            )
+            copy.start()
+            self.copies.append(copy)
+
+    def total(self):
+        for copy in self.copies:
+            copy.wait()
+        total = self.part(self.at["z"])[...].astype(F32)
+        for step in range(self.got.shape[0]):
+            total = total + self.got[step].astype(F32)
+        return total.astype(BF16)
+
+
+def finish_chunks(n, up_rows, down_rows, own_rows, tail_rows):
+    groups = [
+        [Chunk(0, 0, up_rows, "cxyz", "wide", 0, 1, False), Chunk(1, 0, down_rows, "cyxz", "stack", 1, 1, False)],
+        [Chunk(2, 0, own_rows, "cxyz", "own", 2, 1, False), Chunk(3, 0, own_rows, "cyxz", "own", 3, 1, False)],
+        [Chunk(4, 0, up_rows, "cxyz", "wide", 0, 0, True), Chunk(5, 0, down_rows, "cyxz", "stack", 1, 0, True)],
+        [Chunk(6, 0, own_rows, "cxyz", "own", 2, 0, True), Chunk(7, 0, own_rows, "cyxz", "own", 3, 0, True)],
+        [Chunk(8, 0, tail_rows, "cxyz", "stack", 4, 0, True)],
+    ]
+    chunks, numbers = [], []
+    for group in groups:
+        numbers.append(list(range(len(chunks), len(chunks) + len(group))))
+        chunks += group
+    return chunks, numbers
+
+
+def finish_kernel(chunks, groups, counts, *refs):
+    weights, refs = weights_of(0, refs)
+    later, refs = named(LATER[:2] + ("part",) + LATER[3:] + ("router",), refs)
+    (x, normed, routes, lengths, keep, small), refs = refs[:6], refs[6:]
+    kept, refs = named(KEPT, refs)
+    last_grads, refs = refs[:4], refs[4:]
+    input_grad, refs = refs[0], refs[1:]
+    results, refs = refs[:5], refs[5:]
+    small_out, refs = refs[0], refs[1:]
+    out, refs = named(OUT, refs)
+    sums, refs = named(SUMS, refs)
+    (mask, spread, dense, gated), refs = refs[:4], refs[4:]
+    (tail, small_in, got1, got0), refs = refs[:4], refs[4:]
+    scratch, refs = refs[:counts], refs[counts:]
+    small_got, refs = refs[:4], refs[4:]
+    sems, small_sems, (send1, recv1, send0, recv0) = refs[:5], refs[5:7], refs[7:]
+    sources = list(last_grads) + [out.up, out.down, out.w_query, out.w_out, tail]
+    total = Sums(chunks, sources, results, scratch, sems)
+    little = SmallSum(small_in, small_out, small_got, *small_sems)
+    keyval1 = KeyvalSum(later.part, got1, send1, recv1)
+    keyval0 = KeyvalSum(out.keyval, got0, send0, recv0)
+    done = [0] * len(groups)
+
+    def begin(group):
+        for i in groups[group]:
+            total.send_down(i, 0)
+
+    def advance(group):
+        if done[group] < total.stages(groups[group][0]):
+            for i in groups[group]:
+                total.advance(i, done[group])
+            done[group] += 1
+
+    greet("cxyz", total.at, total.size)
+    keyval1.start()
+    begin(0)
+    begin(1)
+    fill_mask(lengths, keep, mask)
+    spread_routes(routes, spread)
+    tail[...] = jnp.zeros(tail.shape, BF16)
+    rows = small.shape[0]
+    experts = weights.w_router.shape[0]
+    small_in[0:rows, :] = small[...]
+    small_in[rows : 2 * rows, :] = later.small[...]
+    small0, small1 = small_in.at[0:rows, :], small_in.at[rows : 2 * rows, :]
+    out.small = small0
+    tail[3, 0:experts, :] = later.router[...].astype(BF16)
+    advance(0)
+    stream_grad = layer_finish(
+        later.x[...], later.normed, keyval1.total(), later.gain1[1:2, :], later.w_kv[...],
+        later.middle_grad, later.normed_grad, tail.at[2, 0 : later.w_kv.shape[1]], small1,
+    )
+
+    def between(place, k=None):
+        if place == "hidden":
+            begin(2)
+            advance(0)
+            advance(1)
+        elif place == "slot":
+
+            @pl.when(k == 2)
+            def _():
+                advance(0)
+
+            @pl.when(k == 5)
+            def _():
+                advance(1)
+                advance(2)
+
+        elif place == "keyval":
+            keyval0.start()
+            advance(0)
+
+    layer_back(stream_grad, normed, weights, mask, spread, dense, gated, kept, sums, out, between)
+    tail[1, 0:experts, :] = out.router[...].astype(BF16)
+    begin(3)
+    advance(1)
+    input_grad[...] = layer_finish(
+        x[...].astype(F32), normed, keyval0.total(), weights.gain1[...], weights.w_kv[...],
+        out.middle_grad, out.normed_grad, tail.at[0, 0 : weights.w_kv.shape[1]], small0,
+    )
+    begin(4)
+    little.start(0)
+    for step in range(2 * len(chunks[-1].order)):
+        for group in range(len(groups)):
+            advance(group)
+        if step < 4:
+            little.advance(step)
+
+
+def finish_all(args, last_grads, out_shapes, work, result_shapes, sizes):
+    specs, arrays = specs_of(args)
+    n, up_rows, _ = last_grads[0].shape
+    tail_shape = result_shapes[4][1:]
+    chunks, groups = finish_chunks(n, up_rows, last_grads[1].shape[1], last_grads[2].shape[1], tail_shape[1])
+    shapes = [array.shape for array in last_grads] * 2 + [tail_shape]
+    scratch, sems = sum_scratch(chunks, shapes, sizes)
+    count, width = out_shapes[-1][0]
+    small_shape = (2 * out_shapes[6][0][0], width)
+    group, pair = out_shapes[5][0]
+    got = pltpu.VMEM((n - 1, group // n, pair), BF16)
+    anywhere = pl.BlockSpec(memory_space=pl.ANY)
+    return pl.pallas_call(
+        partial(finish_kernel, chunks, groups, len(scratch)),
+        out_shape=[jax.ShapeDtypeStruct((count, width), F32)]
+        + [jax.ShapeDtypeStruct(shape, BF16) for shape in result_shapes]
+        + [jax.ShapeDtypeStruct(small_shape, F32)],
+        grid=(1,),
+        in_specs=specs + [anywhere] * len(last_grads),
+        out_specs=[vmem()] + [anywhere] * len(result_shapes) + [vmem()],
+        scratch_shapes=[pltpu.VMEM(shape, dtype) for shape, dtype in out_shapes + work]
+        + [pltpu.VMEM(tail_shape, BF16), pltpu.VMEM(small_shape, F32), got, got]
+        + scratch + small_scratch(small_shape, sizes)[:4] + sems + small_scratch(small_shape, sizes)[4:]
+        + [pltpu.SemaphoreType.DMA((n - 1,))] * 4,
+        compiler_params=pltpu.CompilerParams(
+            collective_id=4, has_side_effects=True, vmem_limit_bytes=62 << 20
+        ),
+        name="first_block_back_and_sums",
+    )(*arrays, *last_grads)
+
+
+FUSED = True
+
+
+def specs_of(args):
     specs, arrays = [], []
     for array, layer in args:
         arrays.append(array)
@@ -822,6 +999,11 @@
             specs.append(pl.BlockSpec(array.shape, lambda *_, nd=array.ndim: (0,) * nd, pipeline_mode=pl.Buffered(1)))
         else:
             specs.append(layer_spec(array, layer))
+    return specs, arrays
+
+
+def call(kernel, args, outs, scratch, name):
+    specs, arrays = specs_of(args)
     return pl.pallas_call(
         kernel,
         out_shape=[jax.ShapeDtypeStruct(shape, dtype) for shape, dtype in outs],
@@ -894,34 +1076,46 @@
         weights(1) + [(x1, None), (normed1, None), (keyval1, None), (routes_t, 1), (lengths, "smem"), (keep, None), (cotangent[0], None)],
         [((count, width), BF16)] + out_shapes, kept_shapes + sum_shapes + work, "second_block",
     )
-    received1 = share(part1, n, True, 1, "scatter_keyval")
-    kv1, small1, up0, down0, out0, query0, router0, part0, small0, mid0, ngrad0 = call(
-        back_kernel,
-        weights(0) + [(x1, None), (normed1, None), (received1, None), (gain1, None), (w_kv, 1), (mid1, None), (ngrad1, None), (small1, None),
-         (normed0, None), (routes_t, 0), (lengths, "smem"), (keep, None), (small0, None), (keyval0, None)] + [(v, None) for v in kept0],
-        [((pair, width), BF16), ((8, width), F32)] + out_shapes, sum_shapes + work, "first_block_back",
-    )
-    received0 = share(part0, n, True, 1, "scatter_keyval")
-    kv0, small0, input_grad = call(
-        end_kernel,
-        [(x0, None), (normed0, None), (received0, None), (gain1, None), (w_kv, 0), (mid0, None), (ngrad0, None), (small0, None)],
-        [((pair, width), BF16), ((8, width), F32), ((count, width), F32)], [], "end",
-    )
-    kv_rows = experts + pair
-    tail = jnp.concatenate([kv0, router0.astype(BF16), kv1, router1.astype(BF16)])
-    tail_rows = rows_of(-(-tail.shape[0] // n))
-    tail = jnp.pad(tail, ((0, n * tail_rows - tail.shape[0]), (0, 0))).reshape(n, tail_rows, width)
-    chunks, starts = sum_plan(n, width, hidden // n, own, dp, tail_rows)
-    arrays = [up1, down1, query1, out1, up0, down0, query0, out0, tail]
-    up, down, expert_query, expert_out, tail, small = reduce_all(
-        arrays, chunks, starts,
-        [(layers,) + up1.shape[1:2] + (hidden,), (layers,) + down1.shape, (layers,) + query1.shape[1:], (layers,) + out1.shape[1:], (1,) + tail.shape],
-        jnp.concatenate([small0, small1]), sizes, 3,
-    )
+    tail_rows = rows_of(pair)
+    result_shapes = [
+        (layers,) + up1.shape[1:2] + (hidden,), (layers,) + down1.shape, (layers,) + query1.shape[1:],
+        (layers,) + out1.shape[1:], (1, n, tail_rows, width),
+    ]
+    fused = FUSED and n * dp == 32
+    if fused:
+        last = [(x1, None), (normed1, None), (part1, None), (gain1, None), (w_kv, 1), (mid1, None), (ngrad1, None), (small1, None), (router1, None)]
+        first = [(x0, None), (normed0, None), (routes_t, 0), (lengths, "smem"), (keep, None), (small0, None), (keyval0, None)]
+        input_grad, up, down, expert_query, expert_out, tail, small = finish_all(
+            weights(0) + last + first + [(v, None) for v in kept0], [up1, down1, query1, out1],
+            out_shapes, sum_shapes + work, result_shapes, sizes,
+        )
+    else:
+        received1 = share(part1, n, True, 1, "scatter_keyval")
+        kv1, small1, up0, down0, out0, query0, router0, part0, small0, mid0, ngrad0 = call(
+            back_kernel,
+            weights(0) + [(x1, None), (normed1, None), (received1, None), (gain1, None), (w_kv, 1), (mid1, None), (ngrad1, None), (small1, None),
+             (normed0, None), (routes_t, 0), (lengths, "smem"), (keep, None), (small0, None), (keyval0, None)] + [(v, None) for v in kept0],
+            [((pair, width), BF16), ((8, width), F32)] + out_shapes, sum_shapes + work, "first_block_back",
+        )
+        received0 = share(part0, n, True, 1, "scatter_keyval")
+        kv0, small0, input_grad = call(
+            end_kernel,
+            [(x0, None), (normed0, None), (received0, None), (gain1, None), (w_kv, 0), (mid0, None), (ngrad0, None), (small0, None)],
+            [((pair, width), BF16), ((8, width), F32), ((count, width), F32)], [], "end",
+        )
+        tail = jnp.zeros((n, tail_rows, width), BF16)
+        for block, rows in enumerate((kv0, router0, kv1, router1)):
+            tail = tail.at[block, : rows.shape[0]].set(rows.astype(BF16))
+        chunks, starts = sum_plan(n, width, hidden // n, own, dp, tail_rows)
+        arrays = [up1, down1, query1, out1, up0, down0, query0, out0, tail]
+        up, down, expert_query, expert_out, tail, small = reduce_all(
+            arrays, chunks, starts,
+            result_shapes,
+            jnp.concatenate([small0, small1]), sizes, 3,
+        )
     down = down[:, :, : hidden // n].reshape(layers, hidden, width).astype(F32)
-    tail = tail.reshape(n * tail_rows, width)[: layers * kv_rows].reshape(layers, kv_rows, width).astype(F32)
-    kv = jnp.swapaxes(tail[:, :pair], 1, 2)
-    router = jnp.swapaxes(tail[:, pair:], 1, 2)
+    kv = jnp.swapaxes(tail[0, 0:4:2, :pair].astype(F32), 1, 2)
+    router = jnp.swapaxes(tail[0, 1:4:2, :experts].astype(F32), 1, 2)
     norms = small.reshape(layers, -1, width)
     expert_query = jnp.swapaxes(expert_query[:, :own].reshape(layers, local, head, width), 2, 3).astype(F32)
     expert_out = expert_out[:, :own].reshape(layers, local, head, width).astype(F32)

time: 320 us -> 297 us (0.928)
  Pallas kernels: 296 us -> 274 us
    pallas_call x5 -> x3, Pallas kernels: 82.1 us -> 53.9 us  [call(): pl.pallas_call(kernel, out_shape=[jax.ShapeDtypeStruct(shape, dtype) for...]
    pallas_call x1, Pallas kernels: 128 us -> 154 us  [finish_all(): pl.pallas_call(partial(finish_kernel, chunks, groups, len(scratch)), out_...]
    pallas_call x4 -> x2, Pallas kernels: 44.5 us -> 24.5 us  [share(): pl.pallas_call(partial(share_kernel, n, scatter), out_shape=jax.ShapeDtyp...]
where the time goes in v2:
time: 297 us; the launch traced here: 295 us
  Pallas kernels  274 us (92%)
  other arithmetic  14.5 us (5%)
  local copies, waits for them, and re-layouts  5.87 us (2%)
    pallas_call x1, Pallas kernels, finish_all(): pl.pallas_call(partial(finish_kernel, chunks, groups, len(scratch)), out_...  154 us
    pallas_call x3, Pallas kernels, call(): pl.pallas_call(kernel, out_shape=[jax.ShapeDtypeStruct(shape, dtype) for...  53.9 us
    pallas_call x1, Pallas kernels, gather_all(): pl.pallas_call(partial(gather_kernel, orders), out_shape=[jax.ShapeDtypeS...  41.1 us
    pallas_call x2, Pallas kernels, share(): pl.pallas_call(partial(share_kernel, n, scatter), out_shape=jax.ShapeDtyp...  24.5 us

profile of v2, /device:TPU:0, one launch (start us, length us, event | category | flops | bytes accessed | tf_op | source)
XLA Modules:
  0.0 295.2 jit_solution(14971273455225827752)
XLA Ops:
  0.6 2.1 pre.1
  2.7 11.8 %gather_keyval.2 = bf16[4,256,128]{2,1,0:T(8,128)(2,1)} custom-call(bf16[256,128]{1,0:T(8,128)(2,1)} %get-tuple-element.51.mine), custom_call_target="tpu_custom_call" | custom-call | tf_op jit(solution)/shard_map/gather_keyval/pallas_call | solution.py:814
  14.5 41.1 %gather_experts.1 = (bf16[4,384,512]{2,1,0:T(8,128)(2,1)}, bf16[4,384,512]{2,1,0:T(8,128)(2,1)}, bf16[4,384,512]{2,1,0:T(8,128)(2,1)}, bf16[4,384,512]{2,1,0:T(8,128)(2,1)}) custom-call(bf16[2,384,512]{2,1,0:T(8,128)(2,1)} %bitcast.61, bf16[2,384,512]{2,1,0:T(8,128)(2,1)} %bitcast.62), custom_call_target="tpu_custom_call" | custom-call | tf_op jit(solution)/shard_map/gather_experts/pallas_call | solution.py:796
  55.7 16.9 %first_block.1 = (f32[256,24]{1,0:T(8,128)}, bf16[8,256,128]{2,1,0:T(8,128)(2,1)}, f32[8,8,256]{2,1,0:T(8,128)}, bf16[8,256,128]{2,1,0:T(8,128)(2,1)}, bf16[256,...) custom-call(f32[2,512]{1,0:T(2,128)} %refs_13_.1, ...), custom_call_target="tpu_custom_call" | custom-call | tf_op jit(solution)/shard_map/first_block/pallas_call | solution.py:1007
  72.5 12.7 %gather_keyval.3 = bf16[4,256,128]{2,1,0:T(8,128)(2,1)} custom-call(bf16[256,128]{1,0:T(8,128)(2,1)} %get-tuple-element.54.mine), custom_call_target="tpu_custom_call" | custom-call | tf_op jit(solution)/shard_map/gather_keyval/pallas_call | solution.py:814
  85.2 35.0 %second_block.1 = (bf16[256,512]{1,0:T(8,128)(2,1)}, bf16[4,512,512]{2,1,0:T(8,128)(2,1)}, bf16[4,512,512]{2,1,0:T(8,128)(2,1)}, bf16[4,384,512]{2,1,0:T(8,128)(...) custom-call(f32[2,512]{1,0:T(2,128)} %refs_13_.1, ...), custom_call_target="tpu_custom_call" | custom-call | tf_op jit(solution)/shard_map/second_block/pallas_call | solution.py:1007
  120.2 154.5 %first_block_back_and_sums.1 = (f32[256,512]{1,0:T(8,128)}, bf16[2,512,2048]{2,1,0:T(8,128)(2,1)}, bf16[2,4,512,512]{3,2,1,0:T(8,128)(2,1)}, bf16[2,384,512]{2,1...) custom-call(f32[2,512]{1,0:T(2,128)} %refs_13_.1, ...), custom_call_target="tpu_custom_call" | custom-call | tf_op jit(solution)/shard_map/first_block_back_and_sums/pallas_call | solution.py:970
  274.7 0.0 copy-start.3
  274.7 1.3 slice.32
  276.1 0.9 fusion
  277.0 0.6 copy_bitcast_fusion
  277.6 0.6 copy_bitcast_fusion.2
  278.2 1.4 convert_bitcast_fusion.2
  279.6 0.0 copy-start.2
  279.6 1.1 convert_bitcast_fusion.1
  280.7 1.0 copy.33
  281.7 0.0 copy-done.3
  281.7 0.0 copy-start.1
  281.7 1.4 convert_bitcast_fusion
  283.1 0.0 copy-done.2
  283.1 1.4 convert.11
  284.4 0.6 copy-done.1
  285.0 0.0 copy-start
  285.0 4.4 %convert_element_type.39 = f32[2,512,2048]{2,1,0:T(8,128)} convert(bf16[2,512,2048]{2,1,0:T(8,128)(2,1)S(1)} %copy-done.1) | non-fusion elementwise | flops 2097152 | bytes 12582912 | tf_op jit(solution)/shard_map/convert_element_type | solution.py:1124
  289.5 0.0 copy-done
  289.5 0.0 copy-start.4
  289.5 4.9 %bitcast_convert_fusion = f32[2,2048,512]{2,1,0:T(8,128)} fusion(bf16[2,4,512,512]{3,2,1,0:T(8,128)(2,1)S(1)} %copy-done), kind=kLoop, calls=%fused_computation | loop fusion | flops 2097152 | bytes 12582912 | tf_op jit(solution)/shard_map/convert_element_type | solution.py:1116
  294.4 0.0 copy-done.4
  294.4 0.8 copy.44
Async XLA Ops:
  274.7 7.0 %copy-start.3 = (bf16[2,384,512]{2,1,0:T(8,128)(2,1)S(1)}, bf16[2,384,512]{2,1,0:T(8,128)(2,1)}, u32[]{:S(2)}) copy-start(bf16[2,384,512]{2,1,0:T(8,128)(2,1)} %get-tuple-element.75) | copy-start | bytes 2359300
  279.6 3.4 %copy-start.2 = (bf16[2,384,512]{2,1,0:T(8,128)(2,1)S(1)}, bf16[2,384,512]{2,1,0:T(8,128)(2,1)}, u32[]{:S(2)}) copy-start(bf16[2,384,512]{2,1,0:T(8,128)(2,1)} %get-tuple-element.76) | copy-start | bytes 2359300
  281.7 3.3 %copy-start.1 = (bf16[2,512,2048]{2,1,0:T(8,128)(2,1)S(1)}, bf16[2,512,2048]{2,1,0:T(8,128)(2,1)}, u32[]{:S(2)}) copy-start(bf16[2,512,2048]{2,1,0:T(8,128)(2,1)} %get-tuple-element.77) | copy-start | bytes 12582916
  285.0 4.5 %copy-start = (bf16[2,4,512,512]{3,2,1,0:T(8,128)(2,1)S(1)}, bf16[2,4,512,512]{3,2,1,0:T(8,128)(2,1)}, u32[]{:S(2)}) copy-start(bf16[2,4,512,512]{3,2,1,0:T(8,128)(2,1)} %get-tuple-element.78) | copy-start | bytes 12582916
  289.5 4.9 %copy-start.4 = (f32[256,512]{1,0:T(8,128)S(1)}, f32[256,512]{1,0:T(8,128)}, u32[]{:S(2)}) copy-start(f32[256,512]{1,0:T(8,128)} %get-tuple-element.72) | copy-start | bytes 1572868

commit v3 on v2

--- a/solution.py
+++ b/solution.py
@@ -134,12 +134,14 @@
     )
 
 
-def layer_forward(x, normed, weights, mask, spread, dense, gated, kept):
+def layer_forward(x, normed, weights, mask, spread, dense, gated, kept, between=None):
+    between = between or (lambda *place: None)
     count = normed.shape[0]
     gates, picked = make_gates(normed[...], weights.w_router[...], spread)
     kept.gates[...] = gates
     dense[...] = nt(normed[...], weights.w_query[...]).astype(BF16).astype(F32) * 0.125
     gated[...] = jnp.zeros(gated.shape, F32)
+    between("queries")
     keys, values = split_keyval(kept.keyval[...])
     keys = keys.astype(BF16)
     values_t = values.T.astype(BF16)
@@ -159,12 +161,15 @@
         kept.attended[k] = attended
         gate = gate_column(kept.gates[...], which)
         place_tiles(gated, chosen, gate * attended.astype(F32))
+        between("slot", k)
         return carry
 
     lax.fori_loop(0, spread.shape[0], slot, 0)
     kept.gated[...] = gated[...].astype(BF16)
+    between("attended")
     middle = x + nn(kept.gated[...], weights.w_out[...])
     kept.middle[...] = middle
+    between("middle")
     hat, _ = norm_parts(middle)
     normed2 = (hat * weights.gain2[...] + weights.bias2[...]).astype(BF16)
     active = gelu_parts(nn(normed2, weights.w_up[...]))[0].astype(BF16)
@@ -202,6 +207,7 @@
     middle_grad = stream_grad + back
     out.middle_grad[...] = middle_grad
     rounded = middle_grad.astype(BF16)
+    between("out")
     gated_t = kept.gated[...].astype(F32).T.astype(BF16)
     for block in range(blocks):
         rows = slice(block * own, (block + 1) * own)
@@ -986,7 +992,355 @@
     )(*arrays, *last_grads)
 
 
-FUSED = True
+class Gather:
+    def __init__(self, sources, targets, orders, send, recv, own_sem):
+        self.sources, self.targets, self.orders = sources, targets, orders
+        self.send, self.recv, self.own_sem = send, recv, own_sem
+        self.at, self.size = place_of()
+        self.stage = [0] * len(sources)
+
+    def copies(self, i, s):
+        rows, order = self.sources[i].shape[0], self.orders[i]
+        first, part = 0, rows
+        for axis in reversed(order[max(s, 1) :]):
+            part = part // self.size[axis]
+            first = first + self.at[axis] * part
+        here = self.at["z"]
+        out = []
+        if s == 0:
+            place = pl.ds(pl.multiple_of(here * rows, rows), rows)
+            out.append(pltpu.make_async_copy(self.sources[i], self.targets[i].at[place, :], self.own_sem.at[i]))
+        for step, (_, device) in enumerate(peers_of(order[s], self.at, self.size)):
+            for other in range(1 if s == 0 else self.size["z"] - 1):
+                block = here if s == 0 else lax.rem(here + 1 + other, self.size["z"])
+                target = self.targets[i].at[pl.ds(pl.multiple_of(block * rows + first, part), part), :]
+                source = self.sources[i].at[pl.ds(pl.multiple_of(first, part), part), :] if s == 0 else target
+                index = (i, s, step, other)
+                out.append(
+                    pltpu.make_async_remote_copy(
+                        src_ref=source, dst_ref=target, send_sem=self.send.at[index], recv_sem=self.recv.at[index],
+                        device_id=device, device_id_type=pl.DeviceIdType.MESH,
+                    )
+                )
+        return out
+
+    def begin(self, i):
+        for copy in self.copies(i, 0):
+            copy.start()
+
+    def advance(self, i):
+        s = self.stage[i]
+        for copy in self.copies(i, s):
+            copy.wait()
+        self.stage[i] = s + 1
+        if s + 1 < len(self.orders[i]):
+            for copy in self.copies(i, s + 1):
+                copy.start()
+
+
+def share_orders(rows, count, size):
+    orders = []
+    for i in range(count):
+        left, axes = rows // 16, ""
+        for axis in "cxy" if i % 2 else "cyx":
+            if left % size[axis] == 0:
+                left, axes = left // size[axis], axis + axes
+        orders.append("z" + axes)
+    return orders
+
+
+class KeyvalGather:
+    def __init__(self, keyval, count, send, recv):
+        self.keyval, self.count, self.send, self.recv = keyval, count, send, recv
+        self.at, self.size = place_of()
+
+    def own(self):
+        return self.keyval.at[pl.ds(pl.multiple_of(self.at["z"] * self.count, self.count), self.count), :]
+
+    def copies(self):
+        return [
+            pltpu.make_async_remote_copy(
+                src_ref=self.own(), dst_ref=self.own(), send_sem=self.send.at[step], recv_sem=self.recv.at[step],
+                device_id=device, device_id_type=pl.DeviceIdType.MESH,
+            )
+            for step, (_, device) in enumerate(peers_of("z", self.at, self.size))
+        ]
+
+    def start(self):
+        for copy in self.copies():
+            copy.start()
+
+    def wait(self):
+        for copy in self.copies():
+            copy.wait()
+
+
+INPUTS = ("x", "cotangent", "routes", "lengths", "keep", "gain1", "bias1", "w_kv", "w_router", "gain2", "bias2")
+GRADS = ("up", "down", "w_query", "w_out")
+
+
+def whole_kernel(chunks, groups, counts, *refs):
+    given, refs = named(INPUTS, refs)
+    (queries, outs, w_up, w_down), refs = refs[:4], refs[4:]
+    (activations, input_grad), refs = refs[:2], refs[2:]
+    results, small_out, refs = refs[:5], refs[5], refs[6:]
+    experts_in, refs = refs[:4], refs[4:]
+    (up_here, down_here), refs = refs[:2], refs[2:]
+    kept, normed = [], []
+    for _ in range(2):
+        normed.append(refs[0])
+        one, refs = named(KEPT, refs[1:])
+        kept.append(one)
+    grads = []
+    for _ in range(2):
+        one, refs = named(GRADS, refs)
+        grads.append(one)
+    (stream, router, middle_grad, normed_grad, part1, part0, tail, small_in), refs = refs[:8], refs[8:]
+    sums, refs = named(SUMS, refs)
+    (mask, spread, dense, gated, got1, got0), refs = refs[:6], refs[6:]
+    scratch, refs = refs[:counts], refs[counts:]
+    small_got, refs = refs[:4], refs[4:]
+    sems, small_sems, refs = refs[:5], refs[5:7], refs[7:]
+    gather_sems, keyval_sems, load_sem = refs[:3], refs[3:11], refs[11]
+
+    count, width = given.x.shape
+    rows = small_in.shape[0] // 2
+    experts = given.w_router.shape[1]
+    pair = given.w_kv.shape[2]
+    sources = []
+    for l in (1, 0):
+        sources += [getattr(grads[l], name) for name in GRADS]
+    total = Sums(chunks, sources + [tail], results, scratch, sems)
+    little = SmallSum(small_in, small_out, small_got, *small_sems)
+    smalls = [small_in.at[0:rows, :], small_in.at[rows : 2 * rows, :]]
+    gather = Gather(
+        [queries.at[0], outs.at[0], queries.at[1], outs.at[1]], experts_in,
+        share_orders(queries.shape[1], 4, total.size), *gather_sems,
+    )
+    keyval_gather = [KeyvalGather(kept[l].keyval, count, *keyval_sems[2 * l : 2 * l + 2]) for l in range(2)]
+    keyval_sum = [KeyvalSum(part0, got0, *keyval_sems[4:6]), KeyvalSum(part1, got1, *keyval_sems[6:8])]
+    weights = []
+    for l in range(2):
+        row = pl.ds(l, 1)
+        weights.append(
+            Refs(
+                gain1=given.gain1.at[row, :], bias1=given.bias1.at[row, :], gain2=given.gain2.at[row, :],
+                bias2=given.bias2.at[row, :], w_kv=given.w_kv.at[l], w_router=given.w_router.at[l],
+                w_query=experts_in[2 * l], w_out=experts_in[2 * l + 1], w_up=up_here, w_down=down_here,
+            )
+        )
+    outputs = [
+        Refs(
+            up=grads[l].up, down=grads[l].down, w_out=grads[l].w_out, w_query=grads[l].w_query, router=router,
+            keyval=(part0, part1)[l], small=smalls[l], middle_grad=middle_grad, normed_grad=normed_grad,
+        )
+        for l in range(2)
+    ]
+
+    def loads(l):
+        return [
+            pltpu.make_async_copy(w_up.at[l], up_here, load_sem.at[l, 0]),
+            pltpu.make_async_copy(w_down.at[l], down_here, load_sem.at[l, 1]),
+        ]
+
+    def load(l):
+        for copy in loads(l):
+            copy.start()
+
+    def loaded(l):
+        for copy in loads(l):
+            copy.wait()
+
+    done = [0] * len(groups)
+
+    def begin(group):
+        for i in groups[group]:
+            total.send_down(i, 0)
+
+    def advance(group):
+        if done[group] < total.stages(groups[group][0]):
+            for i in groups[group]:
+                total.advance(i, done[group])
+            done[group] += 1
+
+    def pre(l, x):
+        pre_layer(x, weights[l].gain1[...], weights[l].bias1[...], weights[l].w_kv[...], normed[l], keyval_gather[l].own())
+        keyval_gather[l].start()
+
+    load(0)
+    greet("cxyz", total.at, total.size)
+    gather.begin(0)
+    gather.begin(1)
+    x = given.x[...].astype(F32)
+    pre(0, x)
+    gather.begin(2)
+    gather.begin(3)
+    fill_mask(given.lengths, given.keep, mask)
+    spread_routes(given.routes.at[0], spread)
+    small_in[...] = jnp.zeros(small_in.shape, F32)
+    tail[...] = jnp.zeros(tail.shape, BF16)
+    for i in (0, 1, 0, 1, 0, 1, 0):
+        gather.advance(i)
+    keyval_gather[0].wait()
+
+    def first_between(place, k=None):
+        if place == "slot":
+            for when in (1, 4):
+
+                @pl.when(k == when)
+                def _():
+                    gather.advance(2)
+                    gather.advance(3)
+
+        elif place == "attended":
+            gather.advance(1)
+            gather.advance(2)
+            gather.advance(3)
+        elif place == "middle":
+            loaded(0)
+
+    result, picked = layer_forward(x, normed[0], weights[0], mask, spread, dense, gated, kept[0], first_between)
+    load(1)
+    count_chosen(picked, given.keep, smalls[0])
+    stream[...] = result
+    pre(1, result)
+    spread_routes(given.routes.at[1], spread)
+
+    def second_between(place, k=None):
+        if place == "queries":
+            keyval_gather[1].wait()
+        elif place == "middle":
+            loaded(1)
+
+    gather.advance(2)
+    gather.advance(3)
+    result, picked = layer_forward(
+        stream[...], normed[1], weights[1], mask, spread, dense, gated, kept[1], second_between
+    )
+    count_chosen(picked, given.keep, smalls[1])
+    activations[...] = result.astype(BF16)
+    kept_col = jnp.broadcast_to(own_columns(given.keep, count).astype(F32), (LANES, count)).T
+    kept_col = jnp.concatenate([kept_col] * (width // LANES), axis=1)
+
+    def last_between(place, k=None):
+        if place == "hidden":
+            load(0)
+            begin(0)
+        elif place == "out":
+            pass
+        elif place == "slot":
+
+            @pl.when(k == 1)
+            def _():
+                advance(0)
+
+        elif place == "keyval":
+            keyval_sum[1].start()
+            advance(0)
+
+    layer_back(
+        given.cotangent[...].astype(F32) * kept_col, normed[1], weights[1], mask, spread, dense, gated, kept[1],
+        sums, outputs[1], last_between,
+    )
+    tail[3, 0:experts, :] = router[...].astype(BF16)
+    begin(1)
+    stream_grad = layer_finish(
+        stream[...], normed[1], keyval_sum[1].total(), weights[1].gain1[...], weights[1].w_kv[...], middle_grad,
+        normed_grad, tail.at[2, 0:pair], smalls[1],
+    )
+    advance(0)
+    advance(1)
+    spread_routes(given.routes.at[0], spread)
+    loaded(0)
+
+    def between(place, k=None):
+        if place == "hidden":
+            begin(2)
+            advance(0)
+            advance(1)
+        elif place == "slot":
+
+            @pl.when(k == 2)
+            def _():
+                advance(0)
+                advance(2)
+
+            @pl.when(k == 5)
+            def _():
+                advance(1)
+
+        elif place == "keyval":
+            keyval_sum[0].start()
+            advance(0)
+            advance(2)
+
+    layer_back(
+        stream_grad, normed[0], weights[0], mask, spread, dense, gated, kept[0], sums, outputs[0], between
+    )
+    tail[1, 0:experts, :] = router[...].astype(BF16)
+    begin(3)
+    advance(1)
+    input_grad[...] = layer_finish(
+        given.x[...].astype(F32), normed[0], keyval_sum[0].total(), weights[0].gain1[...], weights[0].w_kv[...],
+        middle_grad, normed_grad, tail.at[0, 0:pair], smalls[0],
+    )
+    begin(4)
+    little.start(0)
+    for step in range(2 * len(chunks[-1].order)):
+        for group in range(len(groups)):
+            advance(group)
+        if step < 4:
+            little.advance(step)
+
+
+def run_whole(args, weights_out, shapes, sizes):
+    specs, arrays = specs_of(args)
+    queries, _, w_up, w_down = weights_out
+    layers, own, width = queries.shape
+    n = sizes["z"]
+    count, flat, hidden = args[0][0].shape[0], n * own, w_up.shape[2]
+    chunks, groups = finish_chunks(n, shapes.up[1], shapes.down[1], shapes.own[1], shapes.tail[1])
+    scratch, sems = sum_scratch(chunks, [shapes.up, shapes.down, shapes.own, shapes.own] * 2 + [shapes.tail], sizes)
+    small_shape = (16, width)
+    results = [
+        (layers, shapes.up[1], hidden), (layers,) + shapes.down, (layers,) + shapes.own[1:], (layers,) + shapes.own[1:],
+        (1,) + shapes.tail,
+    ]
+    most = max(sizes.values()) - 1
+    gather_sem = pltpu.SemaphoreType.DMA((4, 4, most, n - 1))
+    got = pltpu.VMEM((n - 1, shapes.group // n, shapes.pair), BF16)
+    part = pltpu.VMEM((shapes.group, shapes.pair), BF16)
+    one = pltpu.VMEM((count, width), F32)
+    local = [pltpu.VMEM((flat, width), BF16)] * 4
+    local += [pltpu.VMEM(w_up.shape[1:], BF16), pltpu.VMEM(w_down.shape[1:], BF16)]
+    for _ in range(2):
+        local += [pltpu.VMEM((count, width), BF16), part]
+        local += [pltpu.VMEM(shape, dtype) for shape, dtype in shapes.kept]
+    local += [pltpu.VMEM(shape, BF16) for shape in (shapes.up, shapes.down, shapes.own, shapes.own)] * 2
+    local += [one, pltpu.VMEM((shapes.experts, width), F32), one, one, part, part]
+    local += [pltpu.VMEM(shapes.tail, BF16), pltpu.VMEM(small_shape, F32)]
+    local += [pltpu.VMEM(shape, dtype) for shape, dtype in shapes.sums]
+    mask, spread, dense, gated = [pltpu.VMEM(shape, dtype) for shape, dtype in shapes.work]
+    local += [mask, spread, dense, gated, got, got]
+    small_refs = small_scratch(small_shape, sizes)
+    anywhere = pl.BlockSpec(memory_space=pl.ANY)
+    return pl.pallas_call(
+        partial(whole_kernel, chunks, groups, len(scratch)),
+        out_shape=[jax.ShapeDtypeStruct((count, width), BF16), jax.ShapeDtypeStruct((count, width), F32)]
+        + [jax.ShapeDtypeStruct(shape, BF16) for shape in results]
+        + [jax.ShapeDtypeStruct(small_shape, F32)],
+        grid=(1,),
+        in_specs=specs + [anywhere] * 4,
+        out_specs=[vmem(), vmem()] + [anywhere] * 5 + [vmem()],
+        scratch_shapes=local + scratch + small_refs[:4] + sems + small_refs[4:]
+        + [gather_sem, gather_sem, pltpu.SemaphoreType.DMA((4,))]
+        + [pltpu.SemaphoreType.DMA((n - 1,))] * 8
+        + [pltpu.SemaphoreType.DMA((2, 2))],
+        compiler_params=pltpu.CompilerParams(
+            collective_id=5, has_side_effects=True, vmem_limit_bytes=63 << 20
+        ),
+        name="both_blocks",
+    )(*arrays, *weights_out)
 
 
 def specs_of(args):
@@ -1039,14 +1393,9 @@
     queries_t = jnp.swapaxes(w_query, 2, 3).reshape(layers, own, width)
     outs = w_out.reshape(layers, own, width)
     sizes = axis_sizes()
-    gathered = [array.reshape(flat, width) for array in gather_all((queries_t, outs), sizes, 2)]
-    wq, wo = gathered[0::2], gathered[1::2]
 
     def rows_of(least):
         return -(-least // (16 * dp)) * 16 * dp
-
-    def weights(l):
-        return [(gain1, None), (bias1, None), (w_kv, l), (router_t, l), (wq[l], None), (wo[l], None), (gain2, None), (bias2, None), (w_up, l), (w_down, l)]
 
     kept_shapes = [
         ((count, experts), F32), ((topk, count, LANES), BF16), ((topk, 8, count), F32),
@@ -1059,37 +1408,47 @@
         ((n, rows_of(own), width), BF16), ((n, rows_of(own), width), BF16),
         ((experts, width), F32), ((group, pair), BF16), ((8, width), F32), ((count, width), F32), ((count, width), F32),
     ]
-    normed0, keyval0 = call(
-        pre_kernel, [(x0, None), (gain1, None), (bias1, None), (w_kv, 0)],
-        [((count, width), BF16), ((count, pair), BF16)], [], "pre",
-    )
-    keyval0 = share(keyval0, n, False, 0, "gather_keyval").reshape(group, pair)
-    *kept0, x1, normed1, keyval1, small0 = call(
-        first_kernel,
-        weights(0) + [(x0, None), (normed0, None), (keyval0, None), (routes_t, 0), (lengths, "smem"), (keep, None), (gain1, None), (bias1, None), (w_kv, 1)],
-        kept_shapes + [((count, width), F32), ((count, width), BF16), ((count, pair), BF16), ((8, width), F32)],
-        work, "first_block",
-    )
-    keyval1 = share(keyval1, n, False, 0, "gather_keyval").reshape(group, pair)
-    activations, up1, down1, out1, query1, router1, part1, small1, mid1, ngrad1 = call(
-        turn_kernel,
-        weights(1) + [(x1, None), (normed1, None), (keyval1, None), (routes_t, 1), (lengths, "smem"), (keep, None), (cotangent[0], None)],
-        [((count, width), BF16)] + out_shapes, kept_shapes + sum_shapes + work, "second_block",
-    )
-    tail_rows = rows_of(pair)
-    result_shapes = [
-        (layers,) + up1.shape[1:2] + (hidden,), (layers,) + down1.shape, (layers,) + query1.shape[1:],
-        (layers,) + out1.shape[1:], (1, n, tail_rows, width),
-    ]
-    fused = FUSED and n * dp == 32
-    if fused:
-        last = [(x1, None), (normed1, None), (part1, None), (gain1, None), (w_kv, 1), (mid1, None), (ngrad1, None), (small1, None), (router1, None)]
-        first = [(x0, None), (normed0, None), (routes_t, 0), (lengths, "smem"), (keep, None), (small0, None), (keyval0, None)]
-        input_grad, up, down, expert_query, expert_out, tail, small = finish_all(
-            weights(0) + last + first + [(v, None) for v in kept0], [up1, down1, query1, out1],
-            out_shapes, sum_shapes + work, result_shapes, sizes,
+    if n * dp == 32 and layers == 2:
+        all_shapes = Refs(
+            up=out_shapes[0][0], down=out_shapes[1][0], own=out_shapes[2][0], tail=(n, rows_of(pair), width), group=group,
+            pair=pair, experts=experts, kept=kept_shapes, sums=sum_shapes, work=work,
+        )
+        given = [
+            (x0, None), (cotangent[0], None), (routes_t, None), (lengths, "smem"), (keep, None), (gain1, None),
+            (bias1, None), (w_kv, None), (router_t, None), (gain2, None), (bias2, None),
+        ]
+        activations, input_grad, up, down, expert_query, expert_out, tail, small = run_whole(
+            given, (queries_t, outs, w_up, w_down), all_shapes, sizes
         )
     else:
+        gathered = [array.reshape(flat, width) for array in gather_all((queries_t, outs), sizes, 2)]
+        wq, wo = gathered[0::2], gathered[1::2]
+        def weights(l):
+            return [(gain1, None), (bias1, None), (w_kv, l), (router_t, l), (wq[l], None), (wo[l], None), (gain2, None), (bias2, None), (w_up, l), (w_down, l)]
+
+
+        normed0, keyval0 = call(
+            pre_kernel, [(x0, None), (gain1, None), (bias1, None), (w_kv, 0)],
+            [((count, width), BF16), ((count, pair), BF16)], [], "pre",
+        )
+        keyval0 = share(keyval0, n, False, 0, "gather_keyval").reshape(group, pair)
+        *kept0, x1, normed1, keyval1, small0 = call(
+            first_kernel,
+            weights(0) + [(x0, None), (normed0, None), (keyval0, None), (routes_t, 0), (lengths, "smem"), (keep, None), (gain1, None), (bias1, None), (w_kv, 1)],
+            kept_shapes + [((count, width), F32), ((count, width), BF16), ((count, pair), BF16), ((8, width), F32)],
+            work, "first_block",
+        )
+        keyval1 = share(keyval1, n, False, 0, "gather_keyval").reshape(group, pair)
+        activations, up1, down1, out1, query1, router1, part1, small1, mid1, ngrad1 = call(
+            turn_kernel,
+            weights(1) + [(x1, None), (normed1, None), (keyval1, None), (routes_t, 1), (lengths, "smem"), (keep, None), (cotangent[0], None)],
+            [((count, width), BF16)] + out_shapes, kept_shapes + sum_shapes + work, "second_block",
+        )
+        tail_rows = rows_of(pair)
+        result_shapes = [
+            (layers,) + up1.shape[1:2] + (hidden,), (layers,) + down1.shape, (layers,) + query1.shape[1:],
+            (layers,) + out1.shape[1:], (1, n, tail_rows, width),
+        ]
         received1 = share(part1, n, True, 1, "scatter_keyval")
         kv1, small1, up0, down0, out0, query0, router0, part0, small0, mid0, ngrad0 = call(
             back_kernel,

time: 297 us -> 237 us (0.80)
  Pallas kernels: 274 us -> 213 us
    pallas_call x7 -> x1, Pallas kernels: 274 us -> 213 us  [run_whole(): pl.pallas_call(partial(whole_kernel, chunks, groups, len(scratch)), out_s...]
where the time goes in v3:
time: 237 us; the launch traced here: 236 us
  Pallas kernels  213 us (90%)
  other arithmetic  16.5 us (7%)
  local copies, waits for them, and re-layouts  5.93 us (3%)
    pallas_call x1, Pallas kernels, run_whole(): pl.pallas_call(partial(whole_kernel, chunks, groups, len(scratch)), out_s...  213 us
    convert_element_type x1, other arithmetic, body(): down = down[:, :, :hidden // n].reshape(layers, hidden, width).astype(F32)  6.93 us

profile of v3, /device:TPU:0, one launch (start us, length us, event | category | flops | bytes accessed | tf_op | source)
XLA Modules:
  0.0 235.9 jit_solution(16480977951884783903)
XLA Ops:
  0.7 212.8 %both_blocks.1 = (bf16[256,512]{1,0:T(8,128)(2,1)}, f32[256,512]{1,0:T(8,128)}, bf16[2,512,2048]{2,1,0:T(8,128)(2,1)}, bf16[2,4,512,512]{3,2,1,0:T(8,128)(2,1)},...) custom-call(bf16[256,512]{1,0:T(8,128)(2,1)} %bitcast.48, ...), custom_call_target="tpu_custom_call" | custom-call | tf_op jit(solution)/shard_map/both_blocks/pallas_call | solution.py:1327
  213.4 1.0 fusion
  214.4 0.6 copy_bitcast_fusion
  215.0 0.6 copy_bitcast_fusion.2
  215.6 1.0 convert_bitcast_fusion.1
  216.6 1.0 copy.33
  217.6 1.4 convert_bitcast_fusion.2
  219.1 1.3 slice.32
  220.3 0.0 copy-start
  220.3 6.9 %bitcast_convert_fusion = f32[2,2048,512]{2,1,0:T(8,128)} fusion(bf16[2,4,512,512]{3,2,1,0:T(8,128)(2,1)} %get-tuple-element.28), kind=kLoop, calls=%fused_computation | loop fusion | flops 2097152 | bytes 12582912 | tf_op jit(solution)/shard_map/convert_element_type | solution.py:1475
  227.3 0.0 copy-done
  227.3 0.0 copy-start.2
  227.3 0.0 copy-start.1
  227.3 4.4 %convert_element_type.39 = f32[2,512,2048]{2,1,0:T(8,128)} convert(bf16[2,512,2048]{2,1,0:T(8,128)(2,1)S(1)} %copy-done) | non-fusion elementwise | flops 2097152 | bytes 12582912 | tf_op jit(solution)/shard_map/convert_element_type | solution.py:1483
  231.7 0.0 copy-start.4
  231.7 0.0 copy-start.3
  231.7 0.0 copy-done.2
  231.7 1.4 convert.11
  233.1 0.0 copy-done.1
  233.1 1.4 convert_bitcast_fusion
  234.4 0.0 copy-done.4
  234.4 0.7 copy.45
  235.1 0.0 copy-done.3
  235.1 0.8 copy.46
Async XLA Ops:
  220.3 6.9 %copy-start = (bf16[2,512,2048]{2,1,0:T(8,128)(2,1)S(1)}, bf16[2,512,2048]{2,1,0:T(8,128)(2,1)}, u32[]{:S(2)}) copy-start(bf16[2,512,2048]{2,1,0:T(8,128)(2,1)} %get-tuple-element.27) | copy-start | bytes 12582916
  227.3 4.5 %copy-start.2 = (bf16[2,384,512]{2,1,0:T(8,128)(2,1)S(1)}, bf16[2,384,512]{2,1,0:T(8,128)(2,1)}, u32[]{:S(2)}) copy-start(bf16[2,384,512]{2,1,0:T(8,128)(2,1)} %get-tuple-element.26) | copy-start | bytes 2359300
  227.3 5.8 %copy-start.1 = (bf16[2,384,512]{2,1,0:T(8,128)(2,1)S(1)}, bf16[2,384,512]{2,1,0:T(8,128)(2,1)}, u32[]{:S(2)}) copy-start(bf16[2,384,512]{2,1,0:T(8,128)(2,1)} %get-tuple-element.25) | copy-start | bytes 2359300
  231.7 2.7 %copy-start.4 = (bf16[256,512]{1,0:T(8,128)(2,1)S(1)}, bf16[256,512]{1,0:T(8,128)(2,1)}, u32[]{:S(2)}) copy-start(bf16[256,512]{1,0:T(8,128)(2,1)} %get-tuple-element.21) | copy-start | bytes 786436
  231.7 3.4 %copy-start.3 = (f32[256,512]{1,0:T(8,128)S(1)}, f32[256,512]{1,0:T(8,128)}, u32[]{:S(2)}) copy-start(f32[256,512]{1,0:T(8,128)} %get-tuple-element.22) | copy-start | bytes 1572868

commit v4 on v3

--- a/solution.py
+++ b/solution.py
@@ -9,6 +9,18 @@
 from jax.sharding import PartitionSpec as P
 
 F32 = jnp.float32
+EXP = "exp"
+CLHXY = "clhxy"
+CLHYX = "clhyx"
+CXLHY = "cxlhy"
+CXYLH = "cxylh"
+CXYZ = "cxyz"
+CYLHX = "cylhx"
+CYXLH = "cyxlh"
+CYXZ = "cyxz"
+ZXYC = "zxyc"
+ZYXC = "zyxc"
+WIDE, STACK, OWN = range(3)
 BF16 = jnp.bfloat16
 LANES = 128
 epsilon = 1e-05
@@ -74,7 +86,7 @@
 
 
 def own_columns(ref, count):
-    start = lax.axis_index("exp") * count
+    start = lax.axis_index(EXP) * count
     return ref[:, pl.ds(pl.multiple_of(start, count), count)]
 
 
@@ -87,7 +99,7 @@
 
 def fill_mask(lengths, keep, mask):
     group, count = mask.shape
-    start = lax.axis_index("exp") * count
+    start = lax.axis_index(EXP) * count
     position = start + iota((1, count), 1)
     low = jnp.zeros((1, count), jnp.int32)
     end = 0
@@ -146,37 +158,43 @@
     keys = keys.astype(BF16)
     values_t = values.T.astype(BF16)
 
-    def slot(k, carry):
-        which = spread[k]
-        chosen = which - lane_half((count, LANES))
-        query = select_tiles(dense, chosen).astype(BF16)
-        kept.query[k] = query
-        scores = nt(keys, query) + mask[...]
-        top = jnp.max(scores, axis=0, keepdims=True)
-        shares = jnp.exp(scores - top)
-        total = jnp.sum(shares, axis=0, keepdims=True)
-        kept.lse[k] = jnp.broadcast_to(top + jnp.log(total), kept.lse.shape[1:])
-        shares = (shares * (1.0 / total)).astype(BF16)
-        attended = nn(values_t, shares).T.astype(BF16)
-        kept.attended[k] = attended
-        gate = gate_column(kept.gates[...], which)
-        place_tiles(gated, chosen, gate * attended.astype(F32))
-        between("slot", k)
+    def pair(step, carry):
+        slots = [2 * step, 2 * step + 1]
+        which = [spread[k] for k in slots]
+        chosen = [w - lane_half((count, LANES)) for w in which]
+        queries = [select_tiles(dense, c).astype(BF16) for c in chosen]
+        scores = [nt(keys, query) + mask[...] for query in queries]
+        tops = [jnp.max(score, axis=0, keepdims=True) for score in scores]
+        shares = [jnp.exp(score - top) for score, top in zip(scores, tops)]
+        totals = [jnp.sum(share, axis=0, keepdims=True) for share in shares]
+        rounded = [(share * (1.0 / total)).astype(BF16) for share, total in zip(shares, totals)]
+        attended = [nn(values_t, share).T.astype(BF16) for share in rounded]
+        for i, k in enumerate(slots):
+            kept.query[k] = queries[i]
+            kept.lse[k] = jnp.broadcast_to(tops[i] + jnp.log(totals[i]), kept.lse.shape[1:])
+            kept.attended[k] = attended[i]
+            gate = gate_column(kept.gates[...], which[i])
+            place_tiles(gated, chosen[i], gate * attended[i].astype(F32))
+        between("slot", step)
         return carry
 
-    lax.fori_loop(0, spread.shape[0], slot, 0)
+    lax.fori_loop(0, spread.shape[0] // 2, pair, 0)
     kept.gated[...] = gated[...].astype(BF16)
     between("attended")
     middle = x + nn(kept.gated[...], weights.w_out[...])
     kept.middle[...] = middle
     between("middle")
+    return middle, picked
+
+
+def feed_forward(middle, weights):
     hat, _ = norm_parts(middle)
     normed2 = (hat * weights.gain2[...] + weights.bias2[...]).astype(BF16)
     active = gelu_parts(nn(normed2, weights.w_up[...]))[0].astype(BF16)
-    return middle + nn(active, weights.w_down[...]), picked
-
-
-def layer_back(stream_grad, normed, weights, mask, spread, dense, gated, kept, sums, out, between=None):
+    return middle + nn(active, weights.w_down[...])
+
+
+def layer_back(stream_grad, normed, weights, mask, spread, dense, gated, kept, sums, out, between=None, result=None):
     between = between or (lambda *place: None)
     count, width = normed.shape
     hidden = weights.w_up.shape[1]
@@ -184,7 +202,9 @@
     hat2, scale2 = norm_parts(kept.middle[...])
     normed2 = (hat2 * weights.gain2[...] + weights.bias2[...]).astype(BF16)
     normed2_t = normed2.astype(F32).T.astype(BF16)
-    sums.wide[...] = jnp.zeros(sums.wide.shape, F32)
+    sums.total[...] = jnp.zeros(sums.total.shape, F32)
+    if result is not None:
+        result[...] = jnp.zeros(result.shape, F32)
 
     blocks = out.up.shape[0]
     piece = hidden // blocks
@@ -193,26 +213,29 @@
     def part(c, carry):
         cols = pl.ds(pl.multiple_of(c * piece, piece), piece)
         active, slope = gelu_parts(nn(normed2, weights.w_up[:, cols]))
+        if result is not None:
+            result[...] += nn(active.astype(BF16), weights.w_down[cols, :])
         out.down[c, 0:piece, :] = nn(active.T.astype(BF16), branch).astype(BF16)
         upper_grad = (nt(branch, weights.w_down[cols, :]) * slope).astype(BF16)
         out.up[c, 0:width, :] = nn(normed2_t, upper_grad).astype(BF16)
-        sums.wide[...] += nt(upper_grad, weights.w_up[:, cols])
+        sums.total[...] += nt(upper_grad, weights.w_up[:, cols])
+        between("part", c)
         return carry
 
     lax.fori_loop(0, blocks, part, 0)
     between("hidden")
-    back, gain2_grad, bias2_grad = norm_back(hat2, scale2, weights.gain2[...], sums.wide[...])
+    back, gain2_grad, bias2_grad = norm_back(hat2, scale2, weights.gain2[...], sums.total[...])
     out.small[2:3, :] = gain2_grad
     out.small[3:4, :] = bias2_grad
     middle_grad = stream_grad + back
     out.middle_grad[...] = middle_grad
     rounded = middle_grad.astype(BF16)
-    between("out")
     gated_t = kept.gated[...].astype(F32).T.astype(BF16)
     for block in range(blocks):
         rows = slice(block * own, (block + 1) * own)
         out.w_out[block, 0:own, :] = nn(gated_t[rows], rounded).astype(BF16)
     dense[...] = nt(rounded, weights.w_out[...])
+    between("out")
     gated[...] = jnp.zeros(gated.shape, F32)
     keys, values = split_keyval(kept.keyval[...])
     keys_t = keys.T.astype(BF16)
@@ -223,27 +246,35 @@
     sums.gates[...] = jnp.zeros(sums.gates.shape, F32)
     lanes = iota(sums.gates.shape, 1)
 
-    def slot(k, carry):
-        which = spread[k]
-        chosen = which - lane_half((count, LANES))
-        grad = select_tiles(dense, chosen)
-        gate = gate_column(kept.gates[...], which)
-        gate_grad = jnp.sum(grad * kept.attended[k].astype(F32), axis=1, keepdims=True)
-        sums.gates[...] += jnp.where(which[:, : lanes.shape[1]] == lanes, gate * gate_grad, 0.0)
-        att_grad = (gate * grad).astype(BF16)
-        query = kept.query[k]
-        shares = jnp.exp(nt(keys, query) + mask[...] - kept.lse[k, 0:1, :])
-        sums.values[...] += nn(shares.astype(BF16), att_grad)
-        share_grad = nt(values, att_grad)
-        score_grad = shares * (share_grad - jnp.sum(share_grad * shares, axis=0, keepdims=True))
-        score_grad = score_grad.astype(BF16)
-        sums.keys[...] += nn(score_grad, query)
-        query_grad = nn(keys_t, score_grad).T * 0.125
-        place_tiles(gated, chosen, query_grad.astype(BF16).astype(F32))
-        between("slot", k)
+    def pair(step, carry):
+        slots = [2 * step, 2 * step + 1]
+        which = [spread[k] for k in slots]
+        chosen = [w - lane_half((count, LANES)) for w in which]
+        grads = [select_tiles(dense, c) for c in chosen]
+        weighted, att_grads = [], []
+        for k, w, grad in zip(slots, which, grads):
+            gate = gate_column(kept.gates[...], w)
+            gate_grad = jnp.sum(grad * kept.attended[k].astype(F32), axis=1, keepdims=True)
+            weighted.append(jnp.where(w[:, : lanes.shape[1]] == lanes, gate * gate_grad, 0.0))
+            att_grads.append((gate * grad).astype(BF16))
+        sums.gates[...] += weighted[0] + weighted[1]
+        queries = [kept.query[k] for k in slots]
+        scores = [nt(keys, query) + mask[...] for query in queries]
+        shares = [jnp.exp(score - kept.lse[k, 0:1, :]) for k, score in zip(slots, scores)]
+        share_grads = [nt(values, grad) for grad in att_grads]
+        sums.values[...] += nn(shares[0].astype(BF16), att_grads[0]) + nn(shares[1].astype(BF16), att_grads[1])
+        score_grads = [
+            (share * (grad - jnp.sum(grad * share, axis=0, keepdims=True))).astype(BF16)
+            for share, grad in zip(shares, share_grads)
+        ]
+        sums.keys[...] += nn(score_grads[0], queries[0]) + nn(score_grads[1], queries[1])
+        for c, score_grad in zip(chosen, score_grads):
+            query_grad = nn(keys_t, score_grad).T * 0.125
+            place_tiles(gated, c, query_grad.astype(BF16).astype(F32))
+        between("slot", step)
         return carry
 
-    lax.fori_loop(0, kept.query.shape[0], slot, 0)
+    lax.fori_loop(0, kept.query.shape[0] // 2, pair, 0)
     both_keys = sums.keys[...] + pltpu.roll(sums.keys[...], LANES // 2, 1)
     both_values = sums.values[...] + pltpu.roll(sums.values[...], LANES // 2, 1)
     first = iota(both_keys.shape, 1) < LANES // 2
@@ -302,7 +333,7 @@
 
 WEIGHTS = ("gain1", "bias1", "w_kv", "w_router", "w_query", "w_out", "gain2", "bias2", "w_up", "w_down")
 KEPT = ("keyval", "gates", "query", "lse", "attended", "gated", "middle")
-SUMS = ("wide", "keys", "values", "gates")
+SUMS = ("total", "keys", "values", "gates")
 OUT = ("up", "down", "w_out", "w_query", "router", "keyval", "small", "middle_grad", "normed_grad")
 LATER = ("x", "normed", "received", "gain1", "w_kv", "middle_grad", "normed_grad", "small")
 
@@ -320,9 +351,10 @@
     mask, spread, dense, gated = refs
     fill_mask(lengths, keep, mask)
     spread_routes(routes, spread)
-    result, picked = layer_forward(
+    middle, picked = layer_forward(
         x[...].astype(F32), normed, weights, mask, spread, dense, gated, kept
     )
+    result = feed_forward(middle, weights)
     small[...] = jnp.zeros(small.shape, F32)
     count_chosen(picked, keep, small)
     stream[...] = result
@@ -340,8 +372,8 @@
     mask, spread, dense, gated = refs
     fill_mask(lengths, keep, mask)
     spread_routes(routes, spread)
-    result, picked = layer_forward(x[...], normed, weights, mask, spread, dense, gated, kept)
-    activations[...] = result.astype(BF16)
+    middle, picked = layer_forward(x[...], normed, weights, mask, spread, dense, gated, kept)
+    activations[...] = feed_forward(middle, weights).astype(BF16)
     count = x.shape[0]
     kept_col = jnp.broadcast_to(own_columns(keep, count).astype(F32), (LANES, count)).T
     kept_col = jnp.concatenate([kept_col] * (x.shape[1] // LANES), axis=1)
@@ -380,13 +412,13 @@
 
 
 def share_kernel(n, scatter, mine, everyones, send_sem, recv_sem):
-    me = lax.axis_index("exp")
+    me = lax.axis_index(EXP)
     rows = everyones.shape[1]
     barrier = pltpu.get_barrier_semaphore()
     others = [lax.rem(me + step, n) for step in range(1, n)]
     for other in others:
         pl.semaphore_signal(
-            barrier, inc=1, device_id={"exp": other}, device_id_type=pl.DeviceIdType.MESH
+            barrier, inc=1, device_id={EXP: other}, device_id_type=pl.DeviceIdType.MESH
         )
 
     def part(owner):
@@ -400,7 +432,7 @@
             dst_ref=everyones.at[me],
             send_sem=send_sem.at[step],
             recv_sem=recv_sem.at[step],
-            device_id={"exp": other},
+            device_id={EXP: other},
             device_id_type=pl.DeviceIdType.MESH,
         )
         copy.start()
@@ -418,14 +450,16 @@
     chips = lax.axis_size("dp") // 2
     across = math.isqrt(chips)
     across = across if across * across == chips else chips
-    return {"c": 2, "x": across, "y": chips // across, "z": lax.axis_size("exp")}
+    n = lax.axis_size(EXP)
+    return {"c": 2, "x": across, "y": chips // across, "z": n, "l": 2, "h": n // 2}
 
 
 def place_of():
     size = axis_sizes()
     d = lax.axis_index("dp")
-    at = {"c": lax.rem(d, 2), "x": lax.rem(d // 2, size["x"]), "y": d // (2 * size["x"]), "z": lax.axis_index("exp")}
-    return at, size
+    z = lax.axis_index(EXP)
+    at = {"c": lax.rem(d, 2), "x": lax.rem(d // 2, size["x"]), "y": d // (2 * size["x"])}
+    return {**at, "z": z, "l": lax.rem(z, 2), "h": z // 2}, size
 
 
 def peers_of(axis, at, size):
@@ -433,7 +467,9 @@
     for step in range(1, size[axis]):
         where = dict(at)
         where[axis] = lax.rem(at[axis] + step, size[axis])
-        out.append((where[axis], {"exp": where["z"], "dp": (where["y"] * size["x"] + where["x"]) * 2 + where["c"]}))
+        if axis in "lh":
+            where["z"] = where["h"] * 2 + where["l"]
+        out.append((where[axis], {EXP: where["z"], "dp": (where["y"] * size["x"] + where["x"]) * 2 + where["c"]}))
     return out
 
 
@@ -457,8 +493,8 @@
         z, rows = blocks, self.rows
         got = []
         for axis in self.order:
-            if axis == "z":
-                z = 1
+            if axis in "zlh":
+                z = z // size[axis]
             else:
                 rows = rows // size[axis]
             got.append((size[axis] - 1, z, rows, width))
@@ -468,7 +504,8 @@
 class Sums:
     def __init__(self, chunks, sources, results, scratch, sems):
         self.chunks, self.sources, self.results = chunks, sources, results
-        self.down_send, self.down_recv, self.up_send, self.up_recv, self.own_sem = sems
+        self.send_sem, self.recv_sem, self.own_sem = sems
+        self.first_down, self.first_up, _ = arrivals(chunks, axis_sizes())
         self.at, self.size = place_of()
         self.own, self.base, self.got = [], [], []
         scratch = list(scratch)
@@ -486,8 +523,8 @@
         chunk = self.chunks[i]
         first, rows, z = 0, chunk.rows, None
         for k, axis in enumerate(chunk.order[:stages]):
-            if axis == "z":
-                z = self.at["z"]
+            if axis in "zlh":
+                z = axis if axis == "l" else self.at["z"]
             else:
                 rows = rows // self.size[axis]
                 if k > 0:
@@ -509,22 +546,29 @@
         chunk, axis = self.chunks[i], self.chunks[i].order[s]
         copies = []
         z, first, rows = self.region(i, s)
-        part = rows if axis == "z" else rows // self.size[axis]
+        part = rows if axis in "zlh" else rows // self.size[axis]
+        number = 0
         for step, (place, device) in enumerate(peers_of(axis, self.at, self.size)):
+            start = self.base[i] + first
+            blocks, into = [slice(None) if z is None else pl.ds(z, 1)], [self.got[i][s].at[step]]
             if s == 0:
                 start = chunk.first + place * part
-                source = self.sources[chunk.array].at[:, pl.ds(pl.multiple_of(start, 16), part), :]
             elif axis == "z":
-                start = self.base[i] + first
-                source = self.own[i].at[pl.ds(place, 1), pl.ds(pl.multiple_of(start, 16), part), :]
+                blocks = [pl.ds(place, 1)]
+            elif axis == "h":
+                blocks = [pl.ds(place * 2 + self.at["l"], 1)]
+            elif axis == "l":
+                halves = range(self.size["h"])
+                blocks = [pl.ds(2 * half + place, 1) for half in halves]
+                into = [self.got[i][s].at[step, pl.ds(half, 1)] for half in halves]
             else:
-                start = pl.multiple_of(self.base[i] + first + place * part, 16)
-                blocks = slice(None) if z is None else pl.ds(z, 1)
-                source = self.own[i].at[blocks, pl.ds(start, part), :]
-            index = (i, s, step)
-            copies.append(
-                self.copy_to(source, self.got[i][s].at[step], self.down_send.at[index], self.down_recv.at[index], device)
-            )
+                start = start + place * part
+            source = self.sources[chunk.array] if s == 0 else self.own[i]
+            for block, there in zip(blocks, into):
+                piece = source.at[block, pl.ds(pl.multiple_of(start, 16), part), :]
+                recv = self.recv_sem.at[self.first_down[i][s] + number]
+                copies.append(self.copy_to(piece, there, self.send_sem.at[i, number], recv, device))
+                number += 1
         if s == 0 and not chunk.held_here:
             start = pl.multiple_of(chunk.first + self.at[axis] * part, 16)
             load = pltpu.make_async_copy(
@@ -546,7 +590,7 @@
             block, row = t // (rows // piece), lax.rem(t, rows // piece) * piece
             where = pl.ds(pl.multiple_of(self.base[i] + first + row, 16), piece)
             arrived = pl.ds(pl.multiple_of(row, 16), piece)
-            held = block if z is None else z
+            held = block if z is None else 2 * block + self.at["l"] if axis == "l" else z
             total = own[held, where, :].astype(F32)
             for step in range(self.size[axis] - 1):
                 total = total + got[step, block, arrived, :].astype(F32)
@@ -555,55 +599,64 @@
 
         lax.fori_loop(0, blocks * (rows // piece), one, 0)
 
-    def target(self, i, stages):
+    def targets(self, i, stages):
         chunk = self.chunks[i]
         z, first, rows = self.region(i, stages)
         start = chunk.first + self.at[chunk.order[0]] * (chunk.rows // self.size[chunk.order[0]]) + first
         where = pl.ds(pl.multiple_of(start, 16), rows)
         result = self.results[chunk.result].at[chunk.layer]
-        if chunk.kind == "own":
-            return result.at[where, :]
-        if chunk.kind == "stack":
-            return result.at[:, where, :] if z is None else result.at[z, where, :]
         width = self.own[i].shape[2]
-        return result.at[where, :] if z is None else result.at[where, pl.ds(pl.multiple_of(z * width, width), width)]
+        if chunk.kind == OWN:
+            return [result.at[where, :]]
+        if z is None:
+            return [result.at[where, :] if chunk.kind == WIDE else result.at[:, where, :]]
+        blocks = [2 * half + self.at["l"] for half in range(self.size["h"])] if isinstance(z, str) else [z]
+        if chunk.kind == STACK:
+            return [result.at[block, where, :] for block in blocks]
+        return [result.at[where, pl.ds(pl.multiple_of(block * width, width), width)] for block in blocks]
 
     def send_up(self, i, s):
         for copy in self.up_copies(i, s):
             copy.start()
 
+    def ups(self, i):
+        chunk = self.chunks[i]
+        return [s for s in reversed(range(len(chunk.order))) if chunk.kind != OWN or chunk.order[s] not in "zlh"]
+
     def up_copies(self, i, s):
         chunk, axis = self.chunks[i], self.chunks[i].order[s]
-        target = self.target(i, s + 1)
+        targets = self.targets(i, s + 1)
         copies = []
-        source = target
-        if s == len(chunk.order) - 1:
-            z, first, rows = self.region(i, s + 1)
+        sources = targets
+        if s == self.ups(i)[0]:
+            z, first, rows = self.region(i, len(chunk.order))
             where = pl.ds(pl.multiple_of(self.base[i] + first, 16), rows)
-            source = self.own[i].at[z, where, :]
-            copies.append(pltpu.make_async_copy(source, target, self.own_sem.at[i]))
-        if axis != "z" or chunk.kind != "own":
-            for step, (_, device) in enumerate(peers_of(axis, self.at, self.size)):
-                index = (i, s, step)
-                copies.append(self.copy_to(source, target, self.up_send.at[index], self.up_recv.at[index], device))
+            sources = [self.own[i].at[z, where, :]]
+            copies.append(pltpu.make_async_copy(sources[0], targets[0], self.own_sem.at[i]))
+        number = 0
+        for _, device in peers_of(axis, self.at, self.size):
+            for source, target in zip(sources, targets):
+                recv = self.recv_sem.at[self.first_up[i][s] + number]
+                copies.append(self.copy_to(source, target, self.send_sem.at[i, number], recv, device))
+                number += 1
         return copies
 
     def stages(self, i):
-        return 2 * len(self.chunks[i].order)
+        return len(self.chunks[i].order) + len(self.ups(i))
 
     def advance(self, i, stage):
-        depth = len(self.chunks[i].order)
+        depth, ups = len(self.chunks[i].order), self.ups(i)
         if stage < depth:
             self.add_up(i, stage)
             if stage + 1 < depth:
                 self.send_down(i, stage + 1)
             else:
-                self.send_up(i, depth - 1)
+                self.send_up(i, ups[0])
         else:
-            for copy in self.up_copies(i, 2 * depth - 1 - stage):
+            for copy in self.up_copies(i, ups[stage - depth]):
                 copy.wait()
-            if stage + 1 < 2 * depth:
-                self.send_up(i, 2 * depth - 2 - stage)
+            if stage - depth + 1 < len(ups):
+                self.send_up(i, ups[stage - depth + 1])
 
 
 class SmallSum:
@@ -612,12 +665,12 @@
         self.at, self.size = place_of()
 
     def start(self, s):
-        axis = "cxyz"[s]
+        axis = CXYZ[s]
         source = self.array if s == 0 else self.result
         self.copies = []
         for step, (_, device) in enumerate(peers_of(axis, self.at, self.size)):
             copy = pltpu.make_async_remote_copy(
-                src_ref=source, dst_ref=self.got[s].at[self.at[axis]], send_sem=self.send.at[s, step],
+                src_ref=source, dst_ref=self.got[s].at[self.at[axis]], send_sem=self.send.at[step],
                 recv_sem=self.recv.at[s, step], device_id=device, device_id_type=pl.DeviceIdType.MESH,
             )
             copy.start()
@@ -628,11 +681,27 @@
         for copy in self.copies:
             copy.wait()
         total = self.got[s][0]
-        for j in range(1, self.size["cxyz"[s]]):
+        for j in range(1, self.size[CXYZ[s]]):
             total = total + self.got[s][j]
         self.result[...] = total
         if s < 3:
             self.start(s + 1)
+
+
+def arrivals(chunks, size):
+    down, up, total = [], [], 0
+    for chunk in chunks:
+        for firsts in (down, up):
+            firsts.append([])
+            for axis in chunk.order:
+                firsts[-1].append(total)
+                if firsts is down or chunk.kind != OWN or axis not in "zlh":
+                    total += arriving(axis, size)
+    return down, up, total
+
+
+def arriving(axis, size):
+    return (size[axis] - 1) * (size["h"] if axis == "l" else 1)
 
 
 def sum_scratch(chunks, shapes, size):
@@ -640,15 +709,15 @@
     for chunk in chunks:
         blocks, _, width = shapes[chunk.array]
         scratch += [pltpu.VMEM(shape, BF16) for shape in chunk.shapes(blocks, width, size)]
-    most = max(size.values()) - 1
-    sems = pltpu.SemaphoreType.DMA((len(chunks), 4, most))
-    return scratch, [sems] * 4 + [pltpu.SemaphoreType.DMA((len(chunks),))]
+    most = max(arriving(axis, size) for chunk in chunks for axis in chunk.order)
+    sems = [(len(chunks), most), (arrivals(chunks, size)[2],), (len(chunks),)]
+    return scratch, [pltpu.SemaphoreType.DMA(shape) for shape in sems]
 
 
 def small_scratch(shape, size):
     most = max(size.values()) - 1
-    sems = pltpu.SemaphoreType.DMA((4, most))
-    return [pltpu.VMEM((size[axis],) + shape, F32) for axis in "cxyz"] + [sems] * 2
+    sems = [pltpu.SemaphoreType.DMA((most,)), pltpu.SemaphoreType.DMA((4, most))]
+    return [pltpu.VMEM((size[axis],) + shape, F32) for axis in CXYZ] + sems
 
 
 def reduce_kernel(chunks, starts, counts, *refs):
@@ -656,10 +725,10 @@
     small_in, refs = refs[0], refs[1:]
     results, refs = refs[: counts[1]], refs[counts[1] :]
     small_out, refs = refs[0], refs[1:]
-    scratch, sems, refs = refs[: counts[2]], refs[counts[2] : counts[2] + 5], refs[counts[2] + 5 :]
+    scratch, sems, refs = refs[: counts[2]], refs[counts[2] : counts[2] + 3], refs[counts[2] + 3 :]
     small = SmallSum(small_in, small_out, refs[:4], refs[4], refs[5])
     sums = Sums(chunks, sources, results, scratch, sems)
-    greet("cxyz", sums.at, sums.size)
+    greet(CXYZ, sums.at, sums.size)
     ahead = AHEAD
     for i, start in enumerate(starts):
         if start < ahead:
@@ -707,11 +776,11 @@
                     chunks.append(Chunk(array, cut[k][0], cut[k][1], order, kind, result, layer, False))
                     starts.append(start)
 
-    add([(0, "wide", 0, 1, "cxyz"), (1, "stack", 1, 1, "cyxz")], (up_rows, down_rows))
-    add([(4, "wide", 0, 0, "cxyz"), (5, "stack", 1, 0, "cyxz")], (up_rows, down_rows))
-    add([(2, "own", 2, 1, "cxyz"), (3, "own", 3, 1, "cyxz")], (own_rows, own_rows))
-    add([(6, "own", 2, 0, "cxyz"), (7, "own", 3, 0, "cyxz")], (own_rows, own_rows))
-    chunks.append(Chunk(8, 0, tail_rows, "cxyz", "stack", 4, 0, False))
+    add([(0, WIDE, 0, 1, CXYZ), (1, STACK, 1, 1, CYXZ)], (up_rows, down_rows))
+    add([(4, WIDE, 0, 0, CXYZ), (5, STACK, 1, 0, CYXZ)], (up_rows, down_rows))
+    add([(2, OWN, 2, 1, CXYZ), (3, OWN, 3, 1, CYXZ)], (own_rows, own_rows))
+    add([(6, OWN, 2, 0, CXYZ), (7, OWN, 3, 0, CYXZ)], (own_rows, own_rows))
+    chunks.append(Chunk(8, 0, tail_rows, CXYZ, STACK, 4, 0, False))
     starts.append(0)
     return chunks, starts
 
@@ -729,85 +798,8 @@
         compiler_params=pltpu.CompilerParams(
             collective_id=collective_id, has_side_effects=True, vmem_limit_bytes=VMEM_LIMIT
         ),
-        name="sum_gradients",
+        name="sums",
     )(*arrays, small)
-
-
-def gather_kernel(orders, *refs):
-    count = len(orders)
-    mine, results, sems = refs[:2], refs[2 : 2 + count], refs[2 + count :]
-    mine = [mine[i % 2].at[i // 2] for i in range(count)]
-    send_sem, recv_sem, own_sem = sems
-    at, size = place_of()
-    greet("cxyz", at, size)
-    waiting = {}
-
-    def region(i, s):
-        first, rows = 0, mine[i].shape[0]
-        for axis in reversed(orders[i][s:]):
-            rows = rows // size[axis]
-            first = first + at[axis] * rows
-        return pl.ds(pl.multiple_of(first, rows), rows)
-
-    def send(i, s):
-        axis = orders[i][s]
-        copies = []
-        if s == 0:
-            where = region(i, 1)
-            own = pltpu.make_async_copy(mine[i], results[i].at[at["z"]], own_sem.at[i])
-            own.start()
-            copies.append(own)
-        else:
-            where = region(i, s)
-        for step, (_, device) in enumerate(peers_of(axis, at, size)):
-            for other in range(1 if s == 0 else size["z"] - 1):
-                block = at["z"] if s == 0 else lax.rem(at["z"] + 1 + other, size["z"])
-                source = mine[i].at[where, :] if s == 0 else results[i].at[block, where, :]
-                copy = pltpu.make_async_remote_copy(
-                    src_ref=source,
-                    dst_ref=results[i].at[block, where, :],
-                    send_sem=send_sem.at[i, s, step, other],
-                    recv_sem=recv_sem.at[i, s, step, other],
-                    device_id=device,
-                    device_id_type=pl.DeviceIdType.MESH,
-                )
-                copy.start()
-                copies.append(copy)
-        waiting[i] = copies
-
-    for t in range(count // 2 + max(len(order) for order in orders)):
-        for i in range(count):
-            stage = t - i // 2
-            if 0 <= stage <= len(orders[i]):
-                if stage > 0:
-                    for copy in waiting[i]:
-                        copy.wait()
-                if stage < len(orders[i]):
-                    send(i, stage)
-
-
-def gather_all(arrays, sizes, collective_id):
-    layers, rows, width = arrays[0].shape
-    n = sizes["z"]
-    orders = []
-    for i in range(2 * layers):
-        left, axes = rows // 16, ""
-        for axis in "cxy" if i % 2 else "cyx":
-            if left % sizes[axis] == 0:
-                left, axes = left // sizes[axis], axis + axes
-        orders.append("z" + axes)
-    anywhere = pl.BlockSpec(memory_space=pl.ANY)
-    most = max(sizes.values()) - 1
-    sems = pltpu.SemaphoreType.DMA((len(orders), 4, most, n - 1))
-    return pl.pallas_call(
-        partial(gather_kernel, orders),
-        out_shape=[jax.ShapeDtypeStruct((n, rows, width), BF16) for _ in orders],
-        in_specs=[vmem()] * 2,
-        out_specs=[vmem()] * len(orders),
-        scratch_shapes=[sems, sems, pltpu.SemaphoreType.DMA((len(orders),))],
-        compiler_params=pltpu.CompilerParams(collective_id=collective_id, has_side_effects=True),
-        name="gather_experts",
-    )(*arrays)
 
 
 def layer_spec(array, layer):
@@ -856,197 +848,109 @@
         return total.astype(BF16)
 
 
-def finish_chunks(n, up_rows, down_rows, own_rows, tail_rows):
-    groups = [
-        [Chunk(0, 0, up_rows, "cxyz", "wide", 0, 1, False), Chunk(1, 0, down_rows, "cyxz", "stack", 1, 1, False)],
-        [Chunk(2, 0, own_rows, "cxyz", "own", 2, 1, False), Chunk(3, 0, own_rows, "cyxz", "own", 3, 1, False)],
-        [Chunk(4, 0, up_rows, "cxyz", "wide", 0, 0, True), Chunk(5, 0, down_rows, "cyxz", "stack", 1, 0, True)],
-        [Chunk(6, 0, own_rows, "cxyz", "own", 2, 0, True), Chunk(7, 0, own_rows, "cyxz", "own", 3, 0, True)],
-        [Chunk(8, 0, tail_rows, "cxyz", "stack", 4, 0, True)],
-    ]
-    chunks, numbers = [], []
-    for group in groups:
-        numbers.append(list(range(len(chunks), len(chunks) + len(group))))
-        chunks += group
-    return chunks, numbers
-
-
-def finish_kernel(chunks, groups, counts, *refs):
-    weights, refs = weights_of(0, refs)
-    later, refs = named(LATER[:2] + ("part",) + LATER[3:] + ("router",), refs)
-    (x, normed, routes, lengths, keep, small), refs = refs[:6], refs[6:]
-    kept, refs = named(KEPT, refs)
-    last_grads, refs = refs[:4], refs[4:]
-    input_grad, refs = refs[0], refs[1:]
-    results, refs = refs[:5], refs[5:]
-    small_out, refs = refs[0], refs[1:]
-    out, refs = named(OUT, refs)
-    sums, refs = named(SUMS, refs)
-    (mask, spread, dense, gated), refs = refs[:4], refs[4:]
-    (tail, small_in, got1, got0), refs = refs[:4], refs[4:]
-    scratch, refs = refs[:counts], refs[counts:]
-    small_got, refs = refs[:4], refs[4:]
-    sems, small_sems, (send1, recv1, send0, recv0) = refs[:5], refs[5:7], refs[7:]
-    sources = list(last_grads) + [out.up, out.down, out.w_query, out.w_out, tail]
-    total = Sums(chunks, sources, results, scratch, sems)
-    little = SmallSum(small_in, small_out, small_got, *small_sems)
-    keyval1 = KeyvalSum(later.part, got1, send1, recv1)
-    keyval0 = KeyvalSum(out.keyval, got0, send0, recv0)
-    done = [0] * len(groups)
-
-    def begin(group):
-        for i in groups[group]:
-            total.send_down(i, 0)
-
-    def advance(group):
-        if done[group] < total.stages(groups[group][0]):
-            for i in groups[group]:
-                total.advance(i, done[group])
-            done[group] += 1
-
-    greet("cxyz", total.at, total.size)
-    keyval1.start()
-    begin(0)
-    begin(1)
-    fill_mask(lengths, keep, mask)
-    spread_routes(routes, spread)
-    tail[...] = jnp.zeros(tail.shape, BF16)
-    rows = small.shape[0]
-    experts = weights.w_router.shape[0]
-    small_in[0:rows, :] = small[...]
-    small_in[rows : 2 * rows, :] = later.small[...]
-    small0, small1 = small_in.at[0:rows, :], small_in.at[rows : 2 * rows, :]
-    out.small = small0
-    tail[3, 0:experts, :] = later.router[...].astype(BF16)
-    advance(0)
-    stream_grad = layer_finish(
-        later.x[...], later.normed, keyval1.total(), later.gain1[1:2, :], later.w_kv[...],
-        later.middle_grad, later.normed_grad, tail.at[2, 0 : later.w_kv.shape[1]], small1,
-    )
-
-    def between(place, k=None):
-        if place == "hidden":
-            begin(2)
-            advance(0)
-            advance(1)
-        elif place == "slot":
-
-            @pl.when(k == 2)
-            def _():
-                advance(0)
-
-            @pl.when(k == 5)
-            def _():
-                advance(1)
-                advance(2)
-
-        elif place == "keyval":
-            keyval0.start()
-            advance(0)
-
-    layer_back(stream_grad, normed, weights, mask, spread, dense, gated, kept, sums, out, between)
-    tail[1, 0:experts, :] = out.router[...].astype(BF16)
-    begin(3)
-    advance(1)
-    input_grad[...] = layer_finish(
-        x[...].astype(F32), normed, keyval0.total(), weights.gain1[...], weights.w_kv[...],
-        out.middle_grad, out.normed_grad, tail.at[0, 0 : weights.w_kv.shape[1]], small0,
-    )
-    begin(4)
-    little.start(0)
-    for step in range(2 * len(chunks[-1].order)):
-        for group in range(len(groups)):
-            advance(group)
-        if step < 4:
-            little.advance(step)
-
-
-def finish_all(args, last_grads, out_shapes, work, result_shapes, sizes):
-    specs, arrays = specs_of(args)
-    n, up_rows, _ = last_grads[0].shape
-    tail_shape = result_shapes[4][1:]
-    chunks, groups = finish_chunks(n, up_rows, last_grads[1].shape[1], last_grads[2].shape[1], tail_shape[1])
-    shapes = [array.shape for array in last_grads] * 2 + [tail_shape]
-    scratch, sems = sum_scratch(chunks, shapes, sizes)
-    count, width = out_shapes[-1][0]
-    small_shape = (2 * out_shapes[6][0][0], width)
-    group, pair = out_shapes[5][0]
-    got = pltpu.VMEM((n - 1, group // n, pair), BF16)
-    anywhere = pl.BlockSpec(memory_space=pl.ANY)
-    return pl.pallas_call(
-        partial(finish_kernel, chunks, groups, len(scratch)),
-        out_shape=[jax.ShapeDtypeStruct((count, width), F32)]
-        + [jax.ShapeDtypeStruct(shape, BF16) for shape in result_shapes]
-        + [jax.ShapeDtypeStruct(small_shape, F32)],
-        grid=(1,),
-        in_specs=specs + [anywhere] * len(last_grads),
-        out_specs=[vmem()] + [anywhere] * len(result_shapes) + [vmem()],
-        scratch_shapes=[pltpu.VMEM(shape, dtype) for shape, dtype in out_shapes + work]
-        + [pltpu.VMEM(tail_shape, BF16), pltpu.VMEM(small_shape, F32), got, got]
-        + scratch + small_scratch(small_shape, sizes)[:4] + sems + small_scratch(small_shape, sizes)[4:]
-        + [pltpu.SemaphoreType.DMA((n - 1,))] * 4,
-        compiler_params=pltpu.CompilerParams(
-            collective_id=4, has_side_effects=True, vmem_limit_bytes=62 << 20
-        ),
-        name="first_block_back_and_sums",
-    )(*arrays, *last_grads)
+class Part:
+    def __init__(self, array, layer, first, rows, order):
+        self.array, self.layer, self.first, self.rows, self.order = array, layer, first, rows, order
 
 
 class Gather:
-    def __init__(self, sources, targets, orders, send, recv, own_sem):
-        self.sources, self.targets, self.orders = sources, targets, orders
+    def __init__(self, parts, sources, targets, send, recv, own_sem):
+        self.parts, self.sources, self.targets = parts, sources, targets
         self.send, self.recv, self.own_sem = send, recv, own_sem
         self.at, self.size = place_of()
-        self.stage = [0] * len(sources)
+        self.firsts = gather_arrivals(parts, axis_sizes())[0]
+        self.stage = [-1] * len(parts)
 
     def copies(self, i, s):
-        rows, order = self.sources[i].shape[0], self.orders[i]
-        first, part = 0, rows
-        for axis in reversed(order[max(s, 1) :]):
-            part = part // self.size[axis]
-            first = first + self.at[axis] * part
+        part = self.parts[i]
+        source, target = self.sources[part.array].at[part.layer], self.targets[2 * part.layer + part.array]
+        all_rows, rows, first = source.shape[0], part.rows, part.first
+        for axis in reversed(part.order[max(s, 1) :]):
+            rows = rows // self.size[axis]
+            first = first + self.at[axis] * rows
         here = self.at["z"]
         out = []
         if s == 0:
-            place = pl.ds(pl.multiple_of(here * rows, rows), rows)
-            out.append(pltpu.make_async_copy(self.sources[i], self.targets[i].at[place, :], self.own_sem.at[i]))
-        for step, (_, device) in enumerate(peers_of(order[s], self.at, self.size)):
+            start = pl.multiple_of(here * all_rows + part.first, 16)
+            out.append(
+                pltpu.make_async_copy(
+                    source.at[pl.ds(part.first, part.rows), :], target.at[pl.ds(start, part.rows), :], self.own_sem.at[i]
+                )
+            )
+        number = 0
+        for _, device in peers_of(part.order[s], self.at, self.size):
             for other in range(1 if s == 0 else self.size["z"] - 1):
                 block = here if s == 0 else lax.rem(here + 1 + other, self.size["z"])
-                target = self.targets[i].at[pl.ds(pl.multiple_of(block * rows + first, part), part), :]
-                source = self.sources[i].at[pl.ds(pl.multiple_of(first, part), part), :] if s == 0 else target
-                index = (i, s, step, other)
+                into = target.at[pl.ds(pl.multiple_of(block * all_rows + first, 16), rows), :]
                 out.append(
                     pltpu.make_async_remote_copy(
-                        src_ref=source, dst_ref=target, send_sem=self.send.at[index], recv_sem=self.recv.at[index],
-                        device_id=device, device_id_type=pl.DeviceIdType.MESH,
+                        src_ref=source.at[pl.ds(pl.multiple_of(first, 16), rows), :] if s == 0 else into,
+                        dst_ref=into, send_sem=self.send.at[i, number],
+                        recv_sem=self.recv.at[self.firsts[i][s] + number], device_id=device,
+                        device_id_type=pl.DeviceIdType.MESH,
                     )
                 )
+                number += 1
         return out
 
-    def begin(self, i):
-        for copy in self.copies(i, 0):
-            copy.start()
-
-    def advance(self, i):
+    def move(self, i):
         s = self.stage[i]
-        for copy in self.copies(i, s):
-            copy.wait()
+        if s >= 0:
+            for copy in self.copies(i, s):
+                copy.wait()
         self.stage[i] = s + 1
-        if s + 1 < len(self.orders[i]):
+        if s + 1 < len(self.parts[i].order):
             for copy in self.copies(i, s + 1):
                 copy.start()
 
 
-def share_orders(rows, count, size):
-    orders = []
-    for i in range(count):
-        left, axes = rows // 16, ""
-        for axis in "cxy" if i % 2 else "cyx":
-            if left % size[axis] == 0:
-                left, axes = left // size[axis], axis + axes
-        orders.append("z" + axes)
-    return orders
+def gather_arrivals(parts, size):
+    firsts, total, most = [], 0, 0
+    for part in parts:
+        firsts.append([])
+        for axis in part.order:
+            number = (size[axis] - 1) * (1 if axis == "z" else size["z"] - 1)
+            firsts[-1].append(total)
+            total += number
+            most = max(most, number)
+    return firsts, total, most
+
+
+def gather_sems(parts, size):
+    _, total, most = gather_arrivals(parts, size)
+    return [pltpu.SemaphoreType.DMA(shape) for shape in ((len(parts), most), (total,), (len(parts),))]
+
+
+def gather_kernel(parts, *refs):
+    gather = Gather(parts, refs[:2], refs[2:-3], *refs[-3:])
+    greet(CXYZ, gather.at, gather.size)
+    for _ in range(1 + max(len(part.order) for part in parts)):
+        for i, part in enumerate(parts):
+            if gather.stage[i] < len(part.order):
+                gather.move(i)
+
+
+def gather_all(arrays, sizes, collective_id):
+    layers, rows, width = arrays[0].shape
+    parts = []
+    for layer in range(layers):
+        for array in range(2):
+            left, axes = rows // 16, ""
+            for axis in "cyx":
+                if left % sizes[axis] == 0:
+                    left, axes = left // sizes[axis], axis + axes
+            parts.append(Part(array, layer, 0, rows, "z" + axes))
+    return pl.pallas_call(
+        partial(gather_kernel, parts),
+        out_shape=[jax.ShapeDtypeStruct((sizes["z"] * rows, width), BF16) for _ in parts],
+        in_specs=[pl.BlockSpec(memory_space=pl.ANY)] * 2,
+        out_specs=[vmem()] * len(parts),
+        scratch_shapes=gather_sems(parts, sizes),
+        compiler_params=pltpu.CompilerParams(
+            collective_id=collective_id, has_side_effects=True, vmem_limit_bytes=VMEM_LIMIT
+        ),
+        name="gather",
+    )(*arrays)
 
 
 class KeyvalGather:
@@ -1079,7 +983,52 @@
 GRADS = ("up", "down", "w_query", "w_out")
 
 
-def whole_kernel(chunks, groups, counts, *refs):
+PARTS = (
+    (0, 0, 0, 256, ZYXC),
+    (0, 0, 256, 128, ZXYC),
+    (1, 0, 0, 256, ZXYC),
+    (1, 0, 256, 128, ZYXC),
+    (0, 1, 0, 384, ZYXC),
+    (1, 1, 0, 384, ZXYC),
+)
+MOVES = {
+    "start0": {None: (0, 1, 3, 2)},
+    "pre0": {None: (4, 0, 1, 0, 1, 3)},
+    "keyval0": {None: (2, 4, 1, 3, 0, 5, 2, 1)},
+    "mask0": {None: (0, 3)},
+    "arrived0": {None: (4,)},
+    "slot0": {2: (2,), 6: (5, 3, 2)},
+    "keyval1": {None: (4, 5, 4)},
+    "slot1": {2: (5,), 6: (5,)},
+}
+CHUNKS = (
+    (0, 0, 256, CXYLH, WIDE, 0, 1),
+    (0, 256, 256, CLHXY, WIDE, 0, 1),
+    (1, 0, 256, CYXLH, STACK, 1, 1),
+    (1, 256, 256, CLHYX, STACK, 1, 1),
+    (2, 0, 384, CYLHX, OWN, 2, 1),
+    (3, 0, 384, CXYLH, OWN, 3, 1),
+    (4, 0, 512, CXYLH, WIDE, 0, 0),
+    (5, 0, 512, CYXLH, STACK, 1, 0),
+    (6, 0, 384, CXYLH, OWN, 2, 0),
+    (7, 0, 384, CYXLH, OWN, 3, 0),
+    (8, 0, 128, CXLHY, STACK, 4, 0),
+)
+SCHEDULE = {
+    "hidden1": {None: (1, 2, 0)},
+    "slot1": {0: (5,), 2: (1, 0), 3: (2,), 5: (3,)},
+    "keyval1": {None: (0, 5)},
+    "back1": {None: (4, 2, 0, 1, 3, 4)},
+    "hidden0": {None: (6,)},
+    "out0": {None: (7, 5)},
+    "slot0": {1: (6, 3, 7), 3: (4,), 4: (0,), 5: (2,), 7: (1,)},
+    "keyval0": {None: (3,)},
+    "back0": {None: (9, 8, 4, 7, 6, 5, 2, 0, 3, 9, 1, 8, 6, 3, 5, 4)},
+}
+REST = (2, 10, 7, 10, 6, 5, 8, 0, 2, 1, 7, 9, 0, 6, 4, 5, 10, 3, 1, 7, 10, 2, 4, 0, 6, 7, 5, 8, 10, 1, 5, 6, 10, 9, 3, 2, 7, 0, 10, 8, 6, 7, 9, 1, 10, 2, 8, 3, 4, 1, 9, 6, 10, 4, 7, 9, 2, 1, 8, 0, 10, 3, 6, 8, 7, 9, 3, 10, 8, 9)
+
+
+def whole_kernel(chunks, parts, counts, *refs):
     given, refs = named(INPUTS, refs)
     (queries, outs, w_up, w_down), refs = refs[:4], refs[4:]
     (activations, input_grad), refs = refs[:2], refs[2:]
@@ -1100,7 +1049,7 @@
     (mask, spread, dense, gated, got1, got0), refs = refs[:6], refs[6:]
     scratch, refs = refs[:counts], refs[counts:]
     small_got, refs = refs[:4], refs[4:]
-    sems, small_sems, refs = refs[:5], refs[5:7], refs[7:]
+    sems, small_sems, refs = refs[:3], refs[3:5], refs[5:]
     gather_sems, keyval_sems, load_sem = refs[:3], refs[3:11], refs[11]
 
     count, width = given.x.shape
@@ -1113,10 +1062,7 @@
     total = Sums(chunks, sources + [tail], results, scratch, sems)
     little = SmallSum(small_in, small_out, small_got, *small_sems)
     smalls = [small_in.at[0:rows, :], small_in.at[rows : 2 * rows, :]]
-    gather = Gather(
-        [queries.at[0], outs.at[0], queries.at[1], outs.at[1]], experts_in,
-        share_orders(queries.shape[1], 4, total.size), *gather_sems,
-    )
+    gather = Gather(parts, (queries, outs), experts_in, *gather_sems)
     keyval_gather = [KeyvalGather(kept[l].keyval, count, *keyval_sems[2 * l : 2 * l + 2]) for l in range(2)]
     keyval_sum = [KeyvalSum(part0, got0, *keyval_sems[4:6]), KeyvalSum(part1, got1, *keyval_sems[6:8])]
     weights = []
@@ -1151,146 +1097,122 @@
         for copy in loads(l):
             copy.wait()
 
-    done = [0] * len(groups)
-
-    def begin(group):
-        for i in groups[group]:
+    done = [-1] * len(chunks)
+
+    def listed_moves(table, act, place, k):
+        for when, listed in table.get(place, {None: ()}).items():
+            if when is None:
+                for i in listed:
+                    act(i)
+            else:
+                at = when // 2 if place.startswith("slot") else when
+                pl.when(k == at)(lambda listed=listed: [act(i) for i in listed] and None)
+
+    def move(place, k=None):
+        listed_moves(SCHEDULE, step, place, k)
+
+    def fetch(place, k=None):
+        listed_moves(MOVES, gather.move, place, k)
+
+    def step(i):
+        if done[i] < 0:
             total.send_down(i, 0)
-
-    def advance(group):
-        if done[group] < total.stages(groups[group][0]):
-            for i in groups[group]:
-                total.advance(i, done[group])
-            done[group] += 1
+        else:
+            total.advance(i, done[i])
+        done[i] += 1
 
     def pre(l, x):
         pre_layer(x, weights[l].gain1[...], weights[l].bias1[...], weights[l].w_kv[...], normed[l], keyval_gather[l].own())
+        fetch("pre" + str(l))
         keyval_gather[l].start()
+        fetch("keyval" + str(l))
 
     load(0)
-    greet("cxyz", total.at, total.size)
-    gather.begin(0)
-    gather.begin(1)
+    greet(CXYZ, total.at, total.size)
+    fetch("start0")
     x = given.x[...].astype(F32)
     pre(0, x)
-    gather.begin(2)
-    gather.begin(3)
     fill_mask(given.lengths, given.keep, mask)
+    fetch("mask0")
     spread_routes(given.routes.at[0], spread)
+    fetch("spread0")
     small_in[...] = jnp.zeros(small_in.shape, F32)
     tail[...] = jnp.zeros(tail.shape, BF16)
-    for i in (0, 1, 0, 1, 0, 1, 0):
-        gather.advance(i)
     keyval_gather[0].wait()
+    fetch("arrived0")
 
     def first_between(place, k=None):
-        if place == "slot":
-            for when in (1, 4):
-
-                @pl.when(k == when)
-                def _():
-                    gather.advance(2)
-                    gather.advance(3)
-
-        elif place == "attended":
-            gather.advance(1)
-            gather.advance(2)
-            gather.advance(3)
-        elif place == "middle":
+        if place == "middle":
             loaded(0)
-
-    result, picked = layer_forward(x, normed[0], weights[0], mask, spread, dense, gated, kept[0], first_between)
+        fetch(place + "0", k)
+
+    middle, picked = layer_forward(x, normed[0], weights[0], mask, spread, dense, gated, kept[0], first_between)
+    result = feed_forward(middle, weights[0])
+    fetch("hidden0")
     load(1)
     count_chosen(picked, given.keep, smalls[0])
     stream[...] = result
     pre(1, result)
     spread_routes(given.routes.at[1], spread)
+    fetch("spread1")
 
     def second_between(place, k=None):
         if place == "queries":
             keyval_gather[1].wait()
         elif place == "middle":
             loaded(1)
-
-    gather.advance(2)
-    gather.advance(3)
-    result, picked = layer_forward(
+        fetch(place + "1", k)
+
+    _, picked = layer_forward(
         stream[...], normed[1], weights[1], mask, spread, dense, gated, kept[1], second_between
     )
     count_chosen(picked, given.keep, smalls[1])
-    activations[...] = result.astype(BF16)
     kept_col = jnp.broadcast_to(own_columns(given.keep, count).astype(F32), (LANES, count)).T
     kept_col = jnp.concatenate([kept_col] * (width // LANES), axis=1)
 
     def last_between(place, k=None):
         if place == "hidden":
             load(0)
-            begin(0)
-        elif place == "out":
-            pass
-        elif place == "slot":
-
-            @pl.when(k == 1)
-            def _():
-                advance(0)
-
+            activations[...] = (kept[1].middle[...] + normed_grad[...]).astype(BF16)
         elif place == "keyval":
             keyval_sum[1].start()
-            advance(0)
+        move(place + "1", k)
 
     layer_back(
         given.cotangent[...].astype(F32) * kept_col, normed[1], weights[1], mask, spread, dense, gated, kept[1],
-        sums, outputs[1], last_between,
+        sums, outputs[1], last_between, normed_grad,
     )
     tail[3, 0:experts, :] = router[...].astype(BF16)
-    begin(1)
+    move("back1")
     stream_grad = layer_finish(
         stream[...], normed[1], keyval_sum[1].total(), weights[1].gain1[...], weights[1].w_kv[...], middle_grad,
         normed_grad, tail.at[2, 0:pair], smalls[1],
     )
-    advance(0)
-    advance(1)
+    move("finish1")
     spread_routes(given.routes.at[0], spread)
     loaded(0)
 
     def between(place, k=None):
-        if place == "hidden":
-            begin(2)
-            advance(0)
-            advance(1)
-        elif place == "slot":
-
-            @pl.when(k == 2)
-            def _():
-                advance(0)
-                advance(2)
-
-            @pl.when(k == 5)
-            def _():
-                advance(1)
-
-        elif place == "keyval":
+        if place == "keyval":
             keyval_sum[0].start()
-            advance(0)
-            advance(2)
+        move(place + "0", k)
 
     layer_back(
         stream_grad, normed[0], weights[0], mask, spread, dense, gated, kept[0], sums, outputs[0], between
     )
     tail[1, 0:experts, :] = router[...].astype(BF16)
-    begin(3)
-    advance(1)
+    move("back0")
     input_grad[...] = layer_finish(
         given.x[...].astype(F32), normed[0], keyval_sum[0].total(), weights[0].gain1[...], weights[0].w_kv[...],
         middle_grad, normed_grad, tail.at[0, 0:pair], smalls[0],
     )
-    begin(4)
     little.start(0)
-    for step in range(2 * len(chunks[-1].order)):
-        for group in range(len(groups)):
-            advance(group)
-        if step < 4:
-            little.advance(step)
+    move("finish0")
+    every = len(REST) // 4
+    for number, i in enumerate(REST):
+        step(i)
+        if number % every == every - 1 and number // every < 4:
+            little.advance(number // every)
 
 
 def run_whole(args, weights_out, shapes, sizes):
@@ -1299,15 +1221,16 @@
     layers, own, width = queries.shape
     n = sizes["z"]
     count, flat, hidden = args[0][0].shape[0], n * own, w_up.shape[2]
-    chunks, groups = finish_chunks(n, shapes.up[1], shapes.down[1], shapes.own[1], shapes.tail[1])
+    chunks = [
+        Chunk(array, first, rows, order, kind, result, layer, True) for array, first, rows, order, kind, result, layer in CHUNKS
+    ]
+    parts = [Part(*part) for part in PARTS]
     scratch, sems = sum_scratch(chunks, [shapes.up, shapes.down, shapes.own, shapes.own] * 2 + [shapes.tail], sizes)
     small_shape = (16, width)
     results = [
         (layers, shapes.up[1], hidden), (layers,) + shapes.down, (layers,) + shapes.own[1:], (layers,) + shapes.own[1:],
         (1,) + shapes.tail,
     ]
-    most = max(sizes.values()) - 1
-    gather_sem = pltpu.SemaphoreType.DMA((4, 4, most, n - 1))
     got = pltpu.VMEM((n - 1, shapes.group // n, shapes.pair), BF16)
     part = pltpu.VMEM((shapes.group, shapes.pair), BF16)
     one = pltpu.VMEM((count, width), F32)
@@ -1325,7 +1248,7 @@
     small_refs = small_scratch(small_shape, sizes)
     anywhere = pl.BlockSpec(memory_space=pl.ANY)
     return pl.pallas_call(
-        partial(whole_kernel, chunks, groups, len(scratch)),
+        partial(whole_kernel, chunks, parts, len(scratch)),
         out_shape=[jax.ShapeDtypeStruct((count, width), BF16), jax.ShapeDtypeStruct((count, width), F32)]
         + [jax.ShapeDtypeStruct(shape, BF16) for shape in results]
         + [jax.ShapeDtypeStruct(small_shape, F32)],
@@ -1333,7 +1256,7 @@
         in_specs=specs + [anywhere] * 4,
         out_specs=[vmem(), vmem()] + [anywhere] * 5 + [vmem()],
         scratch_shapes=local + scratch + small_refs[:4] + sems + small_refs[4:]
-        + [gather_sem, gather_sem, pltpu.SemaphoreType.DMA((4,))]
+        + gather_sems(parts, sizes)
         + [pltpu.SemaphoreType.DMA((n - 1,))] * 8
         + [pltpu.SemaphoreType.DMA((2, 2))],
         compiler_params=pltpu.CompilerParams(
@@ -1341,6 +1264,55 @@
         ),
         name="both_blocks",
     )(*arrays, *weights_out)
+
+
+def widen_kernel(*refs):
+    up, down, query, out, result, grad, tail, small = refs[:8]
+    up_out, down_out, query_out, out_out, result_out, grad_out, kv, router, gain1, bias1, gain2, bias2, counts = refs[8:]
+    for source, target in ((up, up_out), (down, down_out), (query, query_out), (out, out_out), (grad, grad_out)):
+        target[...] = source[...].astype(F32)
+    result_out[...] = result[...]
+
+    @pl.when(pl.program_id(0) == 0)
+    def _():
+        rows = small.shape[0] // 2
+        for l in range(2):
+            kv[l] = tail[2 * l].astype(F32).T
+            router[l] = tail[2 * l + 1, 0 : router.shape[1], :].astype(F32)
+            row = slice(l, l + 1)
+            for i, target in enumerate((gain1, bias1, gain2, bias2)):
+                target[row, :] = small[l * rows + i : l * rows + i + 1, :]
+            counts[row, :] = small[l * rows + 4 : l * rows + 5, 0 : counts.shape[1]]
+
+
+def widen(result, grad, up, down, query, out, tail, small, experts):
+    layers, n, rows, width = down.shape
+    steps = layers * n
+    blocked, whole = [], []
+    for array in (up, down, query, out):
+        if array.ndim == 4:
+            blocked.append(pl.BlockSpec((None, 1, rows, width), lambda i: (i // n, i % n, 0, 0)))
+        else:
+            blocked.append(pl.BlockSpec((None, array.shape[1] // n, array.shape[2]), lambda i: (i // n, i % n, 0)))
+    for array in (result, grad):
+        blocked.append(pl.BlockSpec((array.shape[0] // steps, array.shape[1]), lambda i: (i, 0)))
+    tail = tail.reshape(tail.shape[1:])
+    shapes = [(layers, width, tail.shape[1]), (layers, experts, width)] + [(layers, width)] * 4 + [(layers, experts)]
+
+    def fixed(shape):
+        return pl.BlockSpec(shape, lambda i: (0,) * len(shape))
+
+    return pl.pallas_call(
+        widen_kernel,
+        out_shape=[jax.ShapeDtypeStruct(a.shape, F32) for a in (up, down, query, out)]
+        + [jax.ShapeDtypeStruct(a.shape, a.dtype) for a in (result, grad)]
+        + [jax.ShapeDtypeStruct(shape, F32) for shape in shapes],
+        grid=(steps,),
+        in_specs=blocked + [fixed(tail.shape), fixed(small.shape)],
+        out_specs=blocked + [fixed(shape) for shape in shapes],
+        compiler_params=pltpu.CompilerParams(vmem_limit_bytes=VMEM_LIMIT),
+        name="widen",
+    )(up, down, query, out, result, grad, tail, small)
 
 
 def specs_of(args):
@@ -1374,7 +1346,7 @@
     tokens, cotangent, routes, keep, lengths, norm1_gain, norm1_bias, w_kv, w_router, w_query, w_out,
     norm2_gain, norm2_bias, w_up, w_down,
 ):
-    n = lax.axis_size("exp")
+    n = lax.axis_size(EXP)
     dp = lax.axis_size("dp")
     layers, width, pair = w_kv.shape
     count = tokens.shape[1]
@@ -1417,11 +1389,15 @@
             (x0, None), (cotangent[0], None), (routes_t, None), (lengths, "smem"), (keep, None), (gain1, None),
             (bias1, None), (w_kv, None), (router_t, None), (gain2, None), (bias2, None),
         ]
-        activations, input_grad, up, down, expert_query, expert_out, tail, small = run_whole(
-            given, (queries_t, outs, w_up, w_down), all_shapes, sizes
+        results = run_whole(given, (queries_t, outs, w_up, w_down), all_shapes, sizes)
+        up, down, expert_query, expert_out, activations, input_grad, kv, router, *norms, counts = widen(*results, experts)
+        expert_query = jnp.swapaxes(expert_query.reshape(layers, local, head, width), 2, 3)
+        return (
+            activations[None], input_grad[None], norms[0], norms[1], kv, jnp.swapaxes(router, 1, 2), expert_query,
+            expert_out.reshape(layers, local, head, width), norms[2], norms[3], up, down.reshape(layers, hidden, width), counts,
         )
     else:
-        gathered = [array.reshape(flat, width) for array in gather_all((queries_t, outs), sizes, 2)]
+        gathered = gather_all((queries_t, outs), sizes, 2)
         wq, wo = gathered[0::2], gathered[1::2]
         def weights(l):
             return [(gain1, None), (bias1, None), (w_kv, l), (router_t, l), (wq[l], None), (wo[l], None), (gain2, None), (bias2, None), (w_up, l), (w_down, l)]
@@ -1431,32 +1407,32 @@
             pre_kernel, [(x0, None), (gain1, None), (bias1, None), (w_kv, 0)],
             [((count, width), BF16), ((count, pair), BF16)], [], "pre",
         )
-        keyval0 = share(keyval0, n, False, 0, "gather_keyval").reshape(group, pair)
+        keyval0 = share(keyval0, n, False, 0, "share").reshape(group, pair)
         *kept0, x1, normed1, keyval1, small0 = call(
             first_kernel,
             weights(0) + [(x0, None), (normed0, None), (keyval0, None), (routes_t, 0), (lengths, "smem"), (keep, None), (gain1, None), (bias1, None), (w_kv, 1)],
             kept_shapes + [((count, width), F32), ((count, width), BF16), ((count, pair), BF16), ((8, width), F32)],
-            work, "first_block",
+            work, "first",
         )
-        keyval1 = share(keyval1, n, False, 0, "gather_keyval").reshape(group, pair)
+        keyval1 = share(keyval1, n, False, 0, "share").reshape(group, pair)
         activations, up1, down1, out1, query1, router1, part1, small1, mid1, ngrad1 = call(
             turn_kernel,
             weights(1) + [(x1, None), (normed1, None), (keyval1, None), (routes_t, 1), (lengths, "smem"), (keep, None), (cotangent[0], None)],
-            [((count, width), BF16)] + out_shapes, kept_shapes + sum_shapes + work, "second_block",
+            [((count, width), BF16)] + out_shapes, kept_shapes + sum_shapes + work, "turn",
         )
         tail_rows = rows_of(pair)
         result_shapes = [
             (layers,) + up1.shape[1:2] + (hidden,), (layers,) + down1.shape, (layers,) + query1.shape[1:],
             (layers,) + out1.shape[1:], (1, n, tail_rows, width),
         ]
-        received1 = share(part1, n, True, 1, "scatter_keyval")
+        received1 = share(part1, n, True, 1, "scatter")
         kv1, small1, up0, down0, out0, query0, router0, part0, small0, mid0, ngrad0 = call(
             back_kernel,
             weights(0) + [(x1, None), (normed1, None), (received1, None), (gain1, None), (w_kv, 1), (mid1, None), (ngrad1, None), (small1, None),
              (normed0, None), (routes_t, 0), (lengths, "smem"), (keep, None), (small0, None), (keyval0, None)] + [(v, None) for v in kept0],
-            [((pair, width), BF16), ((8, width), F32)] + out_shapes, sum_shapes + work, "first_block_back",
+            [((pair, width), BF16), ((8, width), F32)] + out_shapes, sum_shapes + work, "back",
         )
-        received0 = share(part0, n, True, 1, "scatter_keyval")
+        received0 = share(part0, n, True, 1, "scatter")
         kv0, small0, input_grad = call(
             end_kernel,
             [(x0, None), (normed0, None), (received0, None), (gain1, None), (w_kv, 0), (mid0, None), (ngrad0, None), (small0, None)],
@@ -1489,12 +1465,12 @@
         body,
         mesh=mesh,
         in_specs=(
-            P("dp", "exp", None), P("dp", "exp", None), P(None, "dp", None, None), P("dp", None), P("dp", None),
-            P(), P(), P(), P(), P(None, "exp", None, None), P(None, "exp", None, None), P(), P(), P(), P(),
+            P("dp", EXP, None), P("dp", EXP, None), P(None, "dp", None, None), P("dp", None), P("dp", None),
+            P(), P(), P(), P(), P(None, EXP, None, None), P(None, EXP, None, None), P(), P(), P(), P(),
         ),
         out_specs=(
-            P("dp", "exp", None), P("dp", "exp", None), P(), P(), P(), P(),
-            P(None, "exp", None, None), P(None, "exp", None, None), P(), P(), P(), P(), P(),
+            P("dp", EXP, None), P("dp", EXP, None), P(), P(), P(), P(),
+            P(None, EXP, None, None), P(None, EXP, None, None), P(), P(), P(), P(), P(),
         ),
         check_vma=False,
     )

time: 237 us -> 185 us (0.78)
  Pallas kernels: 213 us -> 184 us
  other arithmetic: 16.5 us -> 0 us
  local copies, waits for them, and re-layouts: 5.93 us -> 0 us
    pallas_call x1 -> x2, Pallas kernels: 213 us -> 184 us  [the longest x1 171 us: run_whole(): pl.pallas_call(partial(whole_kernel, chunks, parts, len(scratch)), out_sh...]
    convert_element_type x4 -> x0, other arithmetic: 14.1 us -> none  [the longest x1 6.93 us: body(): down = down[:, :, :hidden // n].reshape(layers, hidden, width).astype(F32)]
    unnamed x13 -> x0, local copies, waits for them, and re-layouts: 2.51 us -> none
    transpose x2 -> x0, other arithmetic: 2.45 us -> none  [the longest x1 1.45 us: body(): router = jnp.swapaxes(tail[0, 1:4:2, :experts].astype(F32), 1, 2)]
where the time goes in v4:
time: 185 us
  Pallas kernels  184 us (99%)
    pallas_call x1, Pallas kernels, run_whole(): pl.pallas_call(partial(whole_kernel, chunks, parts, len(scratch)), out_sh...  171 us
    pallas_call x1, Pallas kernels, widen(): pl.pallas_call(widen_kernel, out_shape=[jax.ShapeDtypeStruct(a.shape, F32...  12.9 us

profile of v4, /device:TPU:0, one launch (start us, length us, event | category | flops | bytes accessed | tf_op | source)
XLA Modules:
  0.0 184.6 jit_solution(10544626465421045057)
XLA Ops:
  0.7 170.9 %both_blocks.1 = (bf16[256,512]{1,0:T(8,128)(2,1)}, f32[256,512]{1,0:T(8,128)}, bf16[2,512,2048]{2,1,0:T(8,128)(2,1)}, bf16[2,4,512,512]{3,2,1,0:T(8,128)(2,1)},...) custom-call(bf16[256,512]{1,0:T(8,128)(2,1)} %bitcast.22, ...), custom_call_target="tpu_custom_call" | custom-call | tf_op jit(solution)/shard_map/both_blocks/pallas_call | solution.py:1250
  171.5 12.9 %widen.1 = (f32[2,512,2048]{2,1,0:T(8,128)}, f32[2,4,512,512]{3,2,1,0:T(8,128)}, f32[2,384,512]{2,1,0:T(8,128)}, f32[2,384,512]{2,1,0:T(8,128)}, bf16[256,512]{1...) custom-call(bf16[2,512,2048]{2,1,0:T(8,128)(2,1)} %get-tuple-element, ...), custom_call_target="tpu_custom_call" | custom-call | tf_op jit(solution)/shard_map/widen/pallas_call | solution.py:1305

commit v5 on v4

--- a/solution.py
+++ b/solution.py
@@ -12,7 +12,6 @@
 EXP = "exp"
 CLHXY = "clhxy"
 CLHYX = "clhyx"
-CXLHY = "cxlhy"
 CXYLH = "cxylh"
 CXYZ = "cxyz"
 CYLHX = "cylhx"
@@ -980,6 +979,7 @@
 
 
 INPUTS = ("x", "cotangent", "routes", "lengths", "keep", "gain1", "bias1", "w_kv", "w_router", "gain2", "bias2")
+LARGE = ("x", "cotangent", "routes", "w_kv", "w_router")
 GRADS = ("up", "down", "w_query", "w_out")
 
 
@@ -1009,29 +1009,29 @@
     (2, 0, 384, CYLHX, OWN, 2, 1),
     (3, 0, 384, CXYLH, OWN, 3, 1),
     (4, 0, 512, CXYLH, WIDE, 0, 0),
-    (5, 0, 512, CYXLH, STACK, 1, 0),
+    (5, 0, 256, CYXLH, STACK, 1, 0),
+    (5, 256, 256, CYLHX, STACK, 1, 0),
     (6, 0, 384, CXYLH, OWN, 2, 0),
     (7, 0, 384, CYXLH, OWN, 3, 0),
-    (8, 0, 128, CXLHY, STACK, 4, 0),
+    (8, 0, 128, CXYLH, STACK, 4, 0),
 )
 SCHEDULE = {
-    "hidden1": {None: (1, 2, 0)},
-    "slot1": {0: (5,), 2: (1, 0), 3: (2,), 5: (3,)},
-    "keyval1": {None: (0, 5)},
-    "back1": {None: (4, 2, 0, 1, 3, 4)},
-    "hidden0": {None: (6,)},
-    "out0": {None: (7, 5)},
-    "slot0": {1: (6, 3, 7), 3: (4,), 4: (0,), 5: (2,), 7: (1,)},
-    "keyval0": {None: (3,)},
-    "back0": {None: (9, 8, 4, 7, 6, 5, 2, 0, 3, 9, 1, 8, 6, 3, 5, 4)},
+    "hidden1": {None: (1, 0)},
+    "slot1": {0: (2, 1), 2: (0, 2, 5), 4: (3,)},
+    "back1": {None: (4, 0, 5, 2, 3, 1, 4, 0)},
+    "hidden0": {None: (6, 8, 5, 3)},
+    "out0": {None: (4, 0, 1, 2, 6, 7, 8)},
+    "slot0": {0: (5,), 2: (7, 3, 1, 4), 4: (8,), 6: (10,)},
+    "keyval0": {None: (0,)},
+    "back0": {None: (6, 9, 7, 2, 3, 10, 9, 8, 7, 6, 2, 7)},
 }
-REST = (2, 10, 7, 10, 6, 5, 8, 0, 2, 1, 7, 9, 0, 6, 4, 5, 10, 3, 1, 7, 10, 2, 4, 0, 6, 7, 5, 8, 10, 1, 5, 6, 10, 9, 3, 2, 7, 0, 10, 8, 6, 7, 9, 1, 10, 2, 8, 3, 4, 1, 9, 6, 10, 4, 7, 9, 2, 1, 8, 0, 10, 3, 6, 8, 7, 9, 3, 10, 8, 9)
+REST = (8, 0, 11, 1, 3, 6, 11, 2, 9, 8, 5, 4, 7, 11, 1, 6, 2, 8, 3, 9, 0, 11, 10, 4, 7, 2, 6, 11, 0, 8, 1, 7, 5, 6, 11, 9, 10, 8, 5, 3, 11, 6, 10, 4, 1, 5, 5, 11, 2, 0, 9, 7, 8, 4, 3, 0, 2, 10, 1, 11, 6, 9, 1, 10, 7, 11, 6, 8, 3, 4, 11, 10, 9, 10, 7, 3, 9)
 
 
 def whole_kernel(chunks, parts, counts, *refs):
     given, refs = named(INPUTS, refs)
     (queries, outs, w_up, w_down), refs = refs[:4], refs[4:]
-    (activations, input_grad), refs = refs[:2], refs[2:]
+    written, refs = refs[:2], refs[2:]
     results, small_out, refs = refs[:5], refs[5], refs[6:]
     experts_in, refs = refs[:4], refs[4:]
     (up_here, down_here), refs = refs[:2], refs[2:]
@@ -1050,7 +1050,16 @@
     scratch, refs = refs[:counts], refs[counts:]
     small_got, refs = refs[:4], refs[4:]
     sems, small_sems, refs = refs[:3], refs[3:5], refs[5:]
-    gather_sems, keyval_sems, load_sem = refs[:3], refs[3:11], refs[11]
+    gather_sems, keyval_sems, load_sem, refs = refs[:3], refs[3:11], refs[11], refs[12:]
+    (activations, input_grad), fetched, write_sem, fetch_sem = refs[:2], refs[2:-2], refs[-2], refs[-1]
+    fetching = []
+    for i, (name, here) in enumerate(zip(LARGE, fetched)):
+        fetching.append(pltpu.make_async_copy(getattr(given, name), here, fetch_sem.at[i]))
+        setattr(given, name, here)
+    writing = [
+        pltpu.make_async_copy(here, there, write_sem.at[i])
+        for i, (here, there) in enumerate(zip((activations, input_grad), written))
+    ]
 
     count, width = given.x.shape
     rows = small_in.shape[0] // 2
@@ -1127,9 +1136,13 @@
         keyval_gather[l].start()
         fetch("keyval" + str(l))
 
-    load(0)
+    for copy in fetching:
+        copy.start()
     greet(CXYZ, total.at, total.size)
     fetch("start0")
+    load(0)
+    for copy in fetching:
+        copy.wait()
     x = given.x[...].astype(F32)
     pre(0, x)
     fill_mask(given.lengths, given.keep, mask)
@@ -1174,6 +1187,7 @@
         if place == "hidden":
             load(0)
             activations[...] = (kept[1].middle[...] + normed_grad[...]).astype(BF16)
+            writing[0].start()
         elif place == "keyval":
             keyval_sum[1].start()
         move(place + "1", k)
@@ -1206,6 +1220,7 @@
         given.x[...].astype(F32), normed[0], keyval_sum[0].total(), weights[0].gain1[...], weights[0].w_kv[...],
         middle_grad, normed_grad, tail.at[0, 0:pair], smalls[0],
     )
+    writing[1].start()
     little.start(0)
     move("finish0")
     every = len(REST) // 4
@@ -1213,10 +1228,15 @@
         step(i)
         if number % every == every - 1 and number // every < 4:
             little.advance(number // every)
+    for copy in writing:
+        copy.wait()
 
 
 def run_whole(args, weights_out, shapes, sizes):
     specs, arrays = specs_of(args)
+    large = [INPUTS.index(name) for name in LARGE]
+    for i in large:
+        specs[i] = pl.BlockSpec(memory_space=pl.ANY)
     queries, _, w_up, w_down = weights_out
     layers, own, width = queries.shape
     n = sizes["z"]
@@ -1254,11 +1274,13 @@
         + [jax.ShapeDtypeStruct(small_shape, F32)],
         grid=(1,),
         in_specs=specs + [anywhere] * 4,
-        out_specs=[vmem(), vmem()] + [anywhere] * 5 + [vmem()],
+        out_specs=[anywhere] * 7 + [vmem()],
         scratch_shapes=local + scratch + small_refs[:4] + sems + small_refs[4:]
         + gather_sems(parts, sizes)
         + [pltpu.SemaphoreType.DMA((n - 1,))] * 8
-        + [pltpu.SemaphoreType.DMA((2, 2))],
+        + [pltpu.SemaphoreType.DMA((2, 2)), pltpu.VMEM((count, width), BF16), one]
+        + [pltpu.VMEM(arrays[i].shape, arrays[i].dtype) for i in large]
+        + [pltpu.SemaphoreType.DMA((2,)), pltpu.SemaphoreType.DMA((len(large),))],
         compiler_params=pltpu.CompilerParams(
             collective_id=5, has_side_effects=True, vmem_limit_bytes=63 << 20
         ),
@@ -1287,13 +1309,15 @@
 
 def widen(result, grad, up, down, query, out, tail, small, experts):
     layers, n, rows, width = down.shape
-    steps = layers * n
+    cuts = n // 2
+    steps = layers * cuts
     blocked, whole = [], []
     for array in (up, down, query, out):
         if array.ndim == 4:
-            blocked.append(pl.BlockSpec((None, 1, rows, width), lambda i: (i // n, i % n, 0, 0)))
+            blocked.append(pl.BlockSpec((None, n // cuts, rows, width), lambda i: (i // cuts, i % cuts, 0, 0)))
         else:
-            blocked.append(pl.BlockSpec((None, array.shape[1] // n, array.shape[2]), lambda i: (i // n, i % n, 0)))
+            block = (None, array.shape[1] // cuts, array.shape[2])
+            blocked.append(pl.BlockSpec(block, lambda i: (i // cuts, i % cuts, 0)))
     for array in (result, grad):
         blocked.append(pl.BlockSpec((array.shape[0] // steps, array.shape[1]), lambda i: (i, 0)))
     tail = tail.reshape(tail.shape[1:])

time: 185 us -> 180 us (0.973)
  Pallas kernels: 184 us -> 179 us
    pallas_call x1, Pallas kernels: 171 us -> 167 us  [run_whole(): pl.pallas_call(partial(whole_kernel, chunks, parts, len(scratch)), out_sh...]
where the time goes in v5:
time: 180 us
  Pallas kernels  179 us (99%)
    pallas_call x1, Pallas kernels, run_whole(): pl.pallas_call(partial(whole_kernel, chunks, parts, len(scratch)), out_sh...  167 us
    pallas_call x1, Pallas kernels, widen(): pl.pallas_call(widen_kernel, out_shape=[jax.ShapeDtypeStruct(a.shape, F32...  12.2 us

profile of v5, /device:TPU:0, one launch (start us, length us, event | category | flops | bytes accessed | tf_op | source)
XLA Modules:
  0.0 180.0 jit_solution(724164293981660474)
XLA Ops:
  0.7 166.9 %both_blocks.1 = (bf16[256,512]{1,0:T(8,128)(2,1)}, f32[256,512]{1,0:T(8,128)}, bf16[2,512,2048]{2,1,0:T(8,128)(2,1)}, bf16[2,4,512,512]{3,2,1,0:T(8,128)(2,1)},...) custom-call(bf16[256,512]{1,0:T(8,128)(2,1)} %bitcast.22, ...), custom_call_target="tpu_custom_call" | custom-call | tf_op jit(solution)/shard_map/both_blocks/pallas_call | solution.py:1270
  167.6 12.2 %widen.1 = (f32[2,512,2048]{2,1,0:T(8,128)}, f32[2,4,512,512]{3,2,1,0:T(8,128)}, f32[2,384,512]{2,1,0:T(8,128)}, f32[2,384,512]{2,1,0:T(8,128)}, bf16[256,512]{1...) custom-call(bf16[2,512,2048]{2,1,0:T(8,128)(2,1)} %get-tuple-element, ...), custom_call_target="tpu_custom_call" | custom-call | tf_op jit(solution)/shard_map/widen/pallas_call | solution.py:1329
